TPU v7x, 32 devices: a whole 2x2x4 slice. The times are simulated.
32 devices in a mesh: dp: 8 (over z, x), mp: 4 (over y, core).
Axes of the slice: x: 2, y: 2, z: 4, core: 2. Of those that a mesh axis runs over, the one named last changes fastest.
Arguments:
- latents: float32 [8, 1792, 16], P('dp', 'mp'), may hold values from -6 to 6
- noise: float32 [8, 1792, 16], P('dp', 'mp'), may hold values from -6 to 6
- caption: bfloat16 [8, 120, 4096], P('dp'), may hold values from -3 to 3
- caption_lens: int32 [8], replicated, may hold values from 15 to 120
- timesteps: int32 [8], replicated, may hold values from 50 to 999
- grid_hw: int32 [8, 2], replicated, may hold values from 8 to 56, as said below
- frame_counts: int32 [8], replicated, may hold values from 1 to 4, as said below
- attn_mats: float32 [3, 1152, 4608], P(None, 'dp', 'mp'), may hold values from -0.1875 to 0.1875
- ffn_mats: float32 [2, 2, 1152, 4608], P(None, None, 'dp', 'mp'), may hold values from -0.1875 to 0.1875
- embed_mats: float32 [13568, 1152], P('dp', 'mp'), may hold values from -0.1875 to 0.1875
- vectors: float32 [106016], replicated
- attn_first: float32 [3, 1152, 4608], P(None, 'dp', 'mp'), may hold values from -1.5258789e-05 to 1.5258789e-05
- ffn_first: float32 [2, 2, 1152, 4608], P(None, None, 'dp', 'mp'), may hold values from -1.5258789e-05 to 1.5258789e-05
- embed_first: float32 [13568, 1152], P('dp', 'mp'), may hold values from -1.5258789e-05 to 1.5258789e-05
- vector_first: float32 [106016], replicated, may hold values from -1.0999719e-05 to 1.0999719e-05
- attn_second: float32 [3, 1152, 4608], P(None, 'dp', 'mp'), may hold values from 7.562113e-12 to 3.0248453e-11
- ffn_second: float32 [2, 2, 1152, 4608], P(None, None, 'dp', 'mp'), may hold values from 7.562113e-12 to 3.0248453e-11
- embed_second: float32 [13568, 1152], P('dp', 'mp'), may hold values from 7.562113e-12 to 3.0248453e-11
- vector_second: float32 [106016], replicated, may hold values from 4.726321e-13 to 1.20993819e-10
- attn_ema: float32 [3, 1152, 4608], P(None, 'dp', 'mp'), may hold values from -0.1875 to 0.1875
- ffn_ema: float32 [2, 2, 1152, 4608], P(None, None, 'dp', 'mp'), may hold values from -0.1875 to 0.1875
- embed_ema: float32 [13568, 1152], P('dp', 'mp'), may hold values from -0.1875 to 0.1875
- vector_ema: float32 [106016], replicated
Outputs:
- loss_sum: float32 [], replicated
- token_count: float32 [], replicated
- grad_norm: float32 [], replicated
- attn_first_new: float32 [3, 1152, 4608], P(None, 'dp', 'mp')
- ffn_first_new: float32 [2, 2, 1152, 4608], P(None, None, 'dp', 'mp')
- embed_first_new: float32 [13568, 1152], P('dp', 'mp')
- vector_first_new: float32 [106016], replicated
- attn_second_new: float32 [3, 1152, 4608], P(None, 'dp', 'mp')
- ffn_second_new: float32 [2, 2, 1152, 4608], P(None, None, 'dp', 'mp')
- embed_second_new: float32 [13568, 1152], P('dp', 'mp')
- vector_second_new: float32 [106016], replicated
- attn_new: float32 [3, 1152, 4608], P(None, 'dp', 'mp')
- ffn_new: float32 [2, 2, 1152, 4608], P(None, None, 'dp', 'mp')
- embed_new: float32 [13568, 1152], P('dp', 'mp')
- vector_new: float32 [106016], replicated
- attn_ema_new: float32 [3, 1152, 4608], P(None, 'dp', 'mp')
- ffn_ema_new: float32 [2, 2, 1152, 4608], P(None, None, 'dp', 'mp')
- embed_ema_new: float32 [13568, 1152], P('dp', 'mp')
- vector_ema_new: float32 [106016], replicated
Inputs may be any that keep to these rules, and one draw needn't show every extreme that they name: `grid_hw`: each row is a clip's grid: rows between 8 and 31, columns = 448 // rows, so a frame has at most 448 patches; in every draw some clip has exactly 16 rows and 448 patches, some clip has 8 rows and some clip has 31 rows. `frame_counts`: the last clip has 4 frames in every draw.
All inputs are finite; a program needn't handle non-finite values.
Results may differ from a plain program's by a relative error of at most 0.015.
Values may be sent and summed in bfloat16 or wider, within the bound.
A program may use at most 320 MiB of HBM per device.

v0:
```python
import functools
import math

import jax
import jax.numpy as jnp
from jax import lax
from jax.experimental import pallas as pl
from jax.experimental.pallas import tpu as pltpu
from jax.sharding import PartitionSpec as P

D = 1152
HEADS = 16
HD = 72
FF = 4608
TFREQ = 256
TXT = 4096
CIN = 16
COUT = 32
CAP = 120
FR = 4
PM = 448
STEP = 5
DP, MP = "dp", "mp"
AT_SPACE = 0
AT_TIME = 1
AT_CROSS = 2
AT_ATTN = 3
AT_FFN = 4
AT_PARTS = 5
AT_PART = 6
AT_CONTEXT = 7
AT_KEEP = 8
AT_INPUT = 9
AT_GATHERED = 10
AT_QUERY = 11
AT_KEY_ROWS = 12
AT_VALUE_ROWS = 13
AT_LOGSUM = 14
AT_MIXED = 15
AT_BRANCH = 16
AT_PRE = 17
AT_HIDDEN = 18
PATCH_W = 0
PATCH_B = 1
FINAL_W = 2
FINAL_B = 3
T_BIAS_ONE = 4
T_BIAS_TWO = 5
T_BIAS_MOD = 6
C_BIAS_ONE = 7
C_BIAS_TWO = 8
ATTN_BIAS = 9
FFN_BIAS_ONE = 10
FFN_BIAS_TWO = 11
TABLES = 12
FINAL_TABLE = 13


EPS_NORM = 1e-06
LEARN_RATE = 0.03
VECTOR_RATE = 0.15
BETA_FIRST = 0.5
BETA_SECOND = 0.5
ADAM_EPSILON = 1e-08
WEIGHT_DECAY = 0.01
EMA_DECAY = 0.9
CLIP_NORM = 0.02
NEG_LARGE = -1e30
CONTRACT_ROWS = (((0,), (0,)), ((), ()))
CONTRACT_LAST = (((1,), (1,)), ((), ()))


def vector_parts():
    return [
        (PATCH_W, (CIN, D)),
        (PATCH_B, (D,)),
        (FINAL_W, (COUT, D)),
        (FINAL_B, (COUT,)),
        (T_BIAS_ONE, (D,)),
        (T_BIAS_TWO, (D,)),
        (T_BIAS_MOD, (6 * D,)),
        (C_BIAS_ONE, (D,)),
        (C_BIAS_TWO, (D,)),
        (ATTN_BIAS, (3, 3, D)),
        (FFN_BIAS_ONE, (2, FF)),
        (FFN_BIAS_TWO, (2, D)),
        (TABLES, (2, 6, D)),
        (FINAL_TABLE, (2, D)),
    ]


def unpack(flat):
    result = {}
    offset = 0
    for label, extent in vector_parts():
        length = math.prod(extent)
        result[label] = flat[offset : offset + length].reshape(extent)
        offset += length
    return result


def waves(position, width):
    half = width // 2
    freqs = jnp.exp(-math.log(10000.0) * jnp.arange(half, dtype=jnp.float32) / half)
    angles = position[..., None] * freqs
    return jnp.concatenate([jnp.sin(angles), jnp.cos(angles)], -1)


def roster():
    betas = 0.0001 + (0.02 - 0.0001) * jnp.arange(1000, dtype=jnp.float32) / 999.0
    return (betas, jnp.exp(jnp.cumsum(jnp.log1p(-betas))))


def modulate(x, shift_vec, scale_vec):
    centered = x - jnp.mean(x, -1, keepdims=True)
    normed = centered * lax.rsqrt(jnp.mean(centered * centered, -1, keepdims=True) + EPS_NORM)
    return normed * (1.0 + scale_vec) + shift_vec


def gelu_tanh(values):
    return jax.nn.gelu(values, approximate=True)


def token_losses(output, frozen, latent, noise_part, extra):
    noisy, alpha_bar, alpha_prev, beta_now = extra
    eps = output[:, :CIN]
    var_raw = output[:, CIN:]
    mse = jnp.mean((eps - noise_part) ** 2, -1)
    post_var = beta_now * (1.0 - alpha_prev) / (1.0 - alpha_bar)
    log_post = jnp.log(post_var)
    frac = (var_raw + 1.0) / 2.0
    log_var = frac * jnp.log(beta_now) + (1.0 - frac) * log_post
    coef_start = beta_now * jnp.sqrt(alpha_prev) / (1.0 - alpha_bar)
    coef_now = (1.0 - alpha_prev) * jnp.sqrt(1.0 - beta_now) / (1.0 - alpha_bar)
    true_mean = coef_start * latent + coef_now * noisy
    guess = (noisy - jnp.sqrt(1.0 - alpha_bar) * frozen) / jnp.sqrt(alpha_bar)
    model_mean = coef_start * guess + coef_now * noisy
    kl_term = 0.5 * (
        -1.0
        + log_var
        - log_post
        + jnp.exp(log_post - log_var)
        + (true_mean - model_mean) ** 2 * jnp.exp(-log_var)
    )
    return mse + jnp.mean(kl_term, -1) / math.log(2.0)


def attention_forms(kind):
    if kind == AT_SPACE:
        return ("fqhe,fkhe->fhqk", "fhqk,fkhe->fqhe", "fhqk,fqhe->fkhe")
    if kind == AT_TIME:
        return ("qphe,kphe->phqk", "phqk,kphe->qphe", "phqk,qphe->kphe")
    return ("qhe,khe->hqk", "hqk,khe->qhe", "hqk,qhe->khe")


def own_slice(vector, part, width):
    return lax.dynamic_slice_in_dim(vector, part * width, width, 0)


def placed(piece, part, full):
    return lax.dynamic_update_slice_in_dim(
        jnp.zeros((full,), jnp.float32), piece, part * piece.shape[0], 0
    )


def project_in(shard_rows, weight):
    piece = lax.all_gather(shard_rows, MP, axis=0, tiled=True)
    product = jnp.dot(piece, weight, preferred_element_type=jnp.float32)
    return (product, piece)


def project_out(full_rows, weight_t):
    return lax.psum_scatter(
        lax.dot_general(
            full_rows, weight_t, CONTRACT_LAST, preferred_element_type=jnp.float32
        ).astype(jnp.bfloat16),
        MP,
        scatter_dimension=0,
        tiled=True,
    ).astype(jnp.float32)


def back_out(grad_rows, full_rows, weight_t):
    piece = lax.all_gather(grad_rows, MP, axis=0, tiled=True)
    product = jnp.dot(piece, weight_t, preferred_element_type=jnp.float32)
    d_weight = lax.dot_general(piece, full_rows, CONTRACT_ROWS, preferred_element_type=jnp.float32)
    return (product, d_weight)


def back_in(d_full, weight):
    return lax.psum_scatter(
        lax.dot_general(d_full, weight, CONTRACT_LAST, preferred_element_type=jnp.float32).astype(
            jnp.bfloat16
        ),
        MP,
        scatter_dimension=0,
        tiled=True,
    ).astype(jnp.float32)


def attend_forward(query, key_rows, value_rows, keep, forms):
    scores = jnp.einsum(forms[0], query, key_rows, preferred_element_type=jnp.float32) * HD ** (
        -0.5
    )
    scores = jnp.where(keep, scores, NEG_LARGE)
    peak = jnp.max(scores, -1, keepdims=True)
    expd = jnp.exp(scores - peak)
    total = jnp.sum(expd, -1, keepdims=True)
    probs = (expd / total).astype(jnp.bfloat16)
    mixed = jnp.einsum(forms[1], probs, value_rows, preferred_element_type=jnp.float32)
    return (mixed, peak + jnp.log(total))


def attend_backward(query, key_rows, value_rows, keep, forms, logsum, d_mixed):
    scores = jnp.einsum(forms[0], query, key_rows, preferred_element_type=jnp.float32) * HD ** (
        -0.5
    )
    scores = jnp.where(keep, scores, NEG_LARGE)
    probs_full = jnp.exp(scores - logsum)
    probs = probs_full.astype(jnp.bfloat16)
    d_value = jnp.einsum(forms[2], probs, d_mixed, preferred_element_type=jnp.float32)
    d_probs = jnp.einsum(forms[0], d_mixed, value_rows, preferred_element_type=jnp.float32)
    offset = jnp.sum(d_probs * probs_full, -1, keepdims=True)
    d_scores = (probs_full * (d_probs - offset) * HD ** (-0.5)).astype(jnp.bfloat16)
    d_query = jnp.einsum(forms[1], d_scores, key_rows, preferred_element_type=jnp.float32)
    d_key = jnp.einsum(forms[2], d_scores, query, preferred_element_type=jnp.float32)
    return (d_query, d_key, d_value)


def attention_forward(x, index, mods, kind, setup):
    weight = setup[AT_ATTN][index]
    heads = weight.shape[1]
    width_local = heads * HD
    biases = setup[AT_PARTS][ATTN_BIAS][index]
    part = setup[AT_PART]
    forms = attention_forms(kind)
    query_bias = own_slice(biases[0], part, width_local).reshape(heads, HD)
    value_bias = own_slice(biases[1], part, width_local).reshape(heads, HD)
    if kind == AT_CROSS:
        projected, gathered = project_in(
            x.astype(jnp.bfloat16), weight[:, :, 0, :].reshape(D, width_local)
        )
        query = projected.reshape(-1, heads, HD) + query_bias
        context = setup[AT_CONTEXT]
        key_rows = jnp.einsum(
            "cd,dhe->che", context, weight[:, :, 1, :], preferred_element_type=jnp.float32
        )
        value_rows = (
            jnp.einsum(
                "cd,dhe->che", context, weight[:, :, 2, :], preferred_element_type=jnp.float32
            )
            + value_bias
        )
    else:
        source = modulate(x, mods[0], mods[1])
        projected, gathered = project_in(
            source.astype(jnp.bfloat16), weight[:, :, :3, :].reshape(D, 3 * width_local)
        )
        projected = projected.reshape(FR, PM, heads, 3, HD)
        query = projected[:, :, :, 0] + query_bias
        key_rows = projected[:, :, :, 1]
        value_rows = projected[:, :, :, 2] + value_bias
    query = query.astype(jnp.bfloat16)
    key_rows = key_rows.astype(jnp.bfloat16)
    value_rows = value_rows.astype(jnp.bfloat16)
    mixed, logsum = attend_forward(query, key_rows, value_rows, setup[AT_KEEP][kind], forms)
    mixed = mixed.reshape(-1, width_local).astype(jnp.bfloat16)
    branch = project_out(mixed, weight[:, :, 3, :].reshape(D, width_local)) + biases[2]
    saved = {
        AT_INPUT: x,
        AT_GATHERED: gathered,
        AT_QUERY: query,
        AT_KEY_ROWS: key_rows,
        AT_VALUE_ROWS: value_rows,
        AT_LOGSUM: logsum,
        AT_MIXED: mixed,
        AT_BRANCH: branch,
    }
    if kind == AT_CROSS:
        return (x + branch, saved)
    return (x + mods[2] * branch, saved)


def attention_backward(grad_x, index, mods, kind, saved, setup):
    weight = setup[AT_ATTN][index]
    heads = weight.shape[1]
    width_local = heads * HD
    part = setup[AT_PART]
    forms = attention_forms(kind)
    query = saved[AT_QUERY]
    if kind == AT_CROSS:
        gate_vec = 1.0
        d_gate = None
    else:
        gate_vec = mods[2]
        d_gate = jnp.sum(grad_x * saved[AT_BRANCH], 0)
    d_branch = (gate_vec * grad_x).astype(jnp.bfloat16)
    d_out_bias = jnp.sum(d_branch.astype(jnp.float32), 0)
    d_mixed, d_out_weight = back_out(
        d_branch, saved[AT_MIXED], weight[:, :, 3, :].reshape(D, width_local)
    )
    d_mixed = d_mixed.astype(jnp.bfloat16).reshape(query.shape)
    d_query, d_key, d_value = attend_backward(
        query,
        saved[AT_KEY_ROWS],
        saved[AT_VALUE_ROWS],
        setup[AT_KEEP][kind],
        forms,
        saved[AT_LOGSUM],
        d_mixed,
    )
    d_query = d_query.reshape(-1, heads, HD).astype(jnp.bfloat16)
    d_key = d_key.reshape(-1, heads, HD).astype(jnp.bfloat16)
    d_value = d_value.reshape(-1, heads, HD).astype(jnp.bfloat16)
    d_query_bias = jnp.sum(d_query.astype(jnp.float32), 0).reshape(-1)
    d_value_bias = jnp.sum(d_value.astype(jnp.float32), 0).reshape(-1)
    if kind == AT_CROSS:
        context = setup[AT_CONTEXT]
        d_query_weight = lax.dot_general(
            saved[AT_GATHERED],
            d_query.reshape(-1, width_local),
            CONTRACT_ROWS,
            preferred_element_type=jnp.float32,
        ).reshape(D, heads, 1, HD)
        d_key_weight = jnp.einsum("cd,che->dhe", context, d_key, preferred_element_type=jnp.float32)
        d_value_weight = jnp.einsum(
            "cd,che->dhe", context, d_value, preferred_element_type=jnp.float32
        )
        d_in = jnp.concatenate(
            [d_query_weight, d_key_weight[:, :, None], d_value_weight[:, :, None]], 2
        )
        d_context = jnp.einsum(
            "che,dhe->cd", d_key, weight[:, :, 1, :], preferred_element_type=jnp.float32
        ) + jnp.einsum(
            "che,dhe->cd", d_value, weight[:, :, 2, :], preferred_element_type=jnp.float32
        )
        grad_x = grad_x + back_in(
            d_query.reshape(-1, width_local), weight[:, :, 0, :].reshape(D, width_local)
        )
        mod_grads = None
    else:
        d_proj = jnp.stack([d_query, d_key, d_value], 2).reshape(-1, 3 * width_local)
        d_in = lax.dot_general(
            saved[AT_GATHERED], d_proj, CONTRACT_ROWS, preferred_element_type=jnp.float32
        ).reshape(D, heads, 3, HD)
        d_source = back_in(d_proj, weight[:, :, :3, :].reshape(D, 3 * width_local))
        unused, norm_pull = jax.vjp(modulate, saved[AT_INPUT], mods[0], mods[1])
        d_input, d_shift, d_scale = norm_pull(d_source)
        grad_x = grad_x + d_input
        mod_grads = (d_shift, d_scale, d_gate)
        d_context = None
    d_weight = jnp.concatenate([d_in, d_out_weight.reshape(D, heads, 1, HD)], 2)
    d_bias = jnp.stack([placed(d_query_bias, part, D), placed(d_value_bias, part, D), d_out_bias])
    return (grad_x, d_weight, d_bias, mod_grads, d_context)


def ffn_forward(x, index, mods, setup):
    weight_in = setup[AT_FFN][index, 0]
    weight_out = setup[AT_FFN][index, 1]
    source = modulate(x, mods[3], mods[4])
    pre, gathered = project_in(source.astype(jnp.bfloat16), weight_in)
    pre = pre + own_slice(setup[AT_PARTS][FFN_BIAS_ONE][index], setup[AT_PART], weight_in.shape[1])
    hidden = gelu_tanh(pre).astype(jnp.bfloat16)
    branch = project_out(hidden, weight_out) + setup[AT_PARTS][FFN_BIAS_TWO][index]
    saved = {AT_INPUT: x, AT_GATHERED: gathered, AT_PRE: pre, AT_HIDDEN: hidden, AT_BRANCH: branch}
    return (x + mods[5] * branch, saved)


def ffn_backward(grad_x, index, mods, saved, setup):
    weight_in = setup[AT_FFN][index, 0]
    weight_out = setup[AT_FFN][index, 1]
    d_gate = jnp.sum(grad_x * saved[AT_BRANCH], 0)
    d_branch = (mods[5] * grad_x).astype(jnp.bfloat16)
    d_bias_two = jnp.sum(d_branch.astype(jnp.float32), 0)
    d_hidden, d_weight_out = back_out(d_branch, saved[AT_HIDDEN], weight_out)
    unused, gelu_pull = jax.vjp(gelu_tanh, saved[AT_PRE])
    d_pre = gelu_pull(d_hidden)[0].astype(jnp.bfloat16)
    d_bias_one = jnp.sum(d_pre.astype(jnp.float32), 0)
    d_weight_in = lax.dot_general(
        saved[AT_GATHERED], d_pre, CONTRACT_ROWS, preferred_element_type=jnp.float32
    )
    d_source = back_in(d_pre, weight_in)
    unused, norm_pull = jax.vjp(modulate, saved[AT_INPUT], mods[3], mods[4])
    d_input, d_shift, d_scale = norm_pull(d_source)
    biases = (placed(d_bias_one, setup[AT_PART], FF), d_bias_two)
    return (
        grad_x + d_input,
        jnp.stack([d_weight_in, d_weight_out]),
        biases,
        (d_shift, d_scale, d_gate),
    )


def block_forward(x, kind, mods, setup):
    index = 0 if kind == AT_SPACE else 1
    x, first = attention_forward(x, index, mods, kind, setup)
    second = None
    if kind == AT_SPACE:
        x, second = attention_forward(x, 2, mods, AT_CROSS, setup)
    x, third = ffn_forward(x, index, mods, setup)
    return (x, (first, second, third))


def block_backward(grad_x, kind, mods, saved, setup):
    index = 0 if kind == AT_SPACE else 1
    first, second, third = saved
    grad_x, d_ffn, d_ffn_bias, ffn_mods = ffn_backward(grad_x, index, mods, third, setup)
    cross_part = None
    if kind == AT_SPACE:
        grad_x, d_cross, d_cross_bias, unused, d_context = attention_backward(
            grad_x, 2, mods, AT_CROSS, second, setup
        )
        cross_part = (d_cross, d_cross_bias, d_context)
    grad_x, d_attn, d_attn_bias, attn_mods, unused = attention_backward(
        grad_x, index, mods, kind, first, setup
    )
    d_mods = jnp.stack(list(attn_mods) + list(ffn_mods))
    return (grad_x, (d_attn, d_attn_bias, d_ffn, d_ffn_bias, d_mods), cross_part)


def adam_update(weight, first, second, ema, grad, rate):
    first_new = BETA_FIRST * first + (1.0 - BETA_FIRST) * grad
    second_new = BETA_SECOND * second + (1.0 - BETA_SECOND) * grad * grad
    corr_one = 1.0 - BETA_FIRST**STEP
    corr_two = 1.0 - BETA_SECOND**STEP
    weight_new = weight - rate * (
        first_new / corr_one / (jnp.sqrt(second_new / corr_two) + ADAM_EPSILON)
        + WEIGHT_DECAY * weight
    )
    return (first_new, second_new, weight_new, EMA_DECAY * ema + (1.0 - EMA_DECAY) * weight_new)


def per_device(
    latents,
    noise,
    caption,
    caption_lens,
    timesteps,
    grid_hw,
    frame_counts,
    attn_mats,
    ffn_mats,
    embed_mats,
    vectors,
    attn_first,
    ffn_first,
    embed_first,
    vector_first,
    attn_second,
    ffn_second,
    embed_second,
    vector_second,
    attn_ema,
    ffn_ema,
    embed_ema,
    vector_ema,
):
    group = lax.axis_index(DP)
    part = lax.axis_index(MP)
    mp_size = lax.axis_size(MP)
    rows = latents.shape[1]
    heads = HEADS // mp_size
    width_local = D // mp_size
    attn_all, ffn_all, embed_all = (
        lax.all_gather(attn_mats.astype(jnp.bfloat16), DP, axis=1, tiled=True),
        lax.all_gather(ffn_mats.astype(jnp.bfloat16), DP, axis=2, tiled=True),
        lax.all_gather(embed_mats.astype(jnp.bfloat16), DP, axis=0, tiled=True),
    )
    parts = unpack(vectors)
    pick = jnp.arange(timesteps.shape[0], dtype=jnp.int32) == group

    def select(values):
        return jnp.sum(jnp.where(pick, values, 0))

    tstep = select(timesteps)
    cap_len = select(caption_lens)
    height = select(grid_hw[:, 0])
    width_grid = select(grid_hw[:, 1])
    frames = select(frame_counts)
    count = jnp.sum(frame_counts * grid_hw[:, 0] * grid_hw[:, 1]).astype(jnp.float32)
    betas, cumul = roster()
    step_ids = jnp.arange(1000, dtype=jnp.int32)
    alpha_bar = jnp.sum(jnp.where(step_ids == tstep, cumul, 0.0))
    alpha_prev = jnp.sum(jnp.where(step_ids == tstep - 1, cumul, 0.0))
    beta_now = jnp.sum(jnp.where(step_ids == tstep, betas, 0.0))
    t_one = embed_all[:TFREQ]
    c_one = embed_all[TFREQ : TFREQ + TXT]
    t_two = embed_all[TFREQ + TXT : TFREQ + TXT + D]
    c_two = embed_all[TFREQ + TXT + D : TFREQ + TXT + 2 * D]
    t_mod = embed_all[TFREQ + TXT + 2 * D :]
    freq = waves(tstep.astype(jnp.float32), TFREQ).astype(jnp.bfloat16)
    t_pre = jnp.dot(freq, t_one, preferred_element_type=jnp.float32) + own_slice(
        parts[T_BIAS_ONE], part, width_local
    )
    t_hidden = jax.nn.silu(t_pre).astype(jnp.bfloat16)
    t_part = jnp.dot(t_two, t_hidden, preferred_element_type=jnp.float32)
    caption_rows = caption[0]
    c_pre = jnp.dot(caption_rows, c_one, preferred_element_type=jnp.float32) + own_slice(
        parts[C_BIAS_ONE], part, width_local
    )
    c_hidden = gelu_tanh(c_pre).astype(jnp.bfloat16)
    c_part = lax.dot_general(c_hidden, c_two, CONTRACT_LAST, preferred_element_type=jnp.float32)
    t_sum, c_sum = (
        lax.psum(t_part.astype(jnp.bfloat16), MP).astype(jnp.float32),
        lax.psum(c_part.astype(jnp.bfloat16), MP).astype(jnp.float32),
    )
    t_emb = t_sum + parts[T_BIAS_TWO]
    context = (c_sum + parts[C_BIAS_TWO]).astype(jnp.bfloat16)
    t_emb_local = own_slice(t_emb, part, width_local)
    silu_local = jax.nn.silu(t_emb_local).astype(jnp.bfloat16)
    t_mod_vec = (
        lax.psum(jnp.dot(t_mod, silu_local, preferred_element_type=jnp.float32), MP)
        + parts[T_BIAS_MOD]
    )
    token_ids = part * rows + jnp.arange(rows, dtype=jnp.int32)
    frame_slot = token_ids // PM
    patch_slot = token_ids % PM
    area = height * width_grid
    shifted = patch_slot - (PM - area)
    valid = (frame_slot >= FR - frames) & (patch_slot >= PM - area)
    setup = {
        AT_ATTN: attn_all.reshape(3, D, heads, 4, HD),
        AT_FFN: ffn_all,
        AT_PARTS: parts,
        AT_PART: part,
        AT_CONTEXT: context,
        AT_KEEP: {
            AT_SPACE: (jnp.arange(PM, dtype=jnp.int32) >= PM - area).reshape(1, 1, 1, PM),
            AT_TIME: (jnp.arange(FR, dtype=jnp.int32) >= FR - frames).reshape(1, 1, 1, FR),
            AT_CROSS: (jnp.arange(CAP, dtype=jnp.int32) < cap_len).reshape(1, 1, CAP),
        },
    }
    noisy = jnp.sqrt(alpha_bar) * latents[0] + jnp.sqrt(1.0 - alpha_bar) * noise[0]
    noisy_low = noisy.astype(jnp.bfloat16)
    position = jnp.concatenate(
        [
            waves((shifted // width_grid).astype(jnp.float32), D // 2),
            waves((shifted % width_grid).astype(jnp.float32), D // 2),
        ],
        -1,
    )
    x = jnp.dot(
        noisy_low, parts[PATCH_W].astype(jnp.bfloat16), preferred_element_type=jnp.float32
    )
    x = x + parts[PATCH_B] + position
    tables = parts[TABLES] + t_mod_vec.reshape(1, 6, D)
    x, saved_space = block_forward(x, AT_SPACE, tables[0], setup)
    x = x + waves((frame_slot - (FR - frames)).astype(jnp.float32), D)
    x, saved_time = block_forward(x, AT_TIME, tables[1], setup)
    final_mods = parts[FINAL_TABLE] + t_emb
    final_source = modulate(x, final_mods[0], final_mods[1]).astype(jnp.bfloat16)
    final_low = parts[FINAL_W].astype(jnp.bfloat16)
    output = (
        lax.dot_general(final_source, final_low, CONTRACT_LAST, preferred_element_type=jnp.float32)
        + parts[FINAL_B]
    )
    frozen = output[:, :CIN]

    def shard_loss(values):
        losses = token_losses(
            values, frozen, latents[0], noise[0], (noisy, alpha_bar, alpha_prev, beta_now)
        )
        return jnp.sum(jnp.where(valid, losses, 0.0))

    loss_part, loss_pull = jax.vjp(shard_loss, output)
    loss_total = lax.psum(loss_part, (DP, MP))
    d_output = loss_pull(1.0 / count)[0].astype(jnp.bfloat16)
    d_final_w = lax.dot_general(
        d_output, final_source, CONTRACT_ROWS, preferred_element_type=jnp.float32
    )
    d_final_b = jnp.sum(d_output.astype(jnp.float32), 0)
    d_final_source = jnp.dot(d_output, final_low, preferred_element_type=jnp.float32)
    unused, final_pull = jax.vjp(modulate, x, final_mods[0], final_mods[1])
    grad_x, d_final_shift, d_final_scale = final_pull(d_final_source)
    grad_x, time_grads, unused = block_backward(grad_x, AT_TIME, tables[1], saved_time, setup)
    grad_x, space_grads, cross_grads = block_backward(
        grad_x, AT_SPACE, tables[0], saved_space, setup
    )
    d_patch = grad_x.astype(jnp.bfloat16)
    d_patch_b = jnp.sum(d_patch.astype(jnp.float32), 0)
    d_patch_w = lax.dot_general(
        noisy_low, d_patch, CONTRACT_ROWS, preferred_element_type=jnp.float32
    )
    d_mod_part = space_grads[4].reshape(-1) + time_grads[4].reshape(-1)
    d_temb_part = d_final_shift + d_final_scale
    d_mod_vec, d_temb_sum, d_context = (
        lax.psum(d_mod_part.astype(jnp.bfloat16), MP).astype(jnp.float32),
        lax.psum(d_temb_part.astype(jnp.bfloat16), MP).astype(jnp.float32),
        lax.psum(cross_grads[2].astype(jnp.bfloat16), MP).astype(jnp.float32),
    )
    d_t_mod = jnp.outer(d_mod_vec, silu_local.astype(jnp.float32))
    d_silu_local = jnp.dot(d_mod_vec, t_mod, preferred_element_type=jnp.float32)
    unused, silu_pull = jax.vjp(jax.nn.silu, t_emb_local)
    d_temb_local = silu_pull(d_silu_local)[0]
    d_temb = d_temb_sum + lax.all_gather(d_temb_local, MP, axis=0, tiled=True)
    d_t_two = jnp.outer(d_temb, t_hidden.astype(jnp.float32))
    d_t_hidden = jnp.dot(d_temb, t_two, preferred_element_type=jnp.float32)
    unused, pre_pull = jax.vjp(jax.nn.silu, t_pre)
    d_t_pre = pre_pull(d_t_hidden)[0]
    d_t_one = jnp.outer(freq.astype(jnp.float32), d_t_pre)
    d_context = d_context.astype(jnp.bfloat16)
    d_c_bias_two = jnp.sum(d_context.astype(jnp.float32), 0) * (part == 0).astype(jnp.float32)
    d_c_two = lax.dot_general(
        d_context, c_hidden, CONTRACT_ROWS, preferred_element_type=jnp.float32
    )
    d_c_hidden = jnp.dot(d_context, c_two, preferred_element_type=jnp.float32)
    unused, cap_pull = jax.vjp(gelu_tanh, c_pre)
    d_c_pre = cap_pull(d_c_hidden)[0].astype(jnp.bfloat16)
    d_c_one = lax.dot_general(
        caption_rows, d_c_pre, CONTRACT_ROWS, preferred_element_type=jnp.float32
    )
    d_c_bias_one = jnp.sum(d_c_pre.astype(jnp.float32), 0)
    d_attn = jnp.stack([space_grads[0], time_grads[0], cross_grads[0]]).reshape(
        3, D, heads * 4 * HD
    )
    d_ffn = jnp.stack([space_grads[2], time_grads[2]])
    d_embed = jnp.concatenate([d_t_one, d_c_one, d_t_two, d_c_two, d_t_mod], 0)
    vector_grads = {
        PATCH_W: d_patch_w,
        PATCH_B: d_patch_b,
        FINAL_W: d_final_w,
        FINAL_B: d_final_b,
        T_BIAS_ONE: placed(d_t_pre, part, D),
        T_BIAS_TWO: d_temb_part + placed(d_temb_local, part, D),
        T_BIAS_MOD: d_mod_part,
        C_BIAS_ONE: placed(d_c_bias_one, part, D),
        C_BIAS_TWO: d_c_bias_two,
        ATTN_BIAS: jnp.stack([space_grads[1], time_grads[1], cross_grads[1]]),
        FFN_BIAS_ONE: jnp.stack([space_grads[3][0], time_grads[3][0]]),
        FFN_BIAS_TWO: jnp.stack([space_grads[3][1], time_grads[3][1]]),
        TABLES: jnp.stack([space_grads[4], time_grads[4]]),
        FINAL_TABLE: jnp.stack([d_final_shift, d_final_scale]),
    }
    vector_grad = jnp.concatenate(
        [vector_grads[label].reshape(-1) for label, extent in vector_parts()]
    )
    g_attn, g_ffn, g_embed = (
        lax.psum_scatter(d_attn.astype(jnp.bfloat16), DP, scatter_dimension=1, tiled=True).astype(
            jnp.float32
        ),
        lax.psum_scatter(d_ffn.astype(jnp.bfloat16), DP, scatter_dimension=2, tiled=True).astype(
            jnp.float32
        ),
        lax.psum_scatter(
            d_embed.astype(jnp.bfloat16), DP, scatter_dimension=0, tiled=True
        ).astype(jnp.float32),
    )
    g_vector = lax.psum(vector_grad, (DP, MP))
    matrix_squares = jnp.sum(g_attn * g_attn) + jnp.sum(g_ffn * g_ffn) + jnp.sum(g_embed * g_embed)
    squares = lax.psum(matrix_squares, (DP, MP)) + jnp.sum(g_vector * g_vector)
    grad_norm = jnp.sqrt(squares)
    factor = CLIP_NORM / (grad_norm + 1e-06)
    new_attn = adam_update(
        attn_mats, attn_first, attn_second, attn_ema, g_attn * factor, LEARN_RATE
    )
    new_ffn = adam_update(ffn_mats, ffn_first, ffn_second, ffn_ema, g_ffn * factor, LEARN_RATE)
    new_embed = adam_update(
        embed_mats, embed_first, embed_second, embed_ema, g_embed * factor, LEARN_RATE
    )
    new_vector = adam_update(
        vectors, vector_first, vector_second, vector_ema, g_vector * factor, VECTOR_RATE
    )
    return (
        loss_total,
        count,
        grad_norm,
        new_attn[0],
        new_ffn[0],
        new_embed[0],
        new_vector[0],
        new_attn[1],
        new_ffn[1],
        new_embed[1],
        new_vector[1],
        new_attn[2],
        new_ffn[2],
        new_embed[2],
        new_vector[2],
        new_attn[3],
        new_ffn[3],
        new_embed[3],
        new_vector[3],
    )


SPAN = 4 * HD
EMB_ALL = TFREQ + TXT + 8 * D
EMB_LOCAL = EMB_ALL // 8
MESH = pl.DeviceIdType.MESH
BLOCK = 144
BIG = 58 * 2**20
PIECES = {1: 2, 2: 1}


class Chips:
    def __init__(self):
        dp = lax.axis_index(DP)
        mp = lax.axis_index(MP)
        self.z, self.x = dp // 2, dp % 2
        self.y, self.c = mp // 2, mp % 2

    def z_at(self, j):
        z = self.z
        return (z, z + 1 - 2 * (z % 2), z + 2 - 4 * (z // 2), 3 - z)[j]

    def dp_at(self, jz, jx):
        return self.z_at(jz) * 2 + (1 - self.x if jx else self.x)

    def mp_at(self, jy, jc):
        return (1 - self.y if jy else self.y) * 2 + (1 - self.c if jc else self.c)

    def peer_x(self):
        return {DP: self.dp_at(0, 1)}

    def peer_y(self):
        return {MP: self.mp_at(1, 0)}

    def peer_core(self):
        return {MP: self.mp_at(0, 1)}

    def peer_z(self, j):
        return {DP: self.dp_at(j, 0)}

    def greet(self):
        barrier = pltpu.get_barrier_semaphore()
        peers = [self.peer_x(), self.peer_y(), self.peer_core()]
        peers += [self.peer_z(j) for j in (1, 2, 3)]
        for peer in peers:
            pl.semaphore_signal(barrier, inc=1, device_id=peer, device_id_type=MESH)
        pl.semaphore_wait(barrier, len(peers))


class Work:
    def __init__(self, chips, send, recv):
        self.chips, self.send, self.recv = chips, send, recv
        self.started = []

    def start(self, src, dst, slot, peer):
        def copy():
            return pltpu.make_async_remote_copy(
                src_ref=src(),
                dst_ref=dst(),
                send_sem=self.send.at[slot],
                recv_sem=self.recv.at[slot],
                device_id=peer(),
                device_id_type=MESH,
            )

        copy().start()
        self.started.append(copy)

    def arrived(self, dst, slot):
        pltpu.make_async_remote_copy(
            src_ref=dst,
            dst_ref=dst,
            send_sem=self.send.at[slot],
            recv_sem=self.recv.at[slot],
            device_id=self.chips.peer_core(),
            device_id_type=MESH,
        ).wait_recv()

    def finish(self):
        for copy in self.started:
            copy().wait_send()


class Gather(Work):
    def __init__(self, chips, shard, full, send, recv, local):
        super().__init__(chips, send, recv)
        self.shard, self.full, self.local = shard, full, local

    def block(self, jy, jz, jx, jc=0):
        chips = self.chips
        return self.full.at[:, chips.mp_at(jy, jc), chips.dp_at(jz, jx)]

    def arrive(self, jy, jz, jx, jc=0):
        self.arrived(self.block(jy, jz, jx, jc), jc * 16 + jy * 8 + jz * 2 + jx)

    def pass_on(self, place, slot, peer):
        self.start(lambda: self.block(*place), lambda: self.block(*place), slot, peer)

    def core(self, jy, jz, jx):
        self.pass_on((jy, jz, jx), 16 + jy * 8 + jz * 2 + jx, self.chips.peer_core)

    def own(self):
        return pltpu.make_async_copy(self.shard, self.block(0, 0, 0), self.local)

    def begin(self):
        chips = self.chips
        shard, block = (lambda: self.shard), (lambda: self.block(0, 0, 0))
        self.start(shard, block, 1, chips.peer_x)
        self.start(shard, block, 8, chips.peer_y)
        for j in (1, 2, 3):
            self.start(shard, block, 2 * j, functools.partial(chips.peer_z, j))
        self.start(shard, block, 16, chips.peer_core)
        self.own().start()

    def second(self, jz):
        self.arrive(0, jz, 0)
        self.pass_on((0, jz, 0), jz * 2 + 1, self.chips.peer_x)
        self.pass_on((0, jz, 0), jz * 2 + 8, self.chips.peer_y)
        self.core(0, jz, 0)

    def third(self, jz):
        place = (0, jz, 1) if jz < 2 else (1, jz, 0)
        self.arrive(*place)
        self.pass_on(place, 9 + jz * 2, self.chips.peer_y if jz < 2 else self.chips.peer_x)
        self.core(*place)

    def fourth(self, jz):
        place = (1, jz, 0) if jz < 2 else (0, jz, 1)
        self.arrive(*place)
        self.core(*place)

    def fifth(self, jz):
        self.arrive(1, jz, 1)
        self.core(1, jz, 1)

    def last(self):
        self.own().wait()
        for jy in range(2):
            for jz in range(4):
                for jx in range(2):
                    self.arrive(jy, jz, jx, 1)
        self.finish()

    def steps(self):
        order = (0, 2, 1, 3)
        parts = [[self.begin]]
        parts.append([functools.partial(self.second, j) for j in (1, 2, 3)])
        parts.append([functools.partial(self.third, j) for j in order])
        parts.append([functools.partial(self.fourth, j) for j in order])
        parts.append([functools.partial(self.fifth, j) for j in order])
        parts.append([self.last])
        return parts


GATHER_SEMS = [
    pltpu.SemaphoreType.DMA((32,)),
    pltpu.SemaphoreType.DMA((32,)),
    pltpu.SemaphoreType.DMA,
]


class Ticks:
    def __init__(self, steps, spots):
        self.step = pl.program_id(0)
        total = 4 * spots
        self.table = [[] for unused in range(total)]
        count = len(steps)
        for i, step in enumerate(steps):
            at = 0 if i == 0 else total - 1 if i == count - 1 else 1 + (i - 1) * (total - 2) // (count - 2)
            self.table[at].append(step)
        self.spots = spots

    def __call__(self, spot):
        for turn in range(4):
            todo = self.table[turn * self.spots + spot]
            if todo:

                @pl.when(self.step == turn)
                def run(todo=todo):
                    for step in todo:
                        step()


def no_ticks(spot):
    return None


def gather_ticks(refs, spots):
    chips = Chips()
    work = Gather(chips, *refs)
    steps = [step for phase in work.steps() for step in phase]
    begin = steps[0]

    def enter():
        chips.greet()
        begin()

    return Ticks([enter] + steps[1:], spots)


def gather_kernel(count, *refs):
    shards, fulls, sems = refs[:count], refs[count : 2 * count], refs[2 * count :]
    chips = Chips()
    chips.greet()
    plans = [Gather(chips, shards[i], fulls[i], *sems[3 * i : 3 * i + 3]).steps() for i in range(count)]
    for step in woven(plans):
        step()


def gather_all(shards, ident):
    count = len(shards)
    return pl.pallas_call(
        functools.partial(gather_kernel, count),
        out_shape=[jax.ShapeDtypeStruct((s.shape[0], 4, 8) + s.shape[1:], s.dtype) for s in shards],
        in_specs=[pl.BlockSpec(memory_space=pl.ANY)] * count,
        out_specs=[pl.BlockSpec(memory_space=pl.ANY)] * count,
        scratch_shapes=GATHER_SEMS * count,
        compiler_params=pltpu.CompilerParams(collective_id=ident, has_side_effects=True),
    )(*shards)


class Scatter(Work):
    def __init__(self, chips, full, total, m, row, near, far, own, send, recv, load):
        super().__init__(chips, send, recv)
        self.full, self.total = full, total
        self.m, self.row, self.size = m, row, near.shape[1]
        self.near, self.far, self.own, self.load = near, far, own, load
        diagonal = [(1, jz, 1) for jz in (0, 2, 1, 3)]
        straight = [(1, jz, 0) if jz < 2 else (0, jz, 1) for jz in (0, 2, 1, 3)]
        bent = [(0, jz, 1) if jz < 2 else (1, jz, 0) for jz in (0, 2, 1, 3)]
        column = [(0, jz, 0) for jz in (2, 3, 1, 0)]
        self.order = diagonal + straight + bent + column
        self.turns = {jy * 8 + jz * 2 + jx: i for i, (jy, jz, jx) in enumerate(self.order)}

    def block(self, jy, jz, jx, jc):
        chips = self.chips
        return self.full.at[
            self.m, chips.mp_at(jy, jc), chips.dp_at(jz, jx), pl.ds(self.row, self.size)
        ]

    def fetch(self, turn):
        buffer = turn % self.own.shape[0]
        return pltpu.make_async_copy(
            self.block(*self.order[turn], 0), self.own.at[buffer], self.load.at[buffer]
        )

    def begin(self):
        for place in self.order:
            slot = place[0] * 8 + place[1] * 2 + place[2]
            self.start(
                functools.partial(self.block, *place, 1),
                functools.partial(lambda at: self.near.at[at], slot),
                slot,
                self.chips.peer_core,
            )
        for turn in range(self.own.shape[0]):
            self.fetch(turn).start()

    def add(self, slot, others):
        turn, near, own = self.turns[slot], self.near, self.own
        buffer = turn % own.shape[0]
        self.fetch(turn).wait()
        self.arrived(near.at[slot], slot)

        def rows(i, carry):
            at = pl.ds(pl.multiple_of(i * 16, 16), 16)
            value = near[slot, at].astype(jnp.float32) + own[buffer, at].astype(jnp.float32)
            for index in others:
                value += self.far[index, at].astype(jnp.float32)
            near[slot, at] = value.astype(jnp.bfloat16)
            return carry

        lax.fori_loop(0, self.size // 16, rows, 0)
        if turn + own.shape[0] < 16:
            self.fetch(turn + own.shape[0]).start()

    def move(self, slot, index, where, peer):
        self.start(lambda: self.near.at[slot], lambda: self.far.at[index], where, peer)

    def along_x(self, slot, jz):
        self.move(slot, 4 + jz, 20 + jz, self.chips.peer_x)

    def along_y(self, slot, jz):
        self.move(slot, 8 + jz, 24 + jz, self.chips.peer_y)

    def diagonal(self, jz):
        slot = 9 + jz * 2
        self.add(slot, [])
        self.move(slot, jz, 16 + jz, self.chips.peer_y if jz < 2 else self.chips.peer_x)

    def straight(self, jz):
        slot = jz * 2 + (8 if jz < 2 else 1)
        self.add(slot, [])
        (self.along_y if jz < 2 else self.along_x)(slot, jz)

    def bent(self, jz):
        slot = jz * 2 + (1 if jz < 2 else 8)
        self.arrived(self.far.at[jz], 16 + jz)
        self.add(slot, [jz])
        (self.along_x if jz < 2 else self.along_y)(slot, jz)

    def column(self, jz):
        self.arrived(self.far.at[4 + jz], 20 + jz)
        self.arrived(self.far.at[8 + jz], 24 + jz)
        if jz:
            self.add(jz * 2, [4 + jz, 8 + jz])
            self.move(jz * 2, 11 + jz, 27 + jz, functools.partial(self.chips.peer_z, jz))

    def last(self):
        turn, near, own, far = 15, self.near, self.own, self.far
        buffer = turn % own.shape[0]
        self.fetch(turn).wait()
        self.arrived(near.at[0], 0)
        for jz in (2, 3, 1):
            self.arrived(far.at[11 + jz], 27 + jz)

        def rows(i, carry):
            at = pl.ds(pl.multiple_of(i * 16, 16), 16)
            value = near[0, at].astype(jnp.float32) + own[buffer, at].astype(jnp.float32)
            for index in (4, 8, 12, 13, 14):
                value += far[index, at].astype(jnp.float32)
            self.total[self.m, pl.ds(pl.multiple_of(self.row + i * 16, 16), 16)] = value
            return carry

        lax.fori_loop(0, self.size // 16, rows, 0)

    def steps(self):
        order = (0, 2, 1, 3)
        parts = [[self.begin]]
        parts.append([functools.partial(self.diagonal, j) for j in order])
        parts[-1] += [functools.partial(self.straight, j) for j in order]
        parts.append([functools.partial(self.bent, j) for j in order])
        parts.append([functools.partial(self.column, j) for j in (2, 3, 1, 0)])
        parts.append([self.last])
        return parts


def chunks_of(k, pieces):
    sizes = {1: [144], 2: [80, 64], 3: [48, 48, 48]}[pieces]
    return [(m, sum(sizes[:i]), sizes[i]) for m in range(k) for i in range(pieces)]


def scatter_scratch(chunks):
    out = []
    for unused, unused_row, size in chunks:
        out += [
            pltpu.VMEM((16, size, 1152), jnp.bfloat16),
            pltpu.VMEM((15, size, 1152), jnp.bfloat16),
            pltpu.VMEM((4, size, 1152), jnp.bfloat16),
            pltpu.SemaphoreType.DMA((31,)),
            pltpu.SemaphoreType.DMA((31,)),
            pltpu.SemaphoreType.DMA((4,)),
        ]
    return out


def woven(plans):
    order = []
    deep = max(len(plan) for plan in plans)
    for turn in range(len(plans) + deep - 1):
        for i, plan in enumerate(plans):
            if 0 <= turn - i < len(plan):
                order += plan[turn - i]
    return order


def scatter_kernel(chunks, full, total, *scratch):
    chips = Chips()
    chips.greet()
    works = [
        Scatter(chips, full, total, m, row, *scratch[6 * i : 6 * i + 6])
        for i, (m, row, unused) in enumerate(chunks)
    ]
    for step in woven([work.steps() for work in works]):
        step()
    for work in works:
        work.finish()


def scatter_one(full, ident, pieces=PIECES):
    k = full.shape[0]
    chunks = chunks_of(k, pieces[k])
    return pl.pallas_call(
        functools.partial(scatter_kernel, chunks),
        out_shape=jax.ShapeDtypeStruct((k,) + full.shape[3:], jnp.float32),
        in_specs=[pl.BlockSpec(memory_space=pl.ANY)],
        out_specs=pl.BlockSpec(memory_space=pltpu.VMEM),
        scratch_shapes=scatter_scratch(chunks),
        compiler_params=pltpu.CompilerParams(
            collective_id=ident, has_side_effects=True, vmem_limit_bytes=BIG
        ),
    )(full)


CLIPS, PARTS = 8, 4


def all_peers(names):
    peers = []
    for name, size in ((DP, CLIPS), (MP, PARTS)):
        if name in names:
            me = lax.axis_index(name)
            peers += [{name: (me + o) % size} for o in range(1, size)]
    return peers


def greet_all(peers):
    barrier = pltpu.get_barrier_semaphore()
    for peer in peers:
        pl.semaphore_signal(barrier, inc=1, device_id=peer, device_id_type=MESH)
    pl.semaphore_wait(barrier, len(peers))


def trade(name, size, source, target, landing, send, recv, first=0):
    me = lax.axis_index(name)

    def copy(o, src, dst):
        return pltpu.make_async_remote_copy(
            src_ref=src,
            dst_ref=dst,
            send_sem=send.at[first + o],
            recv_sem=recv.at[first + o],
            device_id={name: (me + o) % size},
            device_id_type=MESH,
        )

    out = [copy(o, source((me + o) % size), target()) for o in range(1, size)]
    for one in out:
        one.start()
    for o in range(1, size):
        land = landing((me + size - o) % size)
        copy(o, land, land).wait_recv()
    for one in out:
        one.wait_send()


def exchange_call(kernel, ident, out_shape, scratch, operand, anywhere=False):
    spec = pl.BlockSpec(memory_space=pl.ANY if anywhere else pltpu.VMEM)
    return pl.pallas_call(
        kernel,
        out_shape=out_shape,
        in_specs=[spec],
        out_specs=spec,
        scratch_shapes=scratch + [pltpu.SemaphoreType.DMA((18,)), pltpu.SemaphoreType.DMA((18,))],
        compiler_params=pltpu.CompilerParams(
            collective_id=ident, has_side_effects=True, vmem_limit_bytes=BIG
        ),
    )(operand)


def share_kernel(name, size, x, out, send, recv):
    me = lax.axis_index(name)
    greet_all(all_peers((name,)))
    out[me] = x[...]
    trade(name, size, lambda to: x, lambda: out.at[me], lambda at: out.at[at], send, recv)


def share(x, name, ident):
    size = CLIPS if name == DP else PARTS
    shape = jax.ShapeDtypeStruct((size,) + x.shape, x.dtype)
    return exchange_call(functools.partial(share_kernel, name, size), ident, shape, [], x)


def gathered_sum(refs, count):
    value = refs[0]
    for i in range(1, count):
        value = value + refs[i]
    return value


def part_sum_kernel(x, out, near, one, send, recv):
    part, clip = lax.axis_index(MP), lax.axis_index(DP)
    greet_all(all_peers((DP, MP)))
    near[part] = x[...]
    trade(MP, PARTS, lambda to: x, lambda: near.at[part], lambda at: near.at[at], send, recv, 8)
    one[...] = gathered_sum(near, PARTS)
    out[clip] = one[...]
    trade(DP, CLIPS, lambda to: one, lambda: out.at[clip], lambda at: out.at[at], send, recv)


def part_sum(x, ident):
    scratch = [pltpu.VMEM((PARTS,) + x.shape, x.dtype), pltpu.VMEM(x.shape, x.dtype)]
    shape = jax.ShapeDtypeStruct((CLIPS,) + x.shape, x.dtype)
    return exchange_call(part_sum_kernel, ident, shape, scratch, x)


def whole_sum_kernel(x, out, far, near, one, two, send, recv):
    part, clip = lax.axis_index(MP), lax.axis_index(DP)
    greet_all(all_peers((DP, MP)))
    far[clip] = x[clip]
    trade(DP, CLIPS, lambda to: x.at[to], lambda: far.at[clip], lambda at: far.at[at], send, recv)
    one[...] = gathered_sum(far, CLIPS)
    near[part] = one[...]
    trade(MP, PARTS, lambda to: one, lambda: near.at[part], lambda at: near.at[at], send, recv, 7)
    two[...] = gathered_sum(near, PARTS)
    out[clip] = two[...]
    trade(DP, CLIPS, lambda to: two, lambda: out.at[clip], lambda at: out.at[at], send, recv, 10)


def whole_sum(x, ident):
    row = x.shape[1:]
    scratch = [pltpu.VMEM((n,) + row, x.dtype) for n in (CLIPS, PARTS)]
    scratch += [pltpu.VMEM(row, x.dtype)] * 2
    return exchange_call(whole_sum_kernel, ident, jax.ShapeDtypeStruct(x.shape, x.dtype), scratch, x)


def deal_kernel(x, out, send, recv):
    clip = lax.axis_index(DP)
    greet_all(all_peers((DP,)))
    out[clip] = x[clip]
    trade(DP, CLIPS, lambda to: x.at[to], lambda: out.at[clip], lambda at: out.at[at], send, recv)


def deal(x, ident):
    return exchange_call(deal_kernel, ident, jax.ShapeDtypeStruct(x.shape, x.dtype), [], x)


def to_time_kernel(x, out, local, send, recv):
    part = lax.axis_index(MP)
    greet_all(all_peers((MP,)))
    own = pltpu.make_async_copy(x.at[part], out.at[:, part], local)
    own.start()
    trade(MP, PARTS, lambda to: x.at[to], lambda: out.at[:, part], lambda at: out.at[:, at], send, recv)
    own.wait()


def to_space_kernel(x, out, local, send, recv):
    part = lax.axis_index(MP)
    greet_all(all_peers((MP,)))
    own = pltpu.make_async_copy(x.at[:, part], out.at[part], local)
    own.start()
    trade(MP, PARTS, lambda to: x.at[:, to], lambda: out.at[part], lambda at: out.at[at], send, recv)
    own.wait()


def to_time(x, ident):
    shape = jax.ShapeDtypeStruct((2, FR, PM // 8, D), x.dtype)
    operand = x.reshape(FR, 2, PM // 8, D)
    return exchange_call(
        to_time_kernel, ident, shape, [pltpu.SemaphoreType.DMA], operand, True
    ).reshape(PM, D)


def to_space(x, ident):
    shape = jax.ShapeDtypeStruct((FR, 2, PM // 8, D), x.dtype)
    operand = x.reshape(2, FR, PM // 8, D)
    return exchange_call(
        to_space_kernel, ident, shape, [pltpu.SemaphoreType.DMA], operand, True
    ).reshape(PM, D)


def normal_parts(x):
    centered = x - jnp.mean(x, -1, keepdims=True)
    inverse = lax.rsqrt(jnp.mean(centered * centered, -1, keepdims=True) + EPS_NORM)
    return centered * inverse, inverse


def normal_back(x, scale_vec, grad):
    normed, inverse = normal_parts(x)
    inner = grad * (1.0 + scale_vec)
    d_x = inverse * (
        inner
        - jnp.mean(inner, -1, keepdims=True)
        - normed * jnp.mean(inner * normed, -1, keepdims=True)
    )
    return d_x, jnp.sum(grad, 0, keepdims=True), jnp.sum(grad * normed, 0, keepdims=True)


def mxu(left, right, dims=(((1,), (0,)), ((), ()))):
    return lax.dot_general(left, right, dims, preferred_element_type=jnp.float32)


def padded_heads(pieces, before, after):
    rows = pieces[0].shape[0]
    parts = list(pieces)
    if before:
        parts.insert(0, jnp.zeros((rows, before), pieces[0].dtype))
    if after:
        parts.append(jnp.zeros((rows, after), pieces[0].dtype))
    return jnp.concatenate(parts, 1)


def head_forward(query, key_rows, value_rows, bias):
    scores = mxu(key_rows, query, CONTRACT_LAST) * HD ** (-0.5) + bias
    expd = jnp.exp(scores - jnp.max(scores, 0, keepdims=True))
    probs = (expd / jnp.sum(expd, 0, keepdims=True)).astype(jnp.bfloat16)
    return mxu(probs, value_rows, CONTRACT_ROWS)


def head_backward(query, key_rows, value_rows, bias, d_mixed):
    scores = mxu(key_rows, query, CONTRACT_LAST) * HD ** (-0.5) + bias
    expd = jnp.exp(scores - jnp.max(scores, 0, keepdims=True))
    probs = expd / jnp.sum(expd, 0, keepdims=True)
    d_value = mxu(probs.astype(jnp.bfloat16), d_mixed)
    d_probs = mxu(value_rows, d_mixed, CONTRACT_LAST)
    offset = jnp.sum(d_probs * probs, 0, keepdims=True)
    d_scores = (probs * (d_probs - offset) * HD ** (-0.5)).astype(jnp.bfloat16)
    d_query = mxu(d_scores, key_rows, CONTRACT_ROWS)
    d_key = mxu(d_scores, query)
    return d_query, d_key, d_value


def self_forward_kernel(tiles, tick, x, mods, bias, panel, mask, out, branch, source, proj, mixed, total):
    step = pl.program_id(0)
    rows = PM // tiles
    tick(0)

    @pl.when(step == 0)
    def first():
        normed, unused = normal_parts(x[...])
        source[...] = (normed * (1.0 + mods[1:2]) + mods[0:1]).astype(jnp.bfloat16)
        total[...] = jnp.zeros_like(total)

    values = mxu(source[...], panel[0, :, :896]) + bias[0]
    values = values.astype(jnp.bfloat16)
    proj[0] = values
    heads = []
    for h in range(4):
        tops = []
        for t in range(tiles):
            part = values[t * rows : (t + 1) * rows]
            at = h * HD
            tops.append(
                head_forward(
                    part[:, at : at + HD],
                    part[:, SPAN + at : SPAN + at + HD],
                    part[:, 2 * SPAN + at : 2 * SPAN + at + HD],
                    mask[...],
                )
            )
        heads.append(jnp.concatenate(tops, 0) if tiles > 1 else tops[0])
        tick(h + 1)
    packed = padded_heads(heads, 96, 0).astype(jnp.bfloat16)
    mixed[0] = packed
    total[...] += mxu(packed, panel[0, :, 768:], CONTRACT_LAST)

    @pl.when(step == 3)
    def last():
        value = total[...] + mods[6:7]
        branch[...] = value
        out[...] = x[...] + mods[2:3] * value

    tick(5)


def whole(shape):
    return pl.BlockSpec(shape, lambda i: (0,) * len(shape))


def slab(shape):
    return pl.BlockSpec((1,) + shape, lambda i: (i,) + (0,) * len(shape))


def grid_params(ident=None):
    if ident is None:
        return pltpu.CompilerParams(vmem_limit_bytes=BIG)
    return pltpu.CompilerParams(vmem_limit_bytes=BIG, collective_id=ident, has_side_effects=True)


def with_gather(kernel, spots, inputs, outputs):
    def run(*refs):
        ins, shard = refs[:inputs], refs[inputs]
        outs, full = refs[inputs + 1 : inputs + 1 + outputs], refs[inputs + 1 + outputs]
        scratch, sems = refs[inputs + outputs + 2 : -3], refs[-3:]
        kernel(gather_ticks((shard, full) + sems, spots), *ins, *outs, *scratch)

    return run


def call_with(kernel, spots, operands, in_specs, out_specs, out_shape, scratch, shard, ident):
    if shard is None:
        return pl.pallas_call(
            functools.partial(kernel, no_ticks),
            grid=(4,),
            in_specs=in_specs,
            out_specs=out_specs,
            out_shape=out_shape,
            scratch_shapes=scratch,
            compiler_params=grid_params(),
        )(*operands)
    remote = pl.BlockSpec(memory_space=pl.ANY)
    full = jax.ShapeDtypeStruct((shard.shape[0], 4, 8) + shard.shape[1:], shard.dtype)
    return pl.pallas_call(
        with_gather(kernel, spots, len(in_specs), len(out_specs)),
        grid=(4,),
        in_specs=in_specs + [remote],
        out_specs=out_specs + [remote],
        out_shape=out_shape + [full],
        scratch_shapes=scratch + GATHER_SEMS,
        compiler_params=grid_params(ident),
    )(*operands, shard)


def self_forward(x, mods, bias, panels, mask, tiles, shard=None, ident=None):
    f32, bf16 = jnp.float32, jnp.bfloat16
    rows = PM // tiles
    return call_with(
        functools.partial(self_forward_kernel, tiles),
        6,
        (x, mods, bias, panels, mask),
        [whole((PM, D)), whole((8, D)), slab((1, 896)), slab((D, D)), whole((rows, rows))],
        [whole((PM, D)), whole((PM, D)), whole((PM, D)), slab((PM, 896)), slab((PM, 384))],
        [
            jax.ShapeDtypeStruct((PM, D), f32),
            jax.ShapeDtypeStruct((PM, D), f32),
            jax.ShapeDtypeStruct((PM, D), bf16),
            jax.ShapeDtypeStruct((4, PM, 896), bf16),
            jax.ShapeDtypeStruct((4, PM, 384), bf16),
        ],
        [pltpu.VMEM((PM, D), f32)],
        shard,
        ident,
    )


def self_backward_kernel(
    tiles, x, grad, mods, branch, source, proj, mixed, panel, mask, out, sums, d_bias, d_panel, d_branch, total
):
    step = pl.program_id(0)
    rows = PM // tiles

    @pl.when(step == 0)
    def first():
        value = grad[...]
        low = (mods[2:3] * value).astype(jnp.bfloat16)
        d_branch[...] = low
        sums[2:3] = jnp.sum(value * branch[...], 0, keepdims=True)
        sums[3:4] = jnp.sum(low.astype(jnp.float32), 0, keepdims=True)
        total[...] = jnp.zeros_like(total)

    low = d_branch[...]
    d_mixed = mxu(low, panel[0, :, 768:]).astype(jnp.bfloat16)
    values = proj[0]
    d_query, d_key, d_value = [], [], []
    for h in range(4):
        at = h * HD
        tops = []
        for t in range(tiles):
            part = values[t * rows : (t + 1) * rows]
            tops.append(
                head_backward(
                    part[:, at : at + HD],
                    part[:, SPAN + at : SPAN + at + HD],
                    part[:, 2 * SPAN + at : 2 * SPAN + at + HD],
                    mask[...],
                    d_mixed[t * rows : (t + 1) * rows, 96 + at : 96 + at + HD],
                )
            )
        for store, index in ((d_query, 0), (d_key, 1), (d_value, 2)):
            pieces = [top[index] for top in tops]
            store.append(jnp.concatenate(pieces, 0) if tiles > 1 else pieces[0])
    d_proj = padded_heads(d_query + d_key + d_value, 0, 32).astype(jnp.bfloat16)
    d_bias[0] = jnp.sum(d_proj.astype(jnp.float32), 0, keepdims=True)
    columns = lax.broadcasted_iota(jnp.int32, (1, 896), 1)
    kept = jnp.where(columns < 3 * SPAN, panel[0, :, :896], jnp.zeros((), jnp.bfloat16))
    total[...] += mxu(d_proj, kept, CONTRACT_LAST)
    src = source[...]
    d_panel[0, :, :768] = mxu(src, d_proj[:, :768], CONTRACT_ROWS).astype(jnp.bfloat16)
    packed = mixed[0]
    d_panel[0, :, 768:896] = (
        mxu(src, d_proj[:, 768:], CONTRACT_ROWS) + mxu(low, packed[:, :128], CONTRACT_ROWS)
    ).astype(jnp.bfloat16)
    d_panel[0, :, 896:] = mxu(low, packed[:, 128:], CONTRACT_ROWS).astype(jnp.bfloat16)

    @pl.when(step == 3)
    def last():
        d_x, d_shift, d_scale = normal_back(x[...], mods[1:2], total[...])
        sums[0:1] = d_shift
        sums[1:2] = d_scale
        out[...] = grad[...] + d_x


def self_backward(x, grad, mods, branch, source, proj, mixed, panels, mask, tiles):
    f32, bf16 = jnp.float32, jnp.bfloat16
    rows = PM // tiles
    return pl.pallas_call(
        functools.partial(self_backward_kernel, tiles),
        grid=(4,),
        in_specs=[
            whole((PM, D)),
            whole((PM, D)),
            whole((8, D)),
            whole((PM, D)),
            whole((PM, D)),
            slab((PM, 896)),
            slab((PM, 384)),
            slab((D, D)),
            whole((rows, rows)),
        ],
        out_specs=[whole((PM, D)), whole((8, D)), slab((1, 896)), slab((D, D))],
        out_shape=[
            jax.ShapeDtypeStruct((PM, D), f32),
            jax.ShapeDtypeStruct((8, D), f32),
            jax.ShapeDtypeStruct((4, 1, 896), f32),
            jax.ShapeDtypeStruct((4, D, D), bf16),
        ],
        scratch_shapes=[pltpu.VMEM((PM, D), bf16), pltpu.VMEM((PM, D), f32)],
        compiler_params=grid_params(),
    )(x, grad, mods, branch, source, proj, mixed, panels, mask)


def cross_forward_kernel(tick, x, mods, bias, context, panel, mask, out, proj, pair, mixed, total):
    step = pl.program_id(0)
    tick(0)

    @pl.when(step == 0)
    def first():
        total[...] = jnp.zeros_like(total)

    query = (mxu(x[...].astype(jnp.bfloat16), panel[0, :, :384]) + bias[0, :, :384]).astype(jnp.bfloat16)
    both = (mxu(context[...], panel[0, :, 256:896]) + bias[0, :, 256:896]).astype(jnp.bfloat16)
    proj[0] = query
    pair[0] = both
    heads = []
    for h in range(4):
        at = h * HD
        heads.append(
            head_forward(
                query[:, at : at + HD],
                both[:, 32 + at : 32 + at + HD],
                both[:, 32 + SPAN + at : 32 + SPAN + at + HD],
                mask[...],
            )
        )
        tick(h + 1)
    packed = padded_heads(heads, 96, 0).astype(jnp.bfloat16)
    mixed[0] = packed
    total[...] += mxu(packed, panel[0, :, 768:], CONTRACT_LAST)

    @pl.when(step == 3)
    def last():
        out[...] = x[...] + total[...] + mods[6:7]

    tick(5)


def cross_forward(x, mods, bias, context, panels, mask, shard=None, ident=None):
    f32, bf16 = jnp.float32, jnp.bfloat16
    return call_with(
        cross_forward_kernel,
        6,
        (x, mods, bias, context, panels, mask),
        [
            whole((PM, D)),
            whole((8, D)),
            slab((1, 896)),
            whole((128, D)),
            slab((D, D)),
            whole((128, 1)),
        ],
        [whole((PM, D)), slab((PM, 384)), slab((128, 640)), slab((PM, 384))],
        [
            jax.ShapeDtypeStruct((PM, D), f32),
            jax.ShapeDtypeStruct((4, PM, 384), bf16),
            jax.ShapeDtypeStruct((4, 128, 640), bf16),
            jax.ShapeDtypeStruct((4, PM, 384), bf16),
        ],
        [pltpu.VMEM((PM, D), f32)],
        shard,
        ident,
    )


def cross_backward_kernel(
    x, grad, context, proj, pair, mixed, panel, mask, out, d_context, sums, d_bias, d_panel, total
):
    step = pl.program_id(0)

    @pl.when(step == 0)
    def first():
        low = grad[...].astype(jnp.bfloat16)
        sums[0:1] = jnp.sum(low.astype(jnp.float32), 0, keepdims=True)
        total[...] = jnp.zeros_like(total)
        d_context[...] = jnp.zeros_like(d_context)

    low = grad[...].astype(jnp.bfloat16)
    d_mixed = mxu(low, panel[0, :, 768:]).astype(jnp.bfloat16)
    query, both = proj[0], pair[0]
    d_query, d_key, d_value = [], [], []
    for h in range(4):
        at = h * HD
        one = head_backward(
            query[:, at : at + HD],
            both[:, 32 + at : 32 + at + HD],
            both[:, 32 + SPAN + at : 32 + SPAN + at + HD],
            mask[...],
            d_mixed[:, 96 + at : 96 + at + HD],
        )
        d_query.append(one[0])
        d_key.append(one[1])
        d_value.append(one[2])
    d_ask = padded_heads(d_query, 0, 96).astype(jnp.bfloat16)
    d_both = padded_heads(d_key + d_value, 32, 32).astype(jnp.bfloat16)
    sum_both = jnp.sum(d_both.astype(jnp.float32), 0, keepdims=True)
    d_bias[0, :, :384] = jnp.sum(d_ask.astype(jnp.float32), 0, keepdims=True)
    d_bias[0, :, 384:] = sum_both
    total[...] += mxu(d_ask, panel[0, :, :384], CONTRACT_LAST)
    d_context[...] += mxu(d_both, panel[0, :, 256:896], CONTRACT_LAST)
    src, ctx, packed = x[...].astype(jnp.bfloat16), context[...], mixed[0]
    d_panel[0, :, :256] = mxu(src, d_ask[:, :256], CONTRACT_ROWS).astype(jnp.bfloat16)
    d_panel[0, :, 256:384] = (
        mxu(src, d_ask[:, 256:], CONTRACT_ROWS) + mxu(ctx, d_both[:, :128], CONTRACT_ROWS)
    ).astype(jnp.bfloat16)
    d_panel[0, :, 384:768] = mxu(ctx, d_both[:, 128:512], CONTRACT_ROWS).astype(jnp.bfloat16)
    d_panel[0, :, 768:896] = (
        mxu(ctx, d_both[:, 512:], CONTRACT_ROWS) + mxu(low, packed[:, :128], CONTRACT_ROWS)
    ).astype(jnp.bfloat16)
    d_panel[0, :, 896:] = mxu(low, packed[:, 128:], CONTRACT_ROWS).astype(jnp.bfloat16)

    @pl.when(step == 3)
    def last():
        out[...] = grad[...] + total[...]


def cross_backward(x, grad, context, proj, pair, mixed, panels, mask):
    f32, bf16 = jnp.float32, jnp.bfloat16
    return pl.pallas_call(
        cross_backward_kernel,
        grid=(4,),
        in_specs=[
            whole((PM, D)),
            whole((PM, D)),
            whole((128, D)),
            slab((PM, 384)),
            slab((128, 640)),
            slab((PM, 384)),
            slab((D, D)),
            whole((128, 1)),
        ],
        out_specs=[whole((PM, D)), whole((128, D)), whole((8, D)), slab((1, 1024)), slab((D, D))],
        out_shape=[
            jax.ShapeDtypeStruct((PM, D), f32),
            jax.ShapeDtypeStruct((128, D), f32),
            jax.ShapeDtypeStruct((8, D), f32),
            jax.ShapeDtypeStruct((4, 1, 1024), f32),
            jax.ShapeDtypeStruct((4, D, D), bf16),
        ],
        scratch_shapes=[pltpu.VMEM((PM, D), f32)],
        compiler_params=grid_params(),
    )(x, grad, context, proj, pair, mixed, panels, mask)


GELU_A = math.sqrt(2.0 / math.pi)
GELU_B = 0.044715


def ffn_forward_kernel(tick, x, mods, bias, w_in, w_out, out, branch, source, pre, total):
    step = pl.program_id(0)
    tick(0)

    @pl.when(step == 0)
    def first():
        normed, unused = normal_parts(x[...])
        source[...] = (normed * (1.0 + mods[4:5]) + mods[3:4]).astype(jnp.bfloat16)
        total[...] = jnp.zeros_like(total)

    value = mxu(source[...], w_in[0, 0]) + bias[0]
    pre[0] = value
    tick(1)
    hidden = 0.5 * value * (1.0 + jnp.tanh(GELU_A * (value + GELU_B * value * value * value)))
    tick(2)
    total[...] += mxu(hidden.astype(jnp.bfloat16), w_out[0, 0], CONTRACT_LAST)

    @pl.when(step == 3)
    def last():
        result = total[...] + mods[6:7]
        branch[...] = result
        out[...] = x[...] + mods[5:6] * result

    tick(3)


def half(index):
    return pl.BlockSpec((1, 1, D, D), lambda i: (index, i, 0, 0))


def ffn_forward_chip(x, mods, bias, panels, shard=None, ident=None):
    f32, bf16 = jnp.float32, jnp.bfloat16
    return call_with(
        ffn_forward_kernel,
        4,
        (x, mods, bias, panels, panels),
        [whole((PM, D)), whole((8, D)), slab((1, D)), half(0), half(1)],
        [whole((PM, D)), whole((PM, D)), whole((PM, D)), slab((PM, D))],
        [
            jax.ShapeDtypeStruct((PM, D), f32),
            jax.ShapeDtypeStruct((PM, D), f32),
            jax.ShapeDtypeStruct((PM, D), bf16),
            jax.ShapeDtypeStruct((4, PM, D), f32),
        ],
        [pltpu.VMEM((PM, D), f32)],
        shard,
        ident,
    )


def ffn_backward_kernel(
    x, grad, mods, branch, source, pre, w_in, w_out, out, sums, d_bias, d_panel, d_branch, total
):
    step = pl.program_id(0)

    @pl.when(step == 0)
    def first():
        value = grad[...]
        low = (mods[5:6] * value).astype(jnp.bfloat16)
        d_branch[...] = low
        sums[2:3] = jnp.sum(value * branch[...], 0, keepdims=True)
        sums[3:4] = jnp.sum(low.astype(jnp.float32), 0, keepdims=True)
        total[...] = jnp.zeros_like(total)

    low = d_branch[...]
    value = pre[0]
    square = value * value
    bent = jnp.tanh(GELU_A * (value + GELU_B * value * square))
    slope = 0.5 * (1.0 + bent) + 0.5 * value * (1.0 - bent * bent) * GELU_A * (
        1.0 + 3.0 * GELU_B * square
    )
    hidden = (0.5 * value * (1.0 + bent)).astype(jnp.bfloat16)
    d_pre = (mxu(low, w_out[0, 0]) * slope).astype(jnp.bfloat16)
    d_bias[0] = jnp.sum(d_pre.astype(jnp.float32), 0, keepdims=True)
    total[...] += mxu(d_pre, w_in[0, 0], CONTRACT_LAST)
    d_panel[0, 0] = mxu(source[...], d_pre, CONTRACT_ROWS).astype(jnp.bfloat16)
    d_panel[1, 0] = mxu(low, hidden, CONTRACT_ROWS).astype(jnp.bfloat16)

    @pl.when(step == 3)
    def last():
        d_x, d_shift, d_scale = normal_back(x[...], mods[4:5], total[...])
        sums[0:1] = d_shift
        sums[1:2] = d_scale
        out[...] = grad[...] + d_x


def ffn_backward_chip(x, grad, mods, branch, source, pre, panels):
    f32, bf16 = jnp.float32, jnp.bfloat16
    return pl.pallas_call(
        ffn_backward_kernel,
        grid=(4,),
        in_specs=[
            whole((PM, D)),
            whole((PM, D)),
            whole((8, D)),
            whole((PM, D)),
            whole((PM, D)),
            slab((PM, D)),
            half(0),
            half(1),
        ],
        out_specs=[
            whole((PM, D)),
            whole((8, D)),
            slab((1, D)),
            pl.BlockSpec((2, 1, D, D), lambda i: (0, i, 0, 0)),
        ],
        out_shape=[
            jax.ShapeDtypeStruct((PM, D), f32),
            jax.ShapeDtypeStruct((8, D), f32),
            jax.ShapeDtypeStruct((4, 1, D), f32),
            jax.ShapeDtypeStruct((2, 4, D, D), bf16),
        ],
        scratch_shapes=[pltpu.VMEM((PM, D), bf16), pltpu.VMEM((PM, D), f32)],
        compiler_params=grid_params(),
    )(x, grad, mods, branch, source, pre, panels, panels)


def modulate_back(x, shift_vec, scale_vec, grad):
    unused, pull = jax.vjp(modulate, x, shift_vec, scale_vec)
    return pull(grad)


def padded_rows(value):
    return jnp.pad(value, ((0, 128 - value.shape[0]), (0, 0)))


def local_rows(full, group):
    return lax.dynamic_slice_in_dim(full, group * EMB_LOCAL, EMB_LOCAL, 1)


def per_device_chips(
    latents,
    noise,
    caption,
    caption_lens,
    timesteps,
    grid_hw,
    frame_counts,
    attn_mats,
    ffn_mats,
    embed_mats,
    vectors,
    attn_first,
    ffn_first,
    embed_first,
    vector_first,
    attn_second,
    ffn_second,
    embed_second,
    vector_second,
    attn_ema,
    ffn_ema,
    embed_ema,
    vector_ema,
):
    group = lax.axis_index(DP)
    part = lax.axis_index(MP)
    clips = timesteps.shape[0]
    parts = unpack(vectors)
    bf16 = jnp.bfloat16
    f32 = jnp.float32

    attn_low = attn_mats.astype(bf16).reshape(3, BLOCK, 4, 4, HD).swapaxes(2, 3).reshape(3, BLOCK, D)
    ffn_low = ffn_mats.astype(bf16)

    def panels(full):
        full = full.reshape(full.shape[:2] + (D, D))
        return full if full.shape[0] > 1 else full[0]

    w_space = panels(gather_all([attn_low[0:1]], 0)[0])

    pick = jnp.arange(clips, dtype=jnp.int32) == group

    def select(values):
        return jnp.sum(jnp.where(pick, values, 0))

    tstep = select(timesteps)
    cap_len = select(caption_lens)
    height = select(grid_hw[:, 0])
    width_grid = select(grid_hw[:, 1])
    frames = select(frame_counts)
    count = jnp.sum(frame_counts * grid_hw[:, 0] * grid_hw[:, 1]).astype(f32)
    betas, cumul = roster()
    step_ids = jnp.arange(1000, dtype=jnp.int32)
    alpha_bar = jnp.sum(jnp.where(step_ids == tstep, cumul, 0.0))
    alpha_prev = jnp.sum(jnp.where(step_ids == tstep - 1, cumul, 0.0))
    beta_now = jnp.sum(jnp.where(step_ids == tstep, betas, 0.0))

    embed_low = embed_mats.astype(bf16)
    width_local = embed_low.shape[1]
    captions = lax.all_gather(caption[0], DP, axis=0, tiled=True)
    lead = TFREQ + TXT
    cap_rows = local_rows(jnp.pad(captions, ((0, 0), (TFREQ, EMB_ALL - lead))), group)
    freq = waves(timesteps.astype(f32), TFREQ).astype(bf16)
    freq_rows = local_rows(jnp.pad(freq, ((0, 0), (0, EMB_ALL - TFREQ))), group)

    def from_rows(local):
        return part_sum(local, 1).swapaxes(0, 1).reshape(clips, EMB_ALL)

    def over_clips(value):
        return jnp.sum(share(value, DP, 2), 0)

    t_pre = over_clips(jnp.dot(freq_rows, embed_low, preferred_element_type=f32))
    t_pre = t_pre + own_slice(parts[T_BIAS_ONE], part, width_local)
    t_hidden = jax.nn.silu(t_pre).astype(bf16)
    t_sum = from_rows(lax.dot_general(t_hidden, embed_low, CONTRACT_LAST, preferred_element_type=f32))
    t_emb_all = t_sum[:, lead : lead + D] + parts[T_BIAS_TWO]
    t_emb_local = lax.dynamic_slice_in_dim(t_emb_all, part * width_local, width_local, 1)
    silu_local = jax.nn.silu(t_emb_local).astype(bf16)
    mod_sum = from_rows(
        lax.dot_general(silu_local, embed_low, CONTRACT_LAST, preferred_element_type=f32)
    )[:, lead + 2 * D :]
    t_mod_vec = jnp.sum(jnp.where(pick[:, None], mod_sum, 0.0), 0) + parts[T_BIAS_MOD]
    t_emb = jnp.sum(jnp.where(pick[:, None], t_emb_all, 0.0), 0)

    c_two_row = lead + D - group * EMB_LOCAL
    c_row_ids = c_two_row + jnp.arange(D, dtype=jnp.int32)
    c_held = (c_two_row >= 0) & (c_two_row + D <= EMB_LOCAL)
    c_two = lax.dynamic_slice_in_dim(embed_low, jnp.clip(c_two_row, 0, EMB_LOCAL - D), D, 0)
    c_two = lax.psum(jnp.where(c_held, c_two, jnp.zeros_like(c_two)), DP)
    c_product = jnp.dot(cap_rows, embed_low, preferred_element_type=f32)
    c_pre = jnp.sum(deal(c_product.reshape(clips, CAP, width_local), 3), 0)
    c_pre = c_pre + own_slice(parts[C_BIAS_ONE], part, width_local)
    c_hidden = gelu_tanh(c_pre).astype(bf16)
    c_part = lax.dot_general(c_hidden, c_two, CONTRACT_LAST, preferred_element_type=f32)

    def over_parts(value):
        return jnp.sum(share(padded_rows(value.astype(bf16)), MP, 4).astype(f32), 0)

    context = padded_rows((over_parts(c_part)[:CAP] + parts[C_BIAS_TWO]).astype(bf16))

    area = height * width_grid
    patch_ids = jnp.arange(PM, dtype=jnp.int32)
    shifted = patch_ids - (PM - area)
    noisy = jnp.sqrt(alpha_bar) * latents[0] + jnp.sqrt(1.0 - alpha_bar) * noise[0]
    noisy_low = noisy.astype(bf16)
    position = jnp.concatenate(
        [
            waves((shifted // width_grid).astype(f32), D // 2),
            waves((shifted % width_grid).astype(f32), D // 2),
        ],
        -1,
    )
    x = jnp.dot(noisy_low, parts[PATCH_W].astype(bf16), preferred_element_type=f32)
    x = x + parts[PATCH_B] + position
    tables = parts[TABLES] + t_mod_vec.reshape(1, 6, D)
    mods0, mods1 = tables[0], tables[1]
    mask_space = jnp.where(patch_ids >= PM - area, 0.0, NEG_LARGE)[:, None]
    mask_space = jnp.broadcast_to(mask_space, (PM, PM))
    mask_cross = jnp.where(jnp.arange(128, dtype=jnp.int32) < cap_len, 0.0, NEG_LARGE)[:, None]
    half_ids = jnp.arange(PM // 2, dtype=jnp.int32)
    frame_ids, place_ids = half_ids // (PM // 8), half_ids % (PM // 8)
    mask_time = jnp.where(
        (place_ids[:, None] == place_ids[None]) & (frame_ids[:, None] >= FR - frames), 0.0, NEG_LARGE
    )
    biases = parts[ATTN_BIAS]

    def side(values):
        blank = jnp.zeros((4, SPAN), f32)
        rows = [values[0].reshape(4, SPAN), blank, values[1].reshape(4, SPAN), blank[:, :32]]
        return jnp.concatenate(rows, 1)[:, None]

    def vectors_of(mods, out_bias):
        return jnp.concatenate([mods, out_bias[None], jnp.zeros((1, D), f32)])

    x0 = x
    m_space, m_ffn0 = vectors_of(mods0, biases[0, 2]), vectors_of(mods0, parts[FFN_BIAS_TWO][0])
    x1, branch0, source0, proj0, mixed0, full = self_forward(
        x0, m_space, side(biases[0]), w_space, mask_space, 1, attn_low[2:3], 5
    )
    w_cross = panels(full)
    m_cross = vectors_of(mods0, biases[2, 2])
    x2, cross_q, cross_kv, mixed1, full = cross_forward(
        x1, m_cross, side(biases[2]), context, w_cross, mask_cross, ffn_low[0], 6
    )
    w_ffn0 = panels(full)
    bias_ffn = parts[FFN_BIAS_ONE].reshape(2, 4, 1, D)
    x3, branch2, source2, pre2, full = ffn_forward_chip(
        x2, m_ffn0, bias_ffn[0], w_ffn0, attn_low[1:2], 7
    )
    w_time = panels(full)
    x3 = x3 + waves((part - (FR - frames)).astype(f32)[None], D)

    share_rows = PM // FR
    pixels = jnp.concatenate([latents[0], noise[0]], 1).reshape(FR, share_rows, -1)
    pixels = lax.all_to_all(pixels, MP, 0, 0, tiled=True).reshape(FR, 2, PM // 8, -1)
    pixels = pixels.swapaxes(0, 1).reshape(PM, -1)
    latent_time, noise_time = pixels[:, :CIN], pixels[:, CIN:]
    x4 = to_time(x3, 8)
    m_time, m_ffn1 = vectors_of(mods1, biases[1, 2]), vectors_of(mods1, parts[FFN_BIAS_TWO][1])
    x5, branch4, source4, proj4, mixed4, full = self_forward(
        x4, m_time, side(biases[1]), w_time, mask_time, 2, ffn_low[1], 9
    )
    w_ffn1 = panels(full)
    x6, branch5, source5, pre5 = ffn_forward_chip(x5, m_ffn1, bias_ffn[1], w_ffn1)

    final_mods = parts[FINAL_TABLE] + t_emb
    final_source = modulate(x6, final_mods[0], final_mods[1]).astype(bf16)
    final_low = parts[FINAL_W].astype(bf16)
    output = (
        lax.dot_general(final_source, final_low, CONTRACT_LAST, preferred_element_type=f32)
        + parts[FINAL_B]
    )
    frozen = output[:, :CIN]
    noisy_time = jnp.sqrt(alpha_bar) * latent_time + jnp.sqrt(1.0 - alpha_bar) * noise_time
    row_ids = jnp.arange(PM, dtype=jnp.int32)
    row_frames = (row_ids % (PM // 2)) // (PM // 8)
    row_patches = part * share_rows + (row_ids // (PM // 2)) * (PM // 8) + row_ids % (PM // 8)
    valid = (row_frames >= FR - frames) & (row_patches >= PM - area)

    def shard_loss(values):
        losses = token_losses(
            values, frozen, latent_time, noise_time, (noisy_time, alpha_bar, alpha_prev, beta_now)
        )
        return jnp.sum(jnp.where(valid, losses, 0.0))

    loss_part, loss_pull = jax.vjp(shard_loss, output)
    d_output = loss_pull(1.0 / count)[0].astype(bf16)
    d_final_w = lax.dot_general(d_output, final_source, CONTRACT_ROWS, preferred_element_type=f32)
    d_final_b = jnp.sum(d_output.astype(f32), 0)
    d_final_source = jnp.dot(d_output, final_low, preferred_element_type=f32)
    grad_x, d_final_shift, d_final_scale = modulate_back(
        x6, final_mods[0], final_mods[1], d_final_source
    )

    def blocks(grads):
        return grads.reshape((-1, 4, 8, BLOCK, D))

    grad_x, sums5, bias5, d_ffn1 = ffn_backward_chip(
        x5, grad_x, m_ffn1, branch5, source5, pre5, w_ffn1
    )
    g_ffn1 = scatter_one(blocks(d_ffn1), 10)
    grad_x, sums4, bias4, d_time = self_backward(
        x4, grad_x, m_time, branch4, source4, proj4, mixed4, w_time, mask_time, 2
    )
    g_time = scatter_one(blocks(d_time), 11)
    d_mods1 = jnp.concatenate([sums4[:3], sums5[:3]])
    grad_x = to_space(grad_x, 12)

    grad_x, sums2, bias2, d_ffn0 = ffn_backward_chip(
        x2, grad_x, m_ffn0, branch2, source2, pre2, w_ffn0
    )
    g_ffn0 = scatter_one(blocks(d_ffn0), 10)
    grad_x, d_context, sums1, bias1, d_cross = cross_backward(
        x1, grad_x, context, cross_q, cross_kv, mixed1, w_cross, mask_cross
    )
    g_cross = scatter_one(blocks(d_cross), 11)

    first_part = (part == 0).astype(f32)
    d_context = over_parts(d_context)[:CAP].astype(bf16)
    d_c_bias_two = jnp.sum(d_context.astype(f32), 0) * first_part
    d_c_hidden = jnp.dot(d_context, c_two, preferred_element_type=f32)
    unused, cap_pull = jax.vjp(gelu_tanh, c_pre)
    d_c_pre = cap_pull(d_c_hidden)[0].astype(bf16)
    d_c_bias_one = jnp.sum(d_c_pre.astype(f32), 0)
    caption_all = lax.all_gather(
        jnp.concatenate([d_context, c_hidden, d_c_pre], 1), DP, axis=0, tiled=True
    )
    d_context_all = caption_all[:, :D]
    c_hidden_all = caption_all[:, D : D + width_local]
    d_c_pre_all = caption_all[:, D + width_local :]
    d_c_one = lax.dot_general(cap_rows, d_c_pre_all, CONTRACT_ROWS, preferred_element_type=f32)
    d_c_two = lax.dot_general(d_context_all, c_hidden_all, CONTRACT_ROWS, preferred_element_type=f32)

    grad_x, sums0, bias0, d_space = self_backward(
        x0, grad_x, m_space, branch0, source0, proj0, mixed0, w_space, mask_space, 1
    )
    g_space = scatter_one(blocks(d_space), 11)
    d_mods0 = jnp.concatenate([sums0[:3], sums2[:3]])

    def side_sums(values, at_query, at_value, out_bias):
        rows = [values[:, 0, at : at + SPAN].reshape(-1) for at in (at_query, at_value)]
        return jnp.stack(rows + [out_bias])

    d_patch = grad_x.astype(bf16)
    d_patch_b = jnp.sum(d_patch.astype(f32), 0)
    d_patch_w = lax.dot_general(noisy_low, d_patch, CONTRACT_ROWS, preferred_element_type=f32)

    d_mod_part = (d_mods0 + d_mods1).reshape(-1)
    d_temb_part = d_final_shift + d_final_scale
    d_mod_all = part_sum(jnp.concatenate([d_mod_part, d_temb_part]).reshape(8, 7 * D // 8), 13)
    d_mod_all = d_mod_all.reshape(clips, 7 * D)
    d_temb_sum = d_mod_all[:, 6 * D :]
    d_mod_low = d_mod_all[:, : 6 * D].astype(bf16)
    d_mod_rows = local_rows(jnp.pad(d_mod_low, ((0, 0), (lead + 2 * D, 0))), group)
    d_silu = over_clips(jnp.dot(d_mod_rows, embed_low, preferred_element_type=f32))
    unused, silu_pull = jax.vjp(jax.nn.silu, t_emb_local)
    d_temb_local = silu_pull(d_silu)[0]
    d_temb = share(d_temb_local, MP, 14).swapaxes(0, 1).reshape(clips, D) + d_temb_sum
    d_temb_rows = local_rows(jnp.pad(d_temb, ((0, 0), (lead, EMB_ALL - lead - D))), group)
    d_t_hidden = over_clips(
        jnp.dot(d_temb_rows, embed_low.astype(f32), precision=lax.Precision.HIGHEST)
    )
    unused, pre_pull = jax.vjp(jax.nn.silu, t_pre)
    d_t_pre = pre_pull(d_t_hidden)[0]

    def outer(left, right):
        return lax.dot_general(
            left.astype(f32), right.astype(f32), CONTRACT_ROWS, precision=lax.Precision.HIGHEST
        )

    g_embed = (
        lax.dot_general(d_mod_rows, silu_local, CONTRACT_ROWS, preferred_element_type=f32)
        + outer(jnp.concatenate([d_temb_rows, freq_rows.astype(f32)]), jnp.concatenate([t_hidden.astype(f32), d_t_pre]))
        + d_c_one
    )
    here = lax.dynamic_slice_in_dim(g_embed, jnp.clip(c_two_row, 0, EMB_LOCAL - D), D, 0)
    g_embed = lax.dynamic_update_slice_in_dim(
        g_embed, jnp.where(c_held, d_c_two, here), jnp.clip(c_two_row, 0, EMB_LOCAL - D), 0
    )

    first_clip = pick.astype(f32) * first_part
    vector_grads = {
        PATCH_W: d_patch_w,
        PATCH_B: d_patch_b,
        FINAL_W: d_final_w,
        FINAL_B: d_final_b,
        T_BIAS_ONE: placed(jnp.sum(d_t_pre * pick.astype(f32)[:, None], 0), part, D),
        T_BIAS_TWO: d_temb_part
        + placed(jnp.sum(d_temb_local * pick.astype(f32)[:, None], 0), part, D),
        T_BIAS_MOD: d_mod_part,
        C_BIAS_ONE: placed(d_c_bias_one, part, D),
        C_BIAS_TWO: d_c_bias_two,
        ATTN_BIAS: jnp.stack(
            [
                side_sums(bias0, 0, 2 * SPAN, sums0[3]),
                side_sums(bias4, 0, 2 * SPAN, sums4[3]),
                side_sums(bias1, 0, 416 + SPAN, sums1[0]),
            ]
        ),
        FFN_BIAS_ONE: jnp.stack([bias2, bias5]),
        FFN_BIAS_TWO: jnp.stack([sums2[3], sums5[3]]),
        TABLES: jnp.stack([d_mods0, d_mods1]),
        FINAL_TABLE: jnp.stack([d_final_shift, d_final_scale]),
    }
    vector_grad = jnp.concatenate(
        [vector_grads[label].reshape(-1) for label, extent in vector_parts()]
    )
    g_attn = jnp.stack([g_space[0], g_time[0], g_cross[0]])
    g_attn = g_attn.reshape(3, BLOCK, 4, 4, HD).swapaxes(2, 3).reshape(3, BLOCK, D)
    g_ffn = jnp.stack([g_ffn0, g_ffn1])
    matrix_squares = jnp.sum(g_attn * g_attn) + jnp.sum(g_ffn * g_ffn) + jnp.sum(g_embed * g_embed)
    length = vector_grad.shape[0]
    spare = -(length + 2) % (8 * 8 * 128)
    totals = jnp.concatenate([vector_grad, matrix_squares[None], loss_part[None], jnp.zeros((spare,), f32)])
    totals = whole_sum(totals.reshape(8, -1, 128), 15).reshape(-1)
    g_vector = totals[:length]
    loss_total = totals[length + 1]
    squares = totals[length] + jnp.sum(g_vector * g_vector)
    grad_norm = jnp.sqrt(squares)
    factor = CLIP_NORM / (grad_norm + 1e-06)
    new_attn = adam_update(
        attn_mats, attn_first, attn_second, attn_ema, g_attn * factor, LEARN_RATE
    )
    new_ffn = adam_update(ffn_mats, ffn_first, ffn_second, ffn_ema, g_ffn * factor, LEARN_RATE)
    new_embed = adam_update(
        embed_mats, embed_first, embed_second, embed_ema, g_embed * factor, LEARN_RATE
    )
    new_vector = adam_update(
        vectors, vector_first, vector_second, vector_ema, g_vector * factor, VECTOR_RATE
    )
    return (loss_total, count, grad_norm) + tuple(
        group_new[kind]
        for kind in range(4)
        for group_new in (new_attn, new_ffn, new_embed, new_vector)
    )


def solution(mesh):
    fits = dict(mesh.shape) == {DP: CLIPS, MP: FR}
    program = per_device_chips if fits else per_device
    return jax.shard_map(
        program,
        mesh=mesh,
        in_specs=(
            P(DP, MP, None),
            P(DP, MP, None),
            P(DP, None, None),
            P(),
            P(),
            P(),
            P(),
            P(None, DP, MP),
            P(None, None, DP, MP),
            P(DP, MP),
            P(),
            P(None, DP, MP),
            P(None, None, DP, MP),
            P(DP, MP),
            P(),
            P(None, DP, MP),
            P(None, None, DP, MP),
            P(DP, MP),
            P(),
            P(None, DP, MP),
            P(None, None, DP, MP),
            P(DP, MP),
            P(),
        ),
        out_specs=(
            P(),
            P(),
            P(),
            P(None, DP, MP),
            P(None, None, DP, MP),
            P(DP, MP),
            P(),
            P(None, DP, MP),
            P(None, None, DP, MP),
            P(DP, MP),
            P(),
            P(None, DP, MP),
            P(None, None, DP, MP),
            P(DP, MP),
            P(),
            P(None, DP, MP),
            P(None, None, DP, MP),
            P(DP, MP),
            P(),
        ),
        check_vma=False,
    )
```

profile of v0, /device:TPU:24, one launch (start us, length us, event | category | flops | bytes accessed | tf_op | source)
XLA Modules:
  0.0 1576.8 jit_solution(1557130166346941508)
XLA Ops:
  81.7 27.3 %shard_map.367 = f32[8,8,1696]{2,1,0:T(8,128)} custom-call(f32[8,1696]{1,0:T(8,128)} %fusion.81.x), custom_call_target="tpu_custom_call" | custom-call | tf_op jit(solution)/shard_map/pallas_call | solution.py:1122
  112.1 30.5 %shard_map.368 = f32[8,8,1696]{2,1,0:T(8,128)} custom-call(f32[8,1696]{1,0:T(8,128)} %fusion.79.x), custom_call_target="tpu_custom_call" | custom-call | tf_op jit(solution)/shard_map/pallas_call | solution.py:1122
  178.9 62.3 %shard_map.369 = bf16[1,4,8,144,1152]{4,3,2,1,0:T(8,128)(2,1)} custom-call(bf16[1,144,1152]{2,1,0:T(8,128)(2,1)} %slice.316.refs_0_), custom_call_target="tpu_custom_call" | custom-call | tf_op jit(solution)/shard_map/pallas_call | solution.py:895
  242.3 66.7 %shard_map.370 = (f32[448,1152]{1,0:T(8,128)}, f32[448,1152]{1,0:T(8,128)}, bf16[448,1152]{1,0:T(8,128)(2,1)}, bf16[4,448,896]{2,1,0:T(8,128)(2,1)}, bf16[4,448,...) custom-call(f32[448,1152]{1,0:T(8,128)} %fusion.refs_0_.x, f32[8,1152]{1,0:T(8,128)} %get-tuple-element.209.refs_1_.mods, ...), custom_call_target="tpu_custom_call" | custom-call | tf_op jit(solution)/shard_map/pallas_call | solution.py:1366
  313.5 37.1 %shard_map.371 = f32[8,120,288]{2,1,0:T(8,128)} custom-call(f32[8,120,288]{2,1,0:T(8,128)} %bitcast.147), custom_call_target="tpu_custom_call" | custom-call | tf_op jit(solution)/shard_map/pallas_call | solution.py:1122
  355.2 16.8 %shard_map.372 = bf16[4,128,1152]{2,1,0:T(8,128)(2,1)} custom-call(bf16[128,1152]{1,0:T(8,128)(2,1)} %pad.35.x), custom_call_target="tpu_custom_call" | custom-call | tf_op jit(solution)/shard_map/pallas_call | solution.py:1122
  374.3 117.0 %shard_map.373 = (f32[448,1152]{1,0:T(8,128)}, bf16[4,448,384]{2,1,0:T(8,128)(2,1)}, bf16[4,128,640]{2,1,0:T(8,128)(2,1)}, bf16[4,448,384]{2,1,0:T(8,128)(2,1)}, bf16[2,4,8,144,1152]{4,3,2,1,0:T(8,128)(2,1)}) custom-call(f32[448,1152]{1,0:T(8,128)} %get-tuple-element.66.refs_0_.x, f32[8,1152]{1,0:T(8,128)} %get-tuple-element.210.refs_1_, ...), custom_call_target="tpu_custom_call" | custom-call | tf_op jit(solution)/shard_map/pallas_call | solution.py:1366
  491.3 66.4 %shard_map.374 = (f32[448,1152]{1,0:T(8,128)}, f32[448,1152]{1,0:T(8,128)}, bf16[448,1152]{1,0:T(8,128)(2,1)}, f32[4,448,1152]{2,1,0:T(8,128)}, bf16[1,4,8,144,1152]{4,3,2,1,0:T(8,128)(2,1)}) custom-call(f32[448,1152]{1,0:T(8,128)} %get-tuple-element.68.refs_0_.x, f32[8,1152]{1,0:T(8,128)} %get-tuple-element.211.refs_1_.mods, f32[4,1,1152]{2,1,0:T(1,128)} %slice.331.refs_2_, ...), custom_call_target="tpu_custom_call" | custom-call | tf_op jit(solution)/shard_map/pallas_call | solution.py:1366
  560.7 24.2 %shard_map.375 = f32[2,4,56,1152]{3,2,1,0:T(8,128)} custom-call(f32[4,2,56,1152]{3,2,1,0:T(8,128)} %bitcast.136), custom_call_target="tpu_custom_call" | custom-call | tf_op jit(solution)/shard_map/pallas_call | solution.py:1122
  585.0 115.3 %shard_map.376 = (f32[448,1152]{1,0:T(8,128)}, f32[448,1152]{1,0:T(8,128)}, bf16[448,1152]{1,0:T(8,128)(2,1)}, bf16[4,448,896]{2,1,0:T(8,128)(2,1)}, bf16[4,448,...) custom-call(f32[448,1152]{1,0:T(8,128)} %bitcast.125, f32[8,1152]{1,0:T(8,128)} %get-tuple-element.188.refs_1_.mods, ...), custom_call_target="tpu_custom_call" | custom-call | tf_op jit(solution)/shard_map/pallas_call | solution.py:1366
  700.3 20.8 %shard_map.377 = (f32[448,1152]{1,0:T(8,128)}, f32[448,1152]{1,0:T(8,128)}, bf16[448,1152]{1,0:T(8,128)(2,1)}, f32[4,448,1152]{2,1,0:T(8,128)}) custom-call(f32[448,1152]{1,0:T(8,128)} %get-tuple-element.72.x, f32[8,1152]{1,0:T(8,128)} %get-tuple-element.187.mods, f32[4,1,1152]{2,1,0:T(1,128)} %slice.346.bias, bf16[2,4,1152,1152]{3,2,1,0:T(8,128)(2,1)} %bitcast.113, ...), custom_call_target="tpu_custom_call" | custom-call | tf_op jit(solution)/shard_map/pallas_call | solution.py:1355
  729.2 38.8 %shard_map.378 = (f32[448,1152]{1,0:T(8,128)}, f32[8,1152]{1,0:T(8,128)}, f32[4,1,1152]{2,1,0:T(1,128)}, bf16[2,4,1152,1152]{3,2,1,0:T(8,128)(2,1)}) custom-call(f32[448,1152]{1,0:T(8,128)} %get-tuple-element.72.x, f32[448,1152]{1,0:T(8,128)} %broadcast_add_fusion.grad, f32[8,1152]{1,0:T(8,128)} %get-tuple-element.187.mods, ...), custom_call_target="tpu_custom_call" | custom-call | tf_op jit(solution)/shard_map/pallas_call | solution.py:1718
  768.0 39.0 %shard_map.379 = (f32[448,1152]{1,0:T(8,128)}, f32[8,1152]{1,0:T(8,128)}, f32[4,1,896]{2,1,0:T(1,128)}, bf16[4,1152,1152]{2,1,0:T(8,128)(2,1)}) custom-call(f32[448,1152]{1,0:T(8,128)} %bitcast.126, f32[448,1152]{1,0:T(8,128)} %get-tuple-element.78.grad, f32[8,1152]{1,0:T(8,128)} %get-tuple-element.188.refs_1_.mods, f32[448,1152]{1,0:T(8,128)} %get-tuple-element.79.branch, ...), custom_call_target="tpu_custom_call" | custom-call | tf_op jit(solution)/shard_map/pallas_call | solution.py:1459
  807.1 24.1 %shard_map.380 = f32[4,2,56,1152]{3,2,1,0:T(8,128)} custom-call(f32[2,4,56,1152]{3,2,1,0:T(8,128)} %bitcast.143), custom_call_target="tpu_custom_call" | custom-call | tf_op jit(solution)/shard_map/pallas_call | solution.py:1122
  831.2 38.9 %shard_map.381 = (f32[448,1152]{1,0:T(8,128)}, f32[8,1152]{1,0:T(8,128)}, f32[4,1,1152]{2,1,0:T(1,128)}, bf16[2,4,1152,1152]{3,2,1,0:T(8,128)(2,1)}) custom-call(f32[448,1152]{1,0:T(8,128)} %get-tuple-element.68.refs_0_.x, f32[448,1152]{1,0:T(8,128)} %bitcast.135, f32[8,1152]{1,0:T(8,128)} %get-tuple-element.211.refs_1_.mods, ...), custom_call_target="tpu_custom_call" | custom-call | tf_op jit(solution)/shard_map/pallas_call | solution.py:1718
  870.0 30.4 %shard_map.382 = (f32[448,1152]{1,0:T(8,128)}, f32[128,1152]{1,0:T(8,128)}, f32[8,1152]{1,0:T(8,128)}, f32[4,1,1024]{2,1,0:T(1,128)}, bf16[4,1152,1152]{2,1,0:T(8,128)(2,1)}) custom-call(f32[448,1152]{1,0:T(8,128)} %get-tuple-element.66.refs_0_.x, f32[448,1152]{1,0:T(8,128)} %get-tuple-element.87.grad, bf16[128,1152]{1,0:T(8,128)(2,1)} %pad.36.refs_3_.context, ...), custom_call_target="tpu_custom_call" | custom-call | tf_op jit(solution)/shard_map/pallas_call | solution.py:1600
  902.3 17.4 %shard_map.388 = bf16[4,128,1152]{2,1,0:T(8,128)(2,1)} custom-call(bf16[128,1152]{1,0:T(8,128)(2,1)} %convert_element_type.157.x), custom_call_target="tpu_custom_call" | custom-call | tf_op jit(solution)/shard_map/pallas_call | solution.py:1122
  924.3 40.7 %shard_map.383 = (f32[448,1152]{1,0:T(8,128)}, f32[8,1152]{1,0:T(8,128)}, f32[4,1,896]{2,1,0:T(1,128)}, bf16[4,1152,1152]{2,1,0:T(8,128)(2,1)}) custom-call(f32[448,1152]{1,0:T(8,128)} %fusion.refs_0_.x, f32[448,1152]{1,0:T(8,128)} %get-tuple-element.91.grad, f32[8,1152]{1,0:T(8,128)} %get-tuple-element.209.refs_1_.mods, ...), custom_call_target="tpu_custom_call" | custom-call | tf_op jit(solution)/shard_map/pallas_call | solution.py:1459
  972.2 60.6 %shard_map.389 = f32[1,144,1152]{2,1,0:T(8,128)} custom-call(bf16[1,4,8,144,1152]{4,3,2,1,0:T(8,128)(2,1)} %bitcast.134), custom_call_target="tpu_custom_call" | custom-call | tf_op jit(solution)/shard_map/pallas_call | solution.py:1066
  1089.8 60.4 %shard_map.391 = f32[1,144,1152]{2,1,0:T(8,128)} custom-call(bf16[1,4,8,144,1152]{4,3,2,1,0:T(8,128)(2,1)} %bitcast.133), custom_call_target="tpu_custom_call" | custom-call | tf_op jit(solution)/shard_map/pallas_call | solution.py:1066
  1150.2 62.1 %shard_map.390 = f32[1,144,1152]{2,1,0:T(8,128)} custom-call(bf16[1,4,8,144,1152]{4,3,2,1,0:T(8,128)(2,1)} %bitcast.132), custom_call_target="tpu_custom_call" | custom-call | tf_op jit(solution)/shard_map/pallas_call | solution.py:1066
  1212.3 117.0 %shard_map.392 = f32[2,144,1152]{2,1,0:T(8,128)} custom-call(bf16[2,4,8,144,1152]{4,3,2,1,0:T(8,128)(2,1)} %bitcast.124), custom_call_target="tpu_custom_call" | custom-call | tf_op jit(solution)/shard_map/pallas_call | solution.py:1066
  1329.4 116.4 %shard_map.393 = f32[2,144,1152]{2,1,0:T(8,128)} custom-call(bf16[2,4,8,144,1152]{4,3,2,1,0:T(8,128)(2,1)} %bitcast.123), custom_call_target="tpu_custom_call" | custom-call | tf_op jit(solution)/shard_map/pallas_call | solution.py:1066
  1487.0 30.7 %shard_map.394 = f32[8,104,128]{2,1,0:T(8,128)} custom-call(f32[8,104,128]{2,1,0:T(8,128)} %bitcast.146), custom_call_target="tpu_custom_call" | custom-call | tf_op jit(solution)/shard_map/pallas_call | solution.py:1122
  (440 shorter events, 283.9 us)
Async XLA Ops:
  7.2 303.1 %all-gather.6.cloned.1.call-start = ((), (), s32[]{:S(2)}) async-start(), calls=%async_computation.3 | async-start | bytes 8847360 | tf_op jit(solution)/shard_map/all_gather | solution.py:1821
  10.3 298.9 %all-to-all-start = ((f32[4,112,32]{1,2,0:T(8,128)}), f32[4,112,32]{1,2,0:T(8,128)}, u32[]{:S(2)}, u32[]{:S(2)}) async-start(f32[4,112,32]{1,2,0:T(8,128)} %pad_maximum_fusion.3), calls=%async_computation | async-start | bytes 131072 | tf_op jit(solution)/shard_map/all_to_all | solution.py:1916
  14.2 338.9 %all-reduce.11.cloned.1.call-start = ((), (), s32[]{:S(2)}) async-start(), calls=%async_computation.1 | async-start | bytes 1327104 | tf_op jit(solution)/shard_map/psum | solution.py:1850
  17.2 1439.6 %all-gather.4.cloned.1.call-start = ((), (), s32[]{:S(2)}) async-start(), calls=%async_computation.2 | async-start | bytes 3870720 | tf_op jit(solution)/shard_map/all_gather | solution.py:1986
  67.8 42.6 %copy-start.59 = (f32[1152]{0:T(1024)S(1)}, f32[1152]{0:T(1024)}, u32[]{:S(2)}) copy-start(f32[1152]{0:T(1024)} %get-tuple-element.177) | copy-start | bytes 13828
  171.9 180.2 %copy-start.89 = (f32[288]{0:T(512)}, f32[288]{0:T(512)S(1)}, u32[]{:S(2)}) copy-start(f32[288]{0:T(512)S(1)} %dynamic_slice.31) | copy-start | bytes 3460
  242.3 66.7 %copy-start.85 = (f32[1,576]{1,0:T(1,128)S(1)}, f32[1,576]{1,0:T(1,128)}, u32[]{:S(2)}) copy-start(f32[1,576]{1,0:T(1,128)} %fusion.69) | copy-start | bytes 6916
  242.3 66.7 %copy-start.86 = (f32[1,576]{1,0:T(1,128)S(1)}, f32[1,576]{1,0:T(1,128)}, u32[]{:S(2)}) copy-start(f32[1,576]{1,0:T(1,128)} %fusion.70) | copy-start | bytes 6916
  924.2 42.9 %copy-start.84 = (f32[8,1152]{1,0:T(8,128)S(1)}, f32[8,1152]{1,0:T(8,128)}, u32[]{:S(2)}) copy-start(f32[8,1152]{1,0:T(8,128)} %get-tuple-element.98) | copy-start | bytes 110596
  924.2 43.6 %copy-start.83 = (f32[8,1152]{1,0:T(8,128)S(1)}, f32[8,1152]{1,0:T(8,128)}, u32[]{:S(2)}) copy-start(f32[8,1152]{1,0:T(8,128)} %get-tuple-element.99) | copy-start | bytes 110596
  924.2 44.2 %copy-start.82 = (f32[8,1152]{1,0:T(8,128)S(1)}, f32[8,1152]{1,0:T(8,128)}, u32[]{:S(2)}) copy-start(f32[8,1152]{1,0:T(8,128)} %get-tuple-element.100) | copy-start | bytes 110596
  924.2 44.8 %copy-start.53 = (f32[1152]{0:T(1024)S(1)}, f32[1152]{0:T(1024)}, u32[]{:S(2)}) copy-start(f32[1152]{0:T(1024)} %get-tuple-element.113) | copy-start | bytes 13828
  924.2 44.8 %copy-start.52 = (f32[1152]{0:T(1024)S(1)}, f32[1152]{0:T(1024)}, u32[]{:S(2)}) copy-start(f32[1152]{0:T(1024)} %get-tuple-element.115) | copy-start | bytes 13828
  924.3 45.4 %copy-start.6 = (bf16[448,1152]{1,0:T(8,128)(2,1)S(1)}, bf16[448,1152]{1,0:T(8,128)(2,1)}, u32[]{:S(2)}) copy-start(bf16[448,1152]{1,0:T(8,128)(2,1)} %copy-done.5) | copy-start | bytes 3096580
  924.3 45.4 %copy-start.26 = (f32[448,16]{0,1:T(8,128)S(1)}, f32[448,16]{0,1:T(8,128)}, u32[]{:S(2)}) copy-start(f32[448,16]{0,1:T(8,128)} %copy-done.25) | copy-start | bytes 86020
  924.3 45.4 %copy-start.28 = (f32[448,16]{0,1:T(8,128)S(1)}, f32[448,16]{0,1:T(8,128)}, u32[]{:S(2)}) copy-start(f32[448,16]{0,1:T(8,128)} %copy-done.27) | copy-start | bytes 86020
  972.2 63.9 %copy-start.7 = (f32[448,1152]{1,0:T(8,128)S(1)}, f32[448,1152]{1,0:T(8,128)}, u32[]{:S(2)}) copy-start(f32[448,1152]{1,0:T(8,128)} %get-tuple-element.96) | copy-start | bytes 6193156
  1329.3 116.5 %copy-start.33 = (f32[8,8,288]{2,1,0:T(8,128)S(1)}, f32[8,8,288]{2,1,0:T(8,128)}, u32[]{:S(2)}) copy-start(f32[8,8,288]{2,1,0:T(8,128)} %shard_map.387) | copy-start | bytes 221188
  1329.3 116.5 %copy-start.49 = (f32[8,288]{1,0:T(8,128)S(1)}, f32[8,288]{1,0:T(8,128)}, u32[]{:S(2)}) copy-start(f32[8,288]{1,0:T(8,128)} %copy-done.48) | copy-start | bytes 27652
  1329.4 116.5 %copy-start.50 = (f32[8,288]{1,0:T(8,128)S(1)}, f32[8,288]{1,0:T(8,128)}, u32[]{:S(2)}) copy-start(f32[8,288]{1,0:T(8,128)} %fusion.38.x) | copy-start | bytes 27652
  1329.4 116.5 %copy-start.67 = (f32[288]{0:T(512)S(1)}, f32[288]{0:T(512)}, u32[]{:S(2)}) copy-start(f32[288]{0:T(512)} %copy-done.66) | copy-start | bytes 3460
  1329.4 116.5 %copy-start.96 = (f32[8]{0:T(128)S(1)}, f32[8]{0:T(128)}, u32[]{:S(2)}) copy-start(f32[8]{0:T(128)} %get-tuple-element.219) | copy-start | bytes 100
  1329.4 116.9 %copy-start.93 = (f32[288]{0:T(512)S(1)}, f32[288]{0:T(512)}, u32[]{:S(2)}) copy-start(f32[288]{0:T(512)} %get-tuple-element.215) | copy-start | bytes 3460
  1329.4 117.1 %copy-start.1 = (f32[2,144,1152]{2,1,0:T(8,128)S(1)}, f32[2,144,1152]{2,1,0:T(8,128)}, u32[]{:S(2)}) copy-start(f32[2,144,1152]{2,1,0:T(8,128)} %shard_map.392) | copy-start | bytes 3981316
  (84 other events, 555.8 us)
Sparse Core Ops, SparseCore 0:
  10.2 136.4 all-gather.5
  150.7 86.5 all-reduce.10
  923.6 63.8 all-gather.3
where the time goes:
time: 1580 us
  Pallas kernels  1310 us (83%)
  local copies, waits for them, and re-layouts  118 us (7%)
  other arithmetic  85.4 us (5%)
  between operations  32 us (2%)
  matrix products  26.2 us (2%)
    pallas_call x5, Pallas kernels, scatter_one(): pl.pallas_call(functools.partial(scatter_kernel, chunks), out_shape=jax.S...  416 us
    pallas_call x4, Pallas kernels, call_with(): pl.pallas_call(with_gather(kernel, spots, len(in_specs), len(out_specs)),...  365 us
    pallas_call x13, Pallas kernels, exchange_call(): pl.pallas_call(kernel, out_shape=out_shape, in_specs=[spec], out_specs=sp...  258 us
    pallas_call x2, Pallas kernels, self_backward(): pl.pallas_call(functools.partial(self_backward_kernel, tiles), grid=(4,),...  79.8 us
    pallas_call x2, Pallas kernels, ffn_backward_chip(): pl.pallas_call(ffn_backward_kernel, grid=(4,), in_specs=[whole((PM, D)),...  77.7 us
    pallas_call x1, Pallas kernels, gather_all(): pl.pallas_call(functools.partial(gather_kernel, count), out_shape=[jax.Sh...  62.3 us
  transfers between devices with their start and end apart: 4, of which 0 were waited for; matrix products, arithmetic and copies ran while one was open for 8% of the time, Pallas kernels for 46%

commit v1 on v0

--- a/solution.py
+++ b/solution.py
@@ -689,7 +689,7 @@
 MESH = pl.DeviceIdType.MESH
 BLOCK = 144
 BIG = 58 * 2**20
-PIECES = {1: 2, 2: 1}
+PIECES = {1: 2, 2: 2}
 
 
 class Chips:
@@ -765,13 +765,17 @@
 
 
 class Gather(Work):
-    def __init__(self, chips, shard, full, send, recv, local):
+    def __init__(self, chips, shard, full, row, size, send, recv, local):
         super().__init__(chips, send, recv)
-        self.shard, self.full, self.local = shard, full, local
+        self.source, self.full, self.local = shard, full, local
+        self.rows = pl.ds(row, size)
+
+    def shard(self):
+        return self.source.at[:, self.rows]
 
     def block(self, jy, jz, jx, jc=0):
         chips = self.chips
-        return self.full.at[:, chips.mp_at(jy, jc), chips.dp_at(jz, jx)]
+        return self.full.at[:, chips.mp_at(jy, jc), chips.dp_at(jz, jx), self.rows]
 
     def arrive(self, jy, jz, jx, jc=0):
         self.arrived(self.block(jy, jz, jx, jc), jc * 16 + jy * 8 + jz * 2 + jx)
@@ -783,11 +787,11 @@
         self.pass_on((jy, jz, jx), 16 + jy * 8 + jz * 2 + jx, self.chips.peer_core)
 
     def own(self):
-        return pltpu.make_async_copy(self.shard, self.block(0, 0, 0), self.local)
+        return pltpu.make_async_copy(self.shard(), self.block(0, 0, 0), self.local)
 
     def begin(self):
         chips = self.chips
-        shard, block = (lambda: self.shard), (lambda: self.block(0, 0, 0))
+        shard, block = self.shard, (lambda: self.block(0, 0, 0))
         self.start(shard, block, 1, chips.peer_x)
         self.start(shard, block, 8, chips.peer_y)
         for j in (1, 2, 3):
@@ -822,7 +826,6 @@
             for jz in range(4):
                 for jx in range(2):
                     self.arrive(jy, jz, jx, 1)
-        self.finish()
 
     def steps(self):
         order = (0, 2, 1, 3)
@@ -868,43 +871,99 @@
     return None
 
 
-def gather_ticks(refs, spots):
-    chips = Chips()
-    work = Gather(chips, *refs)
-    steps = [step for phase in work.steps() for step in phase]
-    begin = steps[0]
-
+def woven(plans):
+    order = [step for plan in plans for step in plan[0]]
+    plans = [plan[1:] for plan in plans]
+    deep = max(len(plan) for plan in plans)
+    for turn in range(len(plans) + deep - 1):
+        for i, plan in enumerate(plans):
+            if 0 <= turn - i < len(plan):
+                order += plan[turn - i]
+    return order
+
+
+ROWS = {1: [144], 2: [80, 64], 3: [48, 48, 48]}
+GATHER_PIECES = {1: 3, 2: 3}
+
+
+def gather_steps(chips, shard, full, sems):
+    pieces = len(sems) // 3
+    sizes = ROWS[pieces]
+    works = [
+        Gather(chips, shard, full, sum(sizes[:i]), sizes[i], *sems[3 * i : 3 * i + 3])
+        for i in range(pieces)
+    ]
+
+    def finish():
+        for work in works:
+            work.finish()
+
+    return woven([work.steps() for work in works]) + [finish]
+
+
+def entered(chips, steps, begins, spots):
     def enter():
         chips.greet()
-        begin()
-
-    return Ticks([enter] + steps[1:], spots)
-
-
-def gather_kernel(count, *refs):
-    shards, fulls, sems = refs[:count], refs[count : 2 * count], refs[2 * count :]
+        for begin in steps[:begins]:
+            begin()
+
+    return Ticks([enter] + steps[begins:], spots)
+
+
+def gather_ticks(refs, spots, unused):
+    chips = Chips()
+    return entered(chips, gather_steps(chips, refs[0], refs[1], refs[2:]), len(refs) // 3, spots)
+
+
+def gather_kernel(shard, full, *sems):
     chips = Chips()
     chips.greet()
-    plans = [Gather(chips, shards[i], fulls[i], *sems[3 * i : 3 * i + 3]).steps() for i in range(count)]
-    for step in woven(plans):
+    for step in gather_steps(chips, shard, full, sems):
         step()
 
 
-def gather_all(shards, ident):
-    count = len(shards)
+def gather_all(shard, ident):
     return pl.pallas_call(
-        functools.partial(gather_kernel, count),
-        out_shape=[jax.ShapeDtypeStruct((s.shape[0], 4, 8) + s.shape[1:], s.dtype) for s in shards],
-        in_specs=[pl.BlockSpec(memory_space=pl.ANY)] * count,
-        out_specs=[pl.BlockSpec(memory_space=pl.ANY)] * count,
-        scratch_shapes=GATHER_SEMS * count,
+        gather_kernel,
+        out_shape=jax.ShapeDtypeStruct((shard.shape[0], 4, 8) + shard.shape[1:], shard.dtype),
+        in_specs=[pl.BlockSpec(memory_space=pl.ANY)],
+        out_specs=pl.BlockSpec(memory_space=pl.ANY),
+        scratch_shapes=GATHER_SEMS * GATHER_PIECES[shard.shape[0]],
         compiler_params=pltpu.CompilerParams(collective_id=ident, has_side_effects=True),
-    )(*shards)
+    )(shard)
+
+
+def sorted_columns(value):
+    return jnp.concatenate(
+        [value[:, (h * 4 + k) * HD : (h * 4 + k + 1) * HD] for k in range(4) for h in range(4)], 1
+    )
+
+
+def unsorted_columns(value):
+    return jnp.concatenate(
+        [value[:, (k * 4 + h) * HD : (k * 4 + h + 1) * HD] for h in range(4) for k in range(4)], 1
+    )
+
+
+def sort_kernel(mats, out):
+    out[0] = sorted_columns(mats[0]).astype(jnp.bfloat16)
+
+
+def sort_panels(mats):
+    spec = pl.BlockSpec((1,) + mats.shape[1:], lambda i: (i, 0, 0))
+    return pl.pallas_call(
+        sort_kernel,
+        grid=(3,),
+        in_specs=[spec],
+        out_specs=spec,
+        out_shape=jax.ShapeDtypeStruct(mats.shape, jnp.bfloat16),
+    )(mats)
 
 
 class Scatter(Work):
     def __init__(self, chips, full, total, m, row, near, far, own, send, recv, load):
         super().__init__(chips, send, recv)
+        self.sorted = full.shape[0] == 1
         self.full, self.total = full, total
         self.m, self.row, self.size = m, row, near.shape[1]
         self.near, self.far, self.own, self.load = near, far, own, load
@@ -1002,6 +1061,8 @@
             value = near[0, at].astype(jnp.float32) + own[buffer, at].astype(jnp.float32)
             for index in (4, 8, 12, 13, 14):
                 value += far[index, at].astype(jnp.float32)
+            if self.sorted:
+                value = unsorted_columns(value)
             self.total[self.m, pl.ds(pl.multiple_of(self.row + i * 16, 16), 16)] = value
             return carry
 
@@ -1019,7 +1080,7 @@
 
 
 def chunks_of(k, pieces):
-    sizes = {1: [144], 2: [80, 64], 3: [48, 48, 48]}[pieces]
+    sizes = ROWS[pieces]
     return [(m, sum(sizes[:i]), sizes[i]) for m in range(k) for i in range(pieces)]
 
 
@@ -1037,27 +1098,29 @@
     return out
 
 
-def woven(plans):
-    order = []
-    deep = max(len(plan) for plan in plans)
-    for turn in range(len(plans) + deep - 1):
-        for i, plan in enumerate(plans):
-            if 0 <= turn - i < len(plan):
-                order += plan[turn - i]
-    return order
-
-
-def scatter_kernel(chunks, full, total, *scratch):
-    chips = Chips()
-    chips.greet()
+def scatter_steps(chips, full, total, scratch, chunks):
     works = [
         Scatter(chips, full, total, m, row, *scratch[6 * i : 6 * i + 6])
         for i, (m, row, unused) in enumerate(chunks)
     ]
-    for step in woven([work.steps() for work in works]):
+
+    def finish():
+        for work in works:
+            work.finish()
+
+    return woven([work.steps() for work in works]) + [finish]
+
+
+def scatter_ticks(refs, spots, chunks):
+    chips = Chips()
+    return entered(chips, scatter_steps(chips, refs[0], refs[1], refs[2:], chunks), len(chunks), spots)
+
+
+def scatter_kernel(chunks, full, total, *scratch):
+    chips = Chips()
+    chips.greet()
+    for step in scatter_steps(chips, full, total, scratch, chunks):
         step()
-    for work in works:
-        work.finish()
 
 
 def scatter_one(full, ident, pieces=PIECES):
@@ -1327,7 +1390,7 @@
 
 
 def whole(shape):
-    return pl.BlockSpec(shape, lambda i: (0,) * len(shape))
+    return pl.BlockSpec(shape, lambda i: (0,) * len(shape), pipeline_mode=pl.Buffered(1))
 
 
 def slab(shape):
@@ -1340,18 +1403,18 @@
     return pltpu.CompilerParams(vmem_limit_bytes=BIG, collective_id=ident, has_side_effects=True)
 
 
-def with_gather(kernel, spots, inputs, outputs):
+def beside(kernel, ticks, spots, inputs, outputs, scratch, chunks):
     def run(*refs):
-        ins, shard = refs[:inputs], refs[inputs]
-        outs, full = refs[inputs + 1 : inputs + 1 + outputs], refs[inputs + 1 + outputs]
-        scratch, sems = refs[inputs + outputs + 2 : -3], refs[-3:]
-        kernel(gather_ticks((shard, full) + sems, spots), *ins, *outs, *scratch)
+        ins, given = refs[:inputs], refs[inputs]
+        outs, made = refs[inputs + 1 : inputs + 1 + outputs], refs[inputs + 1 + outputs]
+        rest = refs[inputs + outputs + 2 :]
+        kernel(ticks((given, made) + rest[scratch:], spots, chunks), *ins, *outs, *rest[:scratch])
 
     return run
 
 
-def call_with(kernel, spots, operands, in_specs, out_specs, out_shape, scratch, shard, ident):
-    if shard is None:
+def call_with(kernel, spots, operands, in_specs, out_specs, out_shape, scratch, given, ident):
+    if given is None:
         return pl.pallas_call(
             functools.partial(kernel, no_ticks),
             grid=(4,),
@@ -1362,19 +1425,28 @@
             compiler_params=grid_params(),
         )(*operands)
     remote = pl.BlockSpec(memory_space=pl.ANY)
-    full = jax.ShapeDtypeStruct((shard.shape[0], 4, 8) + shard.shape[1:], shard.dtype)
+    k = given.shape[0]
+    if given.ndim == 3:
+        ticks, chunks, extra = gather_ticks, None, GATHER_SEMS * GATHER_PIECES[k]
+        made = jax.ShapeDtypeStruct((k, 4, 8) + given.shape[1:], given.dtype)
+        made_spec = remote
+    else:
+        ticks, chunks = scatter_ticks, chunks_of(k, PIECES[k])
+        extra = scatter_scratch(chunks)
+        made = jax.ShapeDtypeStruct((k,) + given.shape[3:], jnp.float32)
+        made_spec = whole(made.shape)
     return pl.pallas_call(
-        with_gather(kernel, spots, len(in_specs), len(out_specs)),
+        beside(kernel, ticks, spots, len(in_specs), len(out_specs), len(scratch), chunks),
         grid=(4,),
         in_specs=in_specs + [remote],
-        out_specs=out_specs + [remote],
-        out_shape=out_shape + [full],
-        scratch_shapes=scratch + GATHER_SEMS,
+        out_specs=out_specs + [made_spec],
+        out_shape=out_shape + [made],
+        scratch_shapes=scratch + extra,
         compiler_params=grid_params(ident),
-    )(*operands, shard)
-
-
-def self_forward(x, mods, bias, panels, mask, tiles, shard=None, ident=None):
+    )(*operands, given)
+
+
+def self_forward(x, mods, bias, panels, mask, tiles, given=None, ident=None):
     f32, bf16 = jnp.float32, jnp.bfloat16
     rows = PM // tiles
     return call_with(
@@ -1391,16 +1463,17 @@
             jax.ShapeDtypeStruct((4, PM, 384), bf16),
         ],
         [pltpu.VMEM((PM, D), f32)],
-        shard,
+        given,
         ident,
     )
 
 
 def self_backward_kernel(
-    tiles, x, grad, mods, branch, source, proj, mixed, panel, mask, out, sums, d_bias, d_panel, d_branch, total
+    tiles, tick, x, grad, mods, branch, source, proj, mixed, panel, mask, out, sums, d_bias, d_panel, d_branch, total, pieces, held
 ):
     step = pl.program_id(0)
     rows = PM // tiles
+    tick(0)
 
     @pl.when(step == 0)
     def first():
@@ -1413,32 +1486,33 @@
 
     low = d_branch[...]
     d_mixed = mxu(low, panel[0, :, 768:]).astype(jnp.bfloat16)
-    values = proj[0]
-    d_query, d_key, d_value = [], [], []
+    held[...] = d_mixed
+    pieces[:, 3 * SPAN :] = jnp.zeros((PM, 32), jnp.bfloat16)
     for h in range(4):
         at = h * HD
-        tops = []
         for t in range(tiles):
-            part = values[t * rows : (t + 1) * rows]
-            tops.append(
-                head_backward(
-                    part[:, at : at + HD],
-                    part[:, SPAN + at : SPAN + at + HD],
-                    part[:, 2 * SPAN + at : 2 * SPAN + at + HD],
-                    mask[...],
-                    d_mixed[t * rows : (t + 1) * rows, 96 + at : 96 + at + HD],
-                )
+            here = slice(t * rows, (t + 1) * rows)
+            part = proj[0, here]
+            three = head_backward(
+                part[:, at : at + HD],
+                part[:, SPAN + at : SPAN + at + HD],
+                part[:, 2 * SPAN + at : 2 * SPAN + at + HD],
+                mask[...],
+                held[here, 96 + at : 96 + at + HD],
             )
-        for store, index in ((d_query, 0), (d_key, 1), (d_value, 2)):
-            pieces = [top[index] for top in tops]
-            store.append(jnp.concatenate(pieces, 0) if tiles > 1 else pieces[0])
-    d_proj = padded_heads(d_query + d_key + d_value, 0, 32).astype(jnp.bfloat16)
+            for index in range(3):
+                base = index * SPAN + at
+                pieces[here, base : base + HD] = three[index].astype(jnp.bfloat16)
+        tick(h + 1)
+    low = d_branch[...]
+    d_proj = pieces[...]
     d_bias[0] = jnp.sum(d_proj.astype(jnp.float32), 0, keepdims=True)
     columns = lax.broadcasted_iota(jnp.int32, (1, 896), 1)
     kept = jnp.where(columns < 3 * SPAN, panel[0, :, :896], jnp.zeros((), jnp.bfloat16))
     total[...] += mxu(d_proj, kept, CONTRACT_LAST)
     src = source[...]
     d_panel[0, :, :768] = mxu(src, d_proj[:, :768], CONTRACT_ROWS).astype(jnp.bfloat16)
+    tick(5)
     packed = mixed[0]
     d_panel[0, :, 768:896] = (
         mxu(src, d_proj[:, 768:], CONTRACT_ROWS) + mxu(low, packed[:, :128], CONTRACT_ROWS)
@@ -1452,14 +1526,17 @@
         sums[1:2] = d_scale
         out[...] = grad[...] + d_x
 
-
-def self_backward(x, grad, mods, branch, source, proj, mixed, panels, mask, tiles):
+    tick(6)
+
+
+def self_backward(x, grad, mods, branch, source, proj, mixed, panels, mask, tiles, given=None, ident=None):
     f32, bf16 = jnp.float32, jnp.bfloat16
     rows = PM // tiles
-    return pl.pallas_call(
+    return call_with(
         functools.partial(self_backward_kernel, tiles),
-        grid=(4,),
-        in_specs=[
+        7,
+        (x, grad, mods, branch, source, proj, mixed, panels, mask),
+        [
             whole((PM, D)),
             whole((PM, D)),
             whole((8, D)),
@@ -1470,16 +1547,22 @@
             slab((D, D)),
             whole((rows, rows)),
         ],
-        out_specs=[whole((PM, D)), whole((8, D)), slab((1, 896)), slab((D, D))],
-        out_shape=[
+        [whole((PM, D)), whole((8, D)), slab((1, 896)), slab((D, D))],
+        [
             jax.ShapeDtypeStruct((PM, D), f32),
             jax.ShapeDtypeStruct((8, D), f32),
             jax.ShapeDtypeStruct((4, 1, 896), f32),
             jax.ShapeDtypeStruct((4, D, D), bf16),
         ],
-        scratch_shapes=[pltpu.VMEM((PM, D), bf16), pltpu.VMEM((PM, D), f32)],
-        compiler_params=grid_params(),
-    )(x, grad, mods, branch, source, proj, mixed, panels, mask)
+        [
+            pltpu.VMEM((PM, D), bf16),
+            pltpu.VMEM((PM, D), f32),
+            pltpu.VMEM((PM, 896), bf16),
+            pltpu.VMEM((PM, 384), bf16),
+        ],
+        given,
+        ident,
+    )
 
 
 def cross_forward_kernel(tick, x, mods, bias, context, panel, mask, out, proj, pair, mixed, total):
@@ -1517,7 +1600,7 @@
     tick(5)
 
 
-def cross_forward(x, mods, bias, context, panels, mask, shard=None, ident=None):
+def cross_forward(x, mods, bias, context, panels, mask, given=None, ident=None):
     f32, bf16 = jnp.float32, jnp.bfloat16
     return call_with(
         cross_forward_kernel,
@@ -1539,15 +1622,16 @@
             jax.ShapeDtypeStruct((4, PM, 384), bf16),
         ],
         [pltpu.VMEM((PM, D), f32)],
-        shard,
+        given,
         ident,
     )
 
 
 def cross_backward_kernel(
-    x, grad, context, proj, pair, mixed, panel, mask, out, d_context, sums, d_bias, d_panel, total
+    tick, x, grad, context, proj, pair, mixed, panel, mask, out, d_context, sums, d_bias, d_panel, total, ask, keys, held
 ):
     step = pl.program_id(0)
+    tick(0)
 
     @pl.when(step == 0)
     def first():
@@ -1558,22 +1642,25 @@
 
     low = grad[...].astype(jnp.bfloat16)
     d_mixed = mxu(low, panel[0, :, 768:]).astype(jnp.bfloat16)
-    query, both = proj[0], pair[0]
-    d_query, d_key, d_value = [], [], []
+    held[...] = d_mixed
+    ask[:, SPAN:] = jnp.zeros((PM, 96), jnp.bfloat16)
+    keys[...] = jnp.zeros_like(keys)
     for h in range(4):
         at = h * HD
-        one = head_backward(
+        query, both = proj[0], pair[0]
+        three = head_backward(
             query[:, at : at + HD],
             both[:, 32 + at : 32 + at + HD],
             both[:, 32 + SPAN + at : 32 + SPAN + at + HD],
             mask[...],
-            d_mixed[:, 96 + at : 96 + at + HD],
+            held[:, 96 + at : 96 + at + HD],
         )
-        d_query.append(one[0])
-        d_key.append(one[1])
-        d_value.append(one[2])
-    d_ask = padded_heads(d_query, 0, 96).astype(jnp.bfloat16)
-    d_both = padded_heads(d_key + d_value, 32, 32).astype(jnp.bfloat16)
+        ask[:, at : at + HD] = three[0].astype(jnp.bfloat16)
+        keys[:, 32 + at : 32 + at + HD] = three[1].astype(jnp.bfloat16)
+        keys[:, 32 + SPAN + at : 32 + SPAN + at + HD] = three[2].astype(jnp.bfloat16)
+        tick(h + 1)
+    d_ask, d_both = ask[...], keys[...]
+    low = grad[...].astype(jnp.bfloat16)
     sum_both = jnp.sum(d_both.astype(jnp.float32), 0, keepdims=True)
     d_bias[0, :, :384] = jnp.sum(d_ask.astype(jnp.float32), 0, keepdims=True)
     d_bias[0, :, 384:] = sum_both
@@ -1584,6 +1671,7 @@
     d_panel[0, :, 256:384] = (
         mxu(src, d_ask[:, 256:], CONTRACT_ROWS) + mxu(ctx, d_both[:, :128], CONTRACT_ROWS)
     ).astype(jnp.bfloat16)
+    tick(5)
     d_panel[0, :, 384:768] = mxu(ctx, d_both[:, 128:512], CONTRACT_ROWS).astype(jnp.bfloat16)
     d_panel[0, :, 768:896] = (
         mxu(ctx, d_both[:, 512:], CONTRACT_ROWS) + mxu(low, packed[:, :128], CONTRACT_ROWS)
@@ -1594,13 +1682,16 @@
     def last():
         out[...] = grad[...] + total[...]
 
-
-def cross_backward(x, grad, context, proj, pair, mixed, panels, mask):
+    tick(6)
+
+
+def cross_backward(x, grad, context, proj, pair, mixed, panels, mask, given=None, ident=None):
     f32, bf16 = jnp.float32, jnp.bfloat16
-    return pl.pallas_call(
+    return call_with(
         cross_backward_kernel,
-        grid=(4,),
-        in_specs=[
+        7,
+        (x, grad, context, proj, pair, mixed, panels, mask),
+        [
             whole((PM, D)),
             whole((PM, D)),
             whole((128, D)),
@@ -1610,17 +1701,23 @@
             slab((D, D)),
             whole((128, 1)),
         ],
-        out_specs=[whole((PM, D)), whole((128, D)), whole((8, D)), slab((1, 1024)), slab((D, D))],
-        out_shape=[
+        [whole((PM, D)), whole((128, D)), whole((8, D)), slab((1, 1024)), slab((D, D))],
+        [
             jax.ShapeDtypeStruct((PM, D), f32),
             jax.ShapeDtypeStruct((128, D), f32),
             jax.ShapeDtypeStruct((8, D), f32),
             jax.ShapeDtypeStruct((4, 1, 1024), f32),
             jax.ShapeDtypeStruct((4, D, D), bf16),
         ],
-        scratch_shapes=[pltpu.VMEM((PM, D), f32)],
-        compiler_params=grid_params(),
-    )(x, grad, context, proj, pair, mixed, panels, mask)
+        [
+            pltpu.VMEM((PM, D), f32),
+            pltpu.VMEM((PM, 384), bf16),
+            pltpu.VMEM((128, 640), bf16),
+            pltpu.VMEM((PM, 384), bf16),
+        ],
+        given,
+        ident,
+    )
 
 
 GELU_A = math.sqrt(2.0 / math.pi)
@@ -1657,7 +1754,7 @@
     return pl.BlockSpec((1, 1, D, D), lambda i: (index, i, 0, 0))
 
 
-def ffn_forward_chip(x, mods, bias, panels, shard=None, ident=None):
+def ffn_forward_chip(x, mods, bias, panels, given=None, ident=None):
     f32, bf16 = jnp.float32, jnp.bfloat16
     return call_with(
         ffn_forward_kernel,
@@ -1672,15 +1769,16 @@
             jax.ShapeDtypeStruct((4, PM, D), f32),
         ],
         [pltpu.VMEM((PM, D), f32)],
-        shard,
+        given,
         ident,
     )
 
 
 def ffn_backward_kernel(
-    x, grad, mods, branch, source, pre, w_in, w_out, out, sums, d_bias, d_panel, d_branch, total
+    tick, x, grad, mods, branch, source, pre, w_in, w_out, out, sums, d_bias, d_panel, d_branch, total
 ):
     step = pl.program_id(0)
+    tick(0)
 
     @pl.when(step == 0)
     def first():
@@ -1700,9 +1798,12 @@
     )
     hidden = (0.5 * value * (1.0 + bent)).astype(jnp.bfloat16)
     d_pre = (mxu(low, w_out[0, 0]) * slope).astype(jnp.bfloat16)
+    tick(1)
     d_bias[0] = jnp.sum(d_pre.astype(jnp.float32), 0, keepdims=True)
     total[...] += mxu(d_pre, w_in[0, 0], CONTRACT_LAST)
+    tick(2)
     d_panel[0, 0] = mxu(source[...], d_pre, CONTRACT_ROWS).astype(jnp.bfloat16)
+    tick(3)
     d_panel[1, 0] = mxu(low, hidden, CONTRACT_ROWS).astype(jnp.bfloat16)
 
     @pl.when(step == 3)
@@ -1712,13 +1813,16 @@
         sums[1:2] = d_scale
         out[...] = grad[...] + d_x
 
-
-def ffn_backward_chip(x, grad, mods, branch, source, pre, panels):
+    tick(4)
+
+
+def ffn_backward_chip(x, grad, mods, branch, source, pre, panels, given=None, ident=None):
     f32, bf16 = jnp.float32, jnp.bfloat16
-    return pl.pallas_call(
+    return call_with(
         ffn_backward_kernel,
-        grid=(4,),
-        in_specs=[
+        5,
+        (x, grad, mods, branch, source, pre, panels, panels),
+        [
             whole((PM, D)),
             whole((PM, D)),
             whole((8, D)),
@@ -1728,21 +1832,22 @@
             half(0),
             half(1),
         ],
-        out_specs=[
+        [
             whole((PM, D)),
             whole((8, D)),
             slab((1, D)),
-            pl.BlockSpec((2, 1, D, D), lambda i: (0, i, 0, 0)),
+            pl.BlockSpec((2, 1, D, D), lambda i: (0, i, 0, 0), pipeline_mode=pl.Buffered(1)),
         ],
-        out_shape=[
+        [
             jax.ShapeDtypeStruct((PM, D), f32),
             jax.ShapeDtypeStruct((8, D), f32),
             jax.ShapeDtypeStruct((4, 1, D), f32),
             jax.ShapeDtypeStruct((2, 4, D, D), bf16),
         ],
-        scratch_shapes=[pltpu.VMEM((PM, D), bf16), pltpu.VMEM((PM, D), f32)],
-        compiler_params=grid_params(),
-    )(x, grad, mods, branch, source, pre, panels, panels)
+        [pltpu.VMEM((PM, D), bf16), pltpu.VMEM((PM, D), f32)],
+        given,
+        ident,
+    )
 
 
 def modulate_back(x, shift_vec, scale_vec, grad):
@@ -1790,14 +1895,14 @@
     bf16 = jnp.bfloat16
     f32 = jnp.float32
 
-    attn_low = attn_mats.astype(bf16).reshape(3, BLOCK, 4, 4, HD).swapaxes(2, 3).reshape(3, BLOCK, D)
+    attn_low = sort_panels(attn_mats)
     ffn_low = ffn_mats.astype(bf16)
 
     def panels(full):
         full = full.reshape(full.shape[:2] + (D, D))
         return full if full.shape[0] > 1 else full[0]
 
-    w_space = panels(gather_all([attn_low[0:1]], 0)[0])
+    w_space = panels(gather_all(attn_low[0:1], 0))
 
     pick = jnp.arange(clips, dtype=jnp.int32) == group
 
@@ -1959,22 +2064,18 @@
     grad_x, sums5, bias5, d_ffn1 = ffn_backward_chip(
         x5, grad_x, m_ffn1, branch5, source5, pre5, w_ffn1
     )
-    g_ffn1 = scatter_one(blocks(d_ffn1), 10)
-    grad_x, sums4, bias4, d_time = self_backward(
-        x4, grad_x, m_time, branch4, source4, proj4, mixed4, w_time, mask_time, 2
-    )
-    g_time = scatter_one(blocks(d_time), 11)
+    grad_x, sums4, bias4, d_time, g_ffn1 = self_backward(
+        x4, grad_x, m_time, branch4, source4, proj4, mixed4, w_time, mask_time, 2, blocks(d_ffn1), 10
+    )
     d_mods1 = jnp.concatenate([sums4[:3], sums5[:3]])
     grad_x = to_space(grad_x, 12)
 
-    grad_x, sums2, bias2, d_ffn0 = ffn_backward_chip(
-        x2, grad_x, m_ffn0, branch2, source2, pre2, w_ffn0
-    )
-    g_ffn0 = scatter_one(blocks(d_ffn0), 10)
-    grad_x, d_context, sums1, bias1, d_cross = cross_backward(
-        x1, grad_x, context, cross_q, cross_kv, mixed1, w_cross, mask_cross
-    )
-    g_cross = scatter_one(blocks(d_cross), 11)
+    grad_x, sums2, bias2, d_ffn0, g_time = ffn_backward_chip(
+        x2, grad_x, m_ffn0, branch2, source2, pre2, w_ffn0, blocks(d_time), 11
+    )
+    grad_x, d_context, sums1, bias1, d_cross, g_ffn0 = cross_backward(
+        x1, grad_x, context, cross_q, cross_kv, mixed1, w_cross, mask_cross, blocks(d_ffn0), 16
+    )
 
     first_part = (part == 0).astype(f32)
     d_context = over_parts(d_context)[:CAP].astype(bf16)
@@ -1992,10 +2093,10 @@
     d_c_one = lax.dot_general(cap_rows, d_c_pre_all, CONTRACT_ROWS, preferred_element_type=f32)
     d_c_two = lax.dot_general(d_context_all, c_hidden_all, CONTRACT_ROWS, preferred_element_type=f32)
 
-    grad_x, sums0, bias0, d_space = self_backward(
-        x0, grad_x, m_space, branch0, source0, proj0, mixed0, w_space, mask_space, 1
-    )
-    g_space = scatter_one(blocks(d_space), 11)
+    grad_x, sums0, bias0, d_space, g_cross = self_backward(
+        x0, grad_x, m_space, branch0, source0, proj0, mixed0, w_space, mask_space, 1, blocks(d_cross), 17
+    )
+    g_space = scatter_one(blocks(d_space), 18)
     d_mods0 = jnp.concatenate([sums0[:3], sums2[:3]])
 
     def side_sums(values, at_query, at_value, out_bias):
@@ -2067,7 +2168,6 @@
         [vector_grads[label].reshape(-1) for label, extent in vector_parts()]
     )
     g_attn = jnp.stack([g_space[0], g_time[0], g_cross[0]])
-    g_attn = g_attn.reshape(3, BLOCK, 4, 4, HD).swapaxes(2, 3).reshape(3, BLOCK, D)
     g_ffn = jnp.stack([g_ffn0, g_ffn1])
     matrix_squares = jnp.sum(g_attn * g_attn) + jnp.sum(g_ffn * g_ffn) + jnp.sum(g_embed * g_embed)
     length = vector_grad.shape[0]

time: 1580 us -> 1460 us (0.924)
  Pallas kernels: 1310 us -> 1200 us
  local copies, waits for them, and re-layouts: 118 us -> 99.1 us
    pallas_call x5 -> x1, Pallas kernels: 416 us -> 62 us  [scatter_one(): pl.pallas_call(functools.partial(scatter_kernel, chunks), out_shape=jax.S...]
    pallas_call x10, Pallas kernels: 616 us -> 811 us  [the longest x8 746 us: call_with(): pl.pallas_call(beside(kernel, ticks, spots, len(in_specs), len(out_specs)...]
    pallas_call x1 -> x2, Pallas kernels: 20.8 us -> 66.7 us  [call_with(): pl.pallas_call(functools.partial(kernel, no_ticks), grid=(4,), in_specs=i...]
    mul x3 -> x0, local copies, waits for them, and re-layouts: 18.9 us -> none  [per_device_chips(): g_attn * factor]
  transfers between devices with their start and end apart: 4 -> 4, of which waited for: 0 -> 0; matrix products, arithmetic and copies ran while one was open for 8% -> 9% of each run, Pallas kernels for 46% -> 30%
where the time goes in v1:
time: 1460 us; the launch traced here: 1450 us
  Pallas kernels  1200 us (82%)
  local copies, waits for them, and re-layouts  99.1 us (7%)
  other arithmetic  81.5 us (6%)
  between operations  32.2 us (2%)
  matrix products  28.4 us (2%)
    pallas_call x8, Pallas kernels, call_with(): pl.pallas_call(beside(kernel, ticks, spots, len(in_specs), len(out_specs)...  746 us
    pallas_call x13, Pallas kernels, exchange_call(): pl.pallas_call(kernel, out_shape=out_shape, in_specs=[spec], out_specs=sp...  259 us
    pallas_call x2, Pallas kernels, call_with(): pl.pallas_call(functools.partial(kernel, no_ticks), grid=(4,), in_specs=i...  66.7 us
    pallas_call x1, Pallas kernels, scatter_one(): pl.pallas_call(functools.partial(scatter_kernel, chunks), out_shape=jax.S...  62 us
    pallas_call x1, Pallas kernels, gather_all(): pl.pallas_call(gather_kernel, out_shape=jax.ShapeDtypeStruct((shard.shape...  62 us
  transfers between devices with their start and end apart: 4, of which 0 were waited for; matrix products, arithmetic and copies ran while one was open for 9% of the time, Pallas kernels for 30%

profile of v1, /device:TPU:24, one launch (start us, length us, event | category | flops | bytes accessed | tf_op | source)
XLA Modules:
  0.0 1445.2 jit_solution(12224882910623695791)
XLA Ops:
  48.0 9.2 shard_map.366
  59.1 28.4 %shard_map.367 = f32[8,8,1696]{2,1,0:T(8,128)} custom-call(f32[8,1696]{1,0:T(8,128)} %fusion.80.x), custom_call_target="tpu_custom_call" | custom-call | tf_op jit(solution)/shard_map/pallas_call | solution.py:1185
  90.1 31.5 %shard_map.368 = f32[8,8,1696]{2,1,0:T(8,128)} custom-call(f32[8,1696]{1,0:T(8,128)} %fusion.78.x), custom_call_target="tpu_custom_call" | custom-call | tf_op jit(solution)/shard_map/pallas_call | solution.py:1185
  153.2 62.0 %shard_map.370 = bf16[1,4,8,144,1152]{4,3,2,1,0:T(8,128)(2,1)} custom-call(bf16[1,144,1152]{2,1,0:T(8,128)(2,1)} %get-tuple-element.170.shard), custom_call_target="tpu_custom_call" | custom-call | tf_op jit(solution)/shard_map/pallas_call | solution.py:926
  216.2 66.9 %shard_map.371 = (f32[448,1152]{1,0:T(8,128)}, f32[448,1152]{1,0:T(8,128)}, bf16[448,1152]{1,0:T(8,128)(2,1)}, bf16[4,448,896]{2,1,0:T(8,128)(2,1)}, bf16[4,448,...) custom-call(f32[448,1152]{1,0:T(8,128)} %fusion.refs_0_, f32[8,1152]{1,0:T(8,128)} %get-tuple-element.217.refs_1_.refs_2_, ...), custom_call_target="tpu_custom_call" | custom-call | tf_op jit(solution)/shard_map/pallas_call | solution.py:1438
  288.1 38.8 %shard_map.372 = f32[8,120,288]{2,1,0:T(8,128)} custom-call(f32[8,120,288]{2,1,0:T(8,128)} %bitcast.141), custom_call_target="tpu_custom_call" | custom-call | tf_op jit(solution)/shard_map/pallas_call | solution.py:1185
  331.6 17.2 %shard_map.373 = bf16[4,128,1152]{2,1,0:T(8,128)(2,1)} custom-call(bf16[128,1152]{1,0:T(8,128)(2,1)} %pad.35.x), custom_call_target="tpu_custom_call" | custom-call | tf_op jit(solution)/shard_map/pallas_call | solution.py:1185
  351.1 101.5 %shard_map.374 = (f32[448,1152]{1,0:T(8,128)}, bf16[4,448,384]{2,1,0:T(8,128)(2,1)}, bf16[4,128,640]{2,1,0:T(8,128)(2,1)}, bf16[4,448,384]{2,1,0:T(8,128)(2,1)}, bf16[2,4,8,144,1152]{4,3,2,1,0:T(8,128)(2,1)}) custom-call(f32[448,1152]{1,0:T(8,128)} %get-tuple-element.70.refs_0_, f32[8,1152]{1,0:T(8,128)} %get-tuple-element.218.refs_1_, ...), custom_call_target="tpu_custom_call" | custom-call | tf_op jit(solution)/shard_map/pallas_call | solution.py:1438
  452.6 65.7 %shard_map.375 = (f32[448,1152]{1,0:T(8,128)}, f32[448,1152]{1,0:T(8,128)}, bf16[448,1152]{1,0:T(8,128)(2,1)}, f32[4,448,1152]{2,1,0:T(8,128)}, bf16[1,4,8,144,1152]{4,3,2,1,0:T(8,128)(2,1)}) custom-call(f32[448,1152]{1,0:T(8,128)} %get-tuple-element.72.refs_0_, f32[8,1152]{1,0:T(8,128)} %get-tuple-element.219.refs_1_.refs_2_, ...), custom_call_target="tpu_custom_call" | custom-call | tf_op jit(solution)/shard_map/pallas_call | solution.py:1438
  521.3 23.9 %shard_map.376 = f32[2,4,56,1152]{3,2,1,0:T(8,128)} custom-call(f32[4,2,56,1152]{3,2,1,0:T(8,128)} %bitcast.127), custom_call_target="tpu_custom_call" | custom-call | tf_op jit(solution)/shard_map/pallas_call | solution.py:1185
  545.2 107.5 %shard_map.377 = (f32[448,1152]{1,0:T(8,128)}, f32[448,1152]{1,0:T(8,128)}, bf16[448,1152]{1,0:T(8,128)(2,1)}, bf16[4,448,896]{2,1,0:T(8,128)(2,1)}, bf16[4,448,...) custom-call(f32[448,1152]{1,0:T(8,128)} %bitcast.121, f32[8,1152]{1,0:T(8,128)} %get-tuple-element.196.refs_1_.refs_2_, ...), custom_call_target="tpu_custom_call" | custom-call | tf_op jit(solution)/shard_map/pallas_call | solution.py:1438
  652.7 21.2 %shard_map.378 = (f32[448,1152]{1,0:T(8,128)}, f32[448,1152]{1,0:T(8,128)}, bf16[448,1152]{1,0:T(8,128)(2,1)}, f32[4,448,1152]{2,1,0:T(8,128)}) custom-call(f32[448,1152]{1,0:T(8,128)} %get-tuple-element.76.x, f32[8,1152]{1,0:T(8,128)} %get-tuple-element.195.mods, f32[4,1,1152]{2,1,0:T(1,128)} %slice.334.bias, bf16[2,4,1152,1152]{3,2,1,0:T(8,128)(2,1)} %bitcast.109, ...), custom_call_target="tpu_custom_call" | custom-call | tf_op jit(solution)/shard_map/pallas_call | solution.py:1418
  683.0 45.5 %shard_map.379 = (f32[448,1152]{1,0:T(8,128)}, f32[8,1152]{1,0:T(8,128)}, f32[4,1,1152]{2,1,0:T(1,128)}, bf16[2,4,1152,1152]{3,2,1,0:T(8,128)(2,1)}) custom-call(f32[448,1152]{1,0:T(8,128)} %get-tuple-element.76.x, f32[448,1152]{1,0:T(8,128)} %broadcast_add_fusion.grad, f32[8,1152]{1,0:T(8,128)} %get-tuple-element.195.mods, ...), custom_call_target="tpu_custom_call" | custom-call | tf_op jit(solution)/shard_map/pallas_call | solution.py:1418
  728.6 115.5 %shard_map.380 = (f32[448,1152]{1,0:T(8,128)}, f32[8,1152]{1,0:T(8,128)}, f32[4,1,896]{2,1,0:T(1,128)}, bf16[4,1152,1152]{2,1,0:T(8,128)(2,1)}, f32[2,144,1152]{2,1,0:T(8,128)}) custom-call(f32[448,1152]{1,0:T(8,128)} %bitcast.122, f32[448,1152]{1,0:T(8,128)} %get-tuple-element.82.refs_1_, f32[8,1152]{1,0:T(8,128)} %get-tuple-element.196.refs_1_.refs_2_, ...), custom_call_target="tpu_custom_call" | custom-call | tf_op jit(solution)/shard_map/pallas_call | solution.py:1438
  844.1 26.6 %shard_map.381 = f32[4,2,56,1152]{3,2,1,0:T(8,128)} custom-call(f32[2,4,56,1152]{3,2,1,0:T(8,128)} %bitcast.137), custom_call_target="tpu_custom_call" | custom-call | tf_op jit(solution)/shard_map/pallas_call | solution.py:1185
  870.7 79.3 %shard_map.382 = (f32[448,1152]{1,0:T(8,128)}, f32[8,1152]{1,0:T(8,128)}, f32[4,1,1152]{2,1,0:T(1,128)}, bf16[2,4,1152,1152]{3,2,1,0:T(8,128)(2,1)}, f32[1,144,1152]{2,1,0:T(8,128)}) custom-call(f32[448,1152]{1,0:T(8,128)} %get-tuple-element.72.refs_0_, f32[448,1152]{1,0:T(8,128)} %bitcast.126, f32[8,1152]{1,0:T(8,128)} %get-tuple-element.219.refs_1_.refs_2_, ...), custom_call_target="tpu_custom_call" | custom-call | tf_op jit(solution)/shard_map/pallas_call | solution.py:1438
  950.1 111.1 %shard_map.383 = (f32[448,1152]{1,0:T(8,128)}, f32[128,1152]{1,0:T(8,128)}, f32[8,1152]{1,0:T(8,128)}, f32[4,1,1024]{2,1,0:T(1,128)}, bf16[4,1152,1152]{2,1,0:T(8,128)(2,1)}, /*index=5*/f32[2,144,1152]{2,1,0:T(8,128)}) custom-call(f32[448,1152]{1,0:T(8,128)} %get-tuple-element.70.refs_0_, f32[448,1152]{1,0:T(8,128)} %get-tuple-element.93.refs_1_, ...), custom_call_target="tpu_custom_call" | custom-call | tf_op jit(solution)/shard_map/pallas_call | solution.py:1438
  1063.1 16.0 %shard_map.389 = bf16[4,128,1152]{2,1,0:T(8,128)(2,1)} custom-call(bf16[128,1152]{1,0:T(8,128)(2,1)} %convert_element_type.153.x), custom_call_target="tpu_custom_call" | custom-call | tf_op jit(solution)/shard_map/pallas_call | solution.py:1185
  1083.6 98.4 %shard_map.384 = (f32[448,1152]{1,0:T(8,128)}, f32[8,1152]{1,0:T(8,128)}, f32[4,1,896]{2,1,0:T(1,128)}, bf16[4,1152,1152]{2,1,0:T(8,128)(2,1)}, f32[1,144,1152]{2,1,0:T(8,128)}) custom-call(f32[448,1152]{1,0:T(8,128)} %fusion.refs_0_, f32[448,1152]{1,0:T(8,128)} %get-tuple-element.98.refs_1_, f32[8,1152]{1,0:T(8,128)} %get-tuple-element.217.refs_1_.refs_2_, ...), custom_call_target="tpu_custom_call" | custom-call | tf_op jit(solution)/shard_map/pallas_call | solution.py:1438
  1193.3 62.0 %shard_map.390 = f32[1,144,1152]{2,1,0:T(8,128)} custom-call(bf16[1,4,8,144,1152]{4,3,2,1,0:T(8,128)(2,1)} %bitcast.125), custom_call_target="tpu_custom_call" | custom-call | tf_op jit(solution)/shard_map/pallas_call | solution.py:1129
  1286.8 15.5 %shard_map.385 = f32[8,8,1008]{2,1,0:T(8,128)} custom-call(f32[8,1008]{1,0:T(8,128)} %reshape.397.x), custom_call_target="tpu_custom_call" | custom-call | tf_op jit(solution)/shard_map/pallas_call | solution.py:1185
  1306.8 8.6 shard_map.386
  1364.7 13.4 concatenate.83
  1378.2 29.4 %shard_map.391 = f32[8,104,128]{2,1,0:T(8,128)} custom-call(f32[8,104,128]{2,1,0:T(8,128)} %bitcast.140), custom_call_target="tpu_custom_call" | custom-call | tf_op jit(solution)/shard_map/pallas_call | solution.py:1185
  (413 shorter events, 217.9 us)
Async XLA Ops:
  7.2 277.9 %all-gather.6.cloned.1.call-start = ((), (), s32[]{:S(2)}) async-start(), calls=%async_computation.3 | async-start | bytes 8847360 | tf_op jit(solution)/shard_map/all_gather | solution.py:1926
  10.3 272.9 %all-to-all-start = ((f32[4,112,32]{1,2,0:T(8,128)}), f32[4,112,32]{1,2,0:T(8,128)}, u32[]{:S(2)}, u32[]{:S(2)}) async-start(f32[4,112,32]{1,2,0:T(8,128)} %pad_maximum_fusion.3), calls=%async_computation | async-start | bytes 131072 | tf_op jit(solution)/shard_map/all_to_all | solution.py:2021
  14.2 315.2 %all-reduce.11.cloned.1.call-start = ((), (), s32[]{:S(2)}) async-start(), calls=%async_computation.1 | async-start | bytes 1327104 | tf_op jit(solution)/shard_map/psum | solution.py:1955
  17.2 1330.6 %all-gather.4.cloned.1.call-start = ((), (), s32[]{:S(2)}) async-start(), calls=%async_computation.2 | async-start | bytes 3870720 | tf_op jit(solution)/shard_map/all_gather | solution.py:2087
  23.7 23.2 %copy-start.34 = (bf16[106016]{0:T(1024)(128)(2,1)}, bf16[106016]{0:T(1024)(128)(2,1)S(1)}, u32[]{:S(2)}) copy-start(bf16[106016]{0:T(1024)(128)(2,1)S(1)} %convert.16) | copy-start | bytes 636100
  47.0 42.0 %copy-start.71 = (bf16[8,128]{1,0:T(8,128)(2,1)}, bf16[8,128]{1,0:T(8,128)(2,1)S(1)}, u32[]{:S(2)}) copy-start(bf16[8,128]{1,0:T(8,128)(2,1)S(1)} %get-tuple-element.214) | copy-start | bytes 6148
  57.3 31.6 %copy-start.67 = (f32[288]{0:T(512)}, f32[288]{0:T(512)S(1)}, u32[]{:S(2)}) copy-start(f32[288]{0:T(512)S(1)} %dynamic_slice.28) | copy-start | bytes 3460
  58.2 29.3 %copy-start.52 = (f32[8,288]{1,0:T(8,128)}, f32[8,288]{1,0:T(8,128)S(1)}, u32[]{:S(2)}) copy-start(f32[8,288]{1,0:T(8,128)S(1)} %reduce_sum.352) | copy-start | bytes 27652
  89.1 34.8 %copy-start.47 = (f32[8,1152]{1,0:T(8,128)}, f32[8,1152]{1,0:T(8,128)S(1)}, u32[]{:S(2)}) copy-start(f32[8,1152]{1,0:T(8,128)S(1)} %get-tuple-element.165) | copy-start | bytes 110596
  89.1 587.3 %copy-start.48 = (f32[1152]{0:T(1024)}, f32[1152]{0:T(1024)S(1)}, u32[]{:S(2)}) copy-start(f32[1152]{0:T(1024)S(1)} %get-tuple-element.132) | copy-start | bytes 13828
  150.6 177.9 %copy-start.87 = (f32[288]{0:T(512)}, f32[288]{0:T(512)S(1)}, u32[]{:S(2)}) copy-start(f32[288]{0:T(512)S(1)} %dynamic_slice.31) | copy-start | bytes 3460
  216.2 66.9 %copy-start.85 = (f32[1,576]{1,0:T(1,128)S(1)}, f32[1,576]{1,0:T(1,128)}, u32[]{:S(2)}) copy-start(f32[1,576]{1,0:T(1,128)} %fusion.68) | copy-start | bytes 6916
  216.2 66.9 %copy-start.86 = (f32[1,576]{1,0:T(1,128)S(1)}, f32[1,576]{1,0:T(1,128)}, u32[]{:S(2)}) copy-start(f32[1,576]{1,0:T(1,128)} %fusion.69) | copy-start | bytes 6916
  328.5 21.8 %copy-start.26 = (f32[120,288]{0,1:T(8,128)}, f32[120,288]{0,1:T(8,128)S(1)}, u32[]{:S(2)}) copy-start(f32[120,288]{0,1:T(8,128)S(1)} %copy.75) | copy-start | bytes 414724
  1061.1 19.5 %copy-start.24 = (bf16[1152,288]{0,1:T(8,128)(2,1)S(1)}, bf16[1152,288]{0,1:T(8,128)(2,1)}, u32[]{:S(2)}) copy-start(bf16[1152,288]{0,1:T(8,128)(2,1)} %all-reduce.11.cloned.1.call-done) | copy-start | bytes 1990660
  1080.6 101.5 %copy-start.20 = (bf16[128,1152]{1,0:T(8,128)(2,1)}, bf16[128,1152]{1,0:T(8,128)(2,1)S(1)}, u32[]{:S(2)}) copy-start(bf16[128,1152]{1,0:T(8,128)(2,1)S(1)} %reduce) | copy-start | bytes 884740
  1083.6 101.2 %copy-start.84 = (f32[8,1152]{1,0:T(8,128)S(1)}, f32[8,1152]{1,0:T(8,128)}, u32[]{:S(2)}) copy-start(f32[8,1152]{1,0:T(8,128)} %get-tuple-element.106) | copy-start | bytes 110596
  1083.6 102.5 %copy-start.83 = (f32[8,1152]{1,0:T(8,128)S(1)}, f32[8,1152]{1,0:T(8,128)}, u32[]{:S(2)}) copy-start(f32[8,1152]{1,0:T(8,128)} %get-tuple-element.107) | copy-start | bytes 110596
  1083.6 103.7 %copy-start.82 = (f32[8,1152]{1,0:T(8,128)S(1)}, f32[8,1152]{1,0:T(8,128)}, u32[]{:S(2)}) copy-start(f32[8,1152]{1,0:T(8,128)} %get-tuple-element.108) | copy-start | bytes 110596
  1083.6 104.9 %copy-start.57 = (f32[1152]{0:T(1024)S(1)}, f32[1152]{0:T(1024)}, u32[]{:S(2)}) copy-start(f32[1152]{0:T(1024)} %get-tuple-element.121) | copy-start | bytes 13828
  1083.6 105.5 %copy-start.56 = (f32[1152]{0:T(1024)S(1)}, f32[1152]{0:T(1024)}, u32[]{:S(2)}) copy-start(f32[1152]{0:T(1024)} %get-tuple-element.123) | copy-start | bytes 13828
  1083.6 106.6 %copy-start.3 = (bf16[448,1152]{1,0:T(8,128)(2,1)S(1)}, bf16[448,1152]{1,0:T(8,128)(2,1)}, u32[]{:S(2)}) copy-start(bf16[448,1152]{1,0:T(8,128)(2,1)} %copy-done.2) | copy-start | bytes 3096580
  1083.6 106.6 %copy-start.30 = (f32[448,16]{0,1:T(8,128)S(1)}, f32[448,16]{0,1:T(8,128)}, u32[]{:S(2)}) copy-start(f32[448,16]{0,1:T(8,128)} %copy-done.29) | copy-start | bytes 86020
  1193.3 70.0 %copy-start.4 = (f32[448,1152]{1,0:T(8,128)S(1)}, f32[448,1152]{1,0:T(8,128)}, u32[]{:S(2)}) copy-start(f32[448,1152]{1,0:T(8,128)} %get-tuple-element.104) | copy-start | bytes 6193156
  (77 other events, 444.2 us)
Sparse Core Ops, SparseCore 0:
  10.2 136.0 all-gather.5
  150.3 89.4 all-reduce.10
  1082.9 91.6 all-gather.3

commit v2 on v1

--- a/solution.py
+++ b/solution.py
@@ -1138,163 +1138,6 @@
     )(full)
 
 
-CLIPS, PARTS = 8, 4
-
-
-def all_peers(names):
-    peers = []
-    for name, size in ((DP, CLIPS), (MP, PARTS)):
-        if name in names:
-            me = lax.axis_index(name)
-            peers += [{name: (me + o) % size} for o in range(1, size)]
-    return peers
-
-
-def greet_all(peers):
-    barrier = pltpu.get_barrier_semaphore()
-    for peer in peers:
-        pl.semaphore_signal(barrier, inc=1, device_id=peer, device_id_type=MESH)
-    pl.semaphore_wait(barrier, len(peers))
-
-
-def trade(name, size, source, target, landing, send, recv, first=0):
-    me = lax.axis_index(name)
-
-    def copy(o, src, dst):
-        return pltpu.make_async_remote_copy(
-            src_ref=src,
-            dst_ref=dst,
-            send_sem=send.at[first + o],
-            recv_sem=recv.at[first + o],
-            device_id={name: (me + o) % size},
-            device_id_type=MESH,
-        )
-
-    out = [copy(o, source((me + o) % size), target()) for o in range(1, size)]
-    for one in out:
-        one.start()
-    for o in range(1, size):
-        land = landing((me + size - o) % size)
-        copy(o, land, land).wait_recv()
-    for one in out:
-        one.wait_send()
-
-
-def exchange_call(kernel, ident, out_shape, scratch, operand, anywhere=False):
-    spec = pl.BlockSpec(memory_space=pl.ANY if anywhere else pltpu.VMEM)
-    return pl.pallas_call(
-        kernel,
-        out_shape=out_shape,
-        in_specs=[spec],
-        out_specs=spec,
-        scratch_shapes=scratch + [pltpu.SemaphoreType.DMA((18,)), pltpu.SemaphoreType.DMA((18,))],
-        compiler_params=pltpu.CompilerParams(
-            collective_id=ident, has_side_effects=True, vmem_limit_bytes=BIG
-        ),
-    )(operand)
-
-
-def share_kernel(name, size, x, out, send, recv):
-    me = lax.axis_index(name)
-    greet_all(all_peers((name,)))
-    out[me] = x[...]
-    trade(name, size, lambda to: x, lambda: out.at[me], lambda at: out.at[at], send, recv)
-
-
-def share(x, name, ident):
-    size = CLIPS if name == DP else PARTS
-    shape = jax.ShapeDtypeStruct((size,) + x.shape, x.dtype)
-    return exchange_call(functools.partial(share_kernel, name, size), ident, shape, [], x)
-
-
-def gathered_sum(refs, count):
-    value = refs[0]
-    for i in range(1, count):
-        value = value + refs[i]
-    return value
-
-
-def part_sum_kernel(x, out, near, one, send, recv):
-    part, clip = lax.axis_index(MP), lax.axis_index(DP)
-    greet_all(all_peers((DP, MP)))
-    near[part] = x[...]
-    trade(MP, PARTS, lambda to: x, lambda: near.at[part], lambda at: near.at[at], send, recv, 8)
-    one[...] = gathered_sum(near, PARTS)
-    out[clip] = one[...]
-    trade(DP, CLIPS, lambda to: one, lambda: out.at[clip], lambda at: out.at[at], send, recv)
-
-
-def part_sum(x, ident):
-    scratch = [pltpu.VMEM((PARTS,) + x.shape, x.dtype), pltpu.VMEM(x.shape, x.dtype)]
-    shape = jax.ShapeDtypeStruct((CLIPS,) + x.shape, x.dtype)
-    return exchange_call(part_sum_kernel, ident, shape, scratch, x)
-
-
-def whole_sum_kernel(x, out, far, near, one, two, send, recv):
-    part, clip = lax.axis_index(MP), lax.axis_index(DP)
-    greet_all(all_peers((DP, MP)))
-    far[clip] = x[clip]
-    trade(DP, CLIPS, lambda to: x.at[to], lambda: far.at[clip], lambda at: far.at[at], send, recv)
-    one[...] = gathered_sum(far, CLIPS)
-    near[part] = one[...]
-    trade(MP, PARTS, lambda to: one, lambda: near.at[part], lambda at: near.at[at], send, recv, 7)
-    two[...] = gathered_sum(near, PARTS)
-    out[clip] = two[...]
-    trade(DP, CLIPS, lambda to: two, lambda: out.at[clip], lambda at: out.at[at], send, recv, 10)
-
-
-def whole_sum(x, ident):
-    row = x.shape[1:]
-    scratch = [pltpu.VMEM((n,) + row, x.dtype) for n in (CLIPS, PARTS)]
-    scratch += [pltpu.VMEM(row, x.dtype)] * 2
-    return exchange_call(whole_sum_kernel, ident, jax.ShapeDtypeStruct(x.shape, x.dtype), scratch, x)
-
-
-def deal_kernel(x, out, send, recv):
-    clip = lax.axis_index(DP)
-    greet_all(all_peers((DP,)))
-    out[clip] = x[clip]
-    trade(DP, CLIPS, lambda to: x.at[to], lambda: out.at[clip], lambda at: out.at[at], send, recv)
-
-
-def deal(x, ident):
-    return exchange_call(deal_kernel, ident, jax.ShapeDtypeStruct(x.shape, x.dtype), [], x)
-
-
-def to_time_kernel(x, out, local, send, recv):
-    part = lax.axis_index(MP)
-    greet_all(all_peers((MP,)))
-    own = pltpu.make_async_copy(x.at[part], out.at[:, part], local)
-    own.start()
-    trade(MP, PARTS, lambda to: x.at[to], lambda: out.at[:, part], lambda at: out.at[:, at], send, recv)
-    own.wait()
-
-
-def to_space_kernel(x, out, local, send, recv):
-    part = lax.axis_index(MP)
-    greet_all(all_peers((MP,)))
-    own = pltpu.make_async_copy(x.at[:, part], out.at[part], local)
-    own.start()
-    trade(MP, PARTS, lambda to: x.at[:, to], lambda: out.at[part], lambda at: out.at[at], send, recv)
-    own.wait()
-
-
-def to_time(x, ident):
-    shape = jax.ShapeDtypeStruct((2, FR, PM // 8, D), x.dtype)
-    operand = x.reshape(FR, 2, PM // 8, D)
-    return exchange_call(
-        to_time_kernel, ident, shape, [pltpu.SemaphoreType.DMA], operand, True
-    ).reshape(PM, D)
-
-
-def to_space(x, ident):
-    shape = jax.ShapeDtypeStruct((FR, 2, PM // 8, D), x.dtype)
-    operand = x.reshape(2, FR, PM // 8, D)
-    return exchange_call(
-        to_space_kernel, ident, shape, [pltpu.SemaphoreType.DMA], operand, True
-    ).reshape(PM, D)
-
-
 def normal_parts(x):
     centered = x - jnp.mean(x, -1, keepdims=True)
     inverse = lax.rsqrt(jnp.mean(centered * centered, -1, keepdims=True) + EPS_NORM)
@@ -1836,7 +1679,11 @@
             whole((PM, D)),
             whole((8, D)),
             slab((1, D)),
-            pl.BlockSpec((2, 1, D, D), lambda i: (0, i, 0, 0), pipeline_mode=pl.Buffered(1)),
+            pl.BlockSpec(
+                (2, 1, D, D),
+                lambda i: (0, i, 0, 0),
+                pipeline_mode=pl.Buffered(2 if given is None else 1),
+            ),
         ],
         [
             jax.ShapeDtypeStruct((PM, D), f32),
@@ -1848,6 +1695,346 @@
         given,
         ident,
     )
+
+
+CLIPS, PARTS = 8, 4
+HOLDERS = -(-(TFREQ + TXT) // EMB_LOCAL)
+
+
+def all_peers(names):
+    peers = []
+    for name, size in ((DP, CLIPS), (MP, PARTS)):
+        if name in names:
+            me = lax.axis_index(name)
+            peers += [{name: (me + o) % size} for o in range(1, size)]
+    return peers
+
+
+def greet_all(peers):
+    barrier = pltpu.get_barrier_semaphore()
+    for peer in peers:
+        pl.semaphore_signal(barrier, inc=1, device_id=peer, device_id_type=MESH)
+    pl.semaphore_wait(barrier, len(peers))
+
+
+def trade(name, size, source, target, landing, send, recv, first=0):
+    me = lax.axis_index(name)
+
+    def copy(o, src, dst):
+        return pltpu.make_async_remote_copy(
+            src_ref=src,
+            dst_ref=dst,
+            send_sem=send.at[first + o],
+            recv_sem=recv.at[first + o],
+            device_id={name: (me + o) % size},
+            device_id_type=MESH,
+        )
+
+    out = [copy(o, source((me + o) % size), target()) for o in range(1, size)]
+    for one in out:
+        one.start()
+    for o in range(1, size):
+        land = landing((me + size - o) % size)
+        copy(o, land, land).wait_recv()
+    for one in out:
+        one.wait_send()
+
+
+def exchange_call(kernel, ident, out_shape, scratch, operand, anywhere=False):
+    spec = pl.BlockSpec(memory_space=pl.ANY if anywhere else pltpu.VMEM)
+    return pl.pallas_call(
+        kernel,
+        out_shape=out_shape,
+        in_specs=[spec],
+        out_specs=spec,
+        scratch_shapes=scratch + [pltpu.SemaphoreType.DMA((18,)), pltpu.SemaphoreType.DMA((18,))],
+        compiler_params=pltpu.CompilerParams(
+            collective_id=ident, has_side_effects=True, vmem_limit_bytes=BIG
+        ),
+    )(operand)
+
+
+def share_kernel(name, size, x, out, send, recv):
+    me = lax.axis_index(name)
+    greet_all(all_peers((name,)))
+    out[me] = x[...]
+    trade(name, size, lambda to: x, lambda: out.at[me], lambda at: out.at[at], send, recv)
+
+
+def share(x, name, ident):
+    size = CLIPS if name == DP else PARTS
+    shape = jax.ShapeDtypeStruct((size,) + x.shape, x.dtype)
+    return exchange_call(functools.partial(share_kernel, name, size), ident, shape, [], x)
+
+
+def gathered_sum(refs, count):
+    value = refs[0]
+    for i in range(1, count):
+        value = value + refs[i]
+    return value
+
+
+def part_sum_kernel(x, out, near, one, send, recv):
+    part, clip = lax.axis_index(MP), lax.axis_index(DP)
+    greet_all(all_peers((DP, MP)))
+    near[part] = x[...]
+    trade(MP, PARTS, lambda to: x, lambda: near.at[part], lambda at: near.at[at], send, recv, 8)
+    one[...] = gathered_sum(near, PARTS)
+    out[clip] = one[...]
+    trade(DP, CLIPS, lambda to: one, lambda: out.at[clip], lambda at: out.at[at], send, recv)
+
+
+def part_sum(x, ident):
+    scratch = [pltpu.VMEM((PARTS,) + x.shape, x.dtype), pltpu.VMEM(x.shape, x.dtype)]
+    shape = jax.ShapeDtypeStruct((CLIPS,) + x.shape, x.dtype)
+    return exchange_call(part_sum_kernel, ident, shape, scratch, x)
+
+
+def whole_sum_kernel(rows, count, *refs):
+    pieces, out = refs[:count], refs[count]
+    x, far, near, one, two, send, recv = refs[count + 1 :]
+    part, clip = lax.axis_index(MP), lax.axis_index(DP)
+    greet_all(all_peers((DP, MP)))
+    at = 0
+    for piece in pieces:
+        x[at : at + piece.shape[0]] = piece[...]
+        at += piece.shape[0]
+    x[at:] = jnp.zeros((x.shape[0] - at, x.shape[1]), x.dtype)
+
+    def own(to):
+        return x.at[pl.ds(pl.multiple_of(to * rows, rows), rows)]
+
+    far[clip] = own(clip)[...]
+    trade(DP, CLIPS, own, lambda: far.at[clip], lambda at: far.at[at], send, recv)
+    one[...] = gathered_sum(far, CLIPS)
+    near[part] = one[...]
+    trade(MP, PARTS, lambda to: one, lambda: near.at[part], lambda at: near.at[at], send, recv, 7)
+    two[...] = gathered_sum(near, PARTS)
+    out[clip] = two[...]
+    trade(DP, CLIPS, lambda to: two, lambda: out.at[clip], lambda at: out.at[at], send, recv, 10)
+
+
+def whole_sum(pieces, ident):
+    width = pieces[0].shape[1]
+    total = -(-sum(piece.shape[0] for piece in pieces) // 128) * 128
+    rows, f32 = total // CLIPS, jnp.float32
+    vmem = pl.BlockSpec(memory_space=pltpu.VMEM)
+    return pl.pallas_call(
+        functools.partial(whole_sum_kernel, rows, len(pieces)),
+        out_shape=jax.ShapeDtypeStruct((CLIPS, rows, width), f32),
+        in_specs=[vmem] * len(pieces),
+        out_specs=vmem,
+        scratch_shapes=[
+            pltpu.VMEM((total, width), f32),
+            pltpu.VMEM((CLIPS, rows, width), f32),
+            pltpu.VMEM((PARTS, rows, width), f32),
+            pltpu.VMEM((rows, width), f32),
+            pltpu.VMEM((rows, width), f32),
+            pltpu.SemaphoreType.DMA((18,)),
+            pltpu.SemaphoreType.DMA((18,)),
+        ],
+        compiler_params=pltpu.CompilerParams(
+            collective_id=ident, has_side_effects=True, vmem_limit_bytes=BIG
+        ),
+    )(*pieces).reshape(total, width)
+
+
+def deal_kernel(x, out, send, recv):
+    clip = lax.axis_index(DP)
+    greet_all(all_peers((DP,)))
+
+    def copies(source):
+        return [
+            pltpu.make_async_remote_copy(
+                src_ref=x.at[(clip + o) % CLIPS],
+                dst_ref=out.at[source],
+                send_sem=send.at[o],
+                recv_sem=recv.at[source],
+                device_id={DP: (clip + o) % CLIPS},
+                device_id_type=MESH,
+            )
+            for o in range(1, CLIPS)
+        ]
+
+    for source in range(HOLDERS):
+
+        @pl.when(clip == source)
+        def give(source=source):
+            out[source] = x[source]
+            for copy in copies(source):
+                copy.start()
+
+    for source in range(HOLDERS):
+
+        @pl.when(clip != source)
+        def take(source=source):
+            land = out.at[source]
+            pltpu.make_async_remote_copy(
+                src_ref=land,
+                dst_ref=land,
+                send_sem=send.at[1],
+                recv_sem=recv.at[source],
+                device_id={DP: (clip + 1) % CLIPS},
+                device_id_type=MESH,
+            ).wait_recv()
+
+        @pl.when(clip == source)
+        def sent(source=source):
+            for copy in copies(source):
+                copy.wait_send()
+
+
+def deal(x, ident):
+    shape = jax.ShapeDtypeStruct((HOLDERS,) + x.shape[1:], x.dtype)
+    return exchange_call(deal_kernel, ident, shape, [], x)
+
+
+def silu(value):
+    return value * jax.nn.sigmoid(value)
+
+
+def start_kernel(
+    shard, freq, table, bias_one, bias_two, full, t_pre, t_emb, mods, *scratch
+):
+    part, clip = lax.axis_index(MP), lax.axis_index(DP)
+    far_one, near_two, far_two, near_three = scratch[:4]
+    one, two, three, send, recv = scratch[4:9]
+    sems = scratch[9:]
+    chips = Chips()
+    greet_all(all_peers((DP, MP)))
+    one[...] = mxu(freq[...], table[...])
+    far_one[clip] = one[...]
+    trade(DP, CLIPS, lambda to: one, lambda: far_one.at[clip], lambda at: far_one.at[at], send, recv)
+    pre = gathered_sum(far_one, CLIPS) + bias_one[...]
+    t_pre[...] = pre
+    near_two[part] = mxu(silu(pre).astype(jnp.bfloat16), table[...], CONTRACT_LAST)
+    mine = near_two.at[part]
+    trade(MP, PARTS, lambda to: mine, lambda: mine, lambda at: near_two.at[at], send, recv, 7)
+    two[...] = gathered_sum(near_two, PARTS)
+    lead = TFREQ + TXT
+    holder, row = lead // EMB_LOCAL, lead % EMB_LOCAL
+    give(two, far_two, (holder, holder + 1), send, recv, 11)
+    steps = gather_steps(chips, shard, full, sems)
+    for step in steps[: len(sems) // 3]:
+        step()
+    emb = [far_two[0][:, row:], far_two[1][:, : D + row - EMB_LOCAL]]
+    emb = jnp.concatenate(emb, 1) + bias_two[...]
+    t_emb[...] = emb
+    local = emb[:, :SPAN]
+    for i in range(1, PARTS):
+        local = jnp.where(part == i, emb[:, i * SPAN : (i + 1) * SPAN], local)
+    near_three[part] = mxu(silu(local).astype(jnp.bfloat16), table[...], CONTRACT_LAST)
+    last = near_three.at[part]
+    trade(MP, PARTS, lambda to: last, lambda: last, lambda at: near_three.at[at], send, recv, 21)
+    product = gathered_sum(near_three, PARTS)
+    for i in range(CLIPS):
+        three[i] = product[i : i + 1]
+    mods[clip] = three[clip]
+    trade(DP, CLIPS, lambda to: three.at[to], lambda: mods.at[clip], lambda at: mods.at[at], send, recv, 24)
+    for step in steps[len(sems) // 3 :]:
+        step()
+
+
+def give(x, out, sources, send, recv, first):
+    clip = lax.axis_index(DP)
+
+    def copies(i):
+        return [
+            pltpu.make_async_remote_copy(
+                src_ref=x,
+                dst_ref=out.at[i],
+                send_sem=send.at[first + o],
+                recv_sem=recv.at[first + i],
+                device_id={DP: (clip + o) % CLIPS},
+                device_id_type=MESH,
+            )
+            for o in range(1, CLIPS)
+        ]
+
+    for i, source in enumerate(sources):
+
+        @pl.when(clip == source)
+        def begin(i=i):
+            out[i] = x[...]
+            for copy in copies(i):
+                copy.start()
+
+    for i, source in enumerate(sources):
+
+        @pl.when(clip != source)
+        def take(i=i):
+            copies(i)[0].wait_recv()
+
+        @pl.when(clip == source)
+        def sent(i=i):
+            for copy in copies(i):
+                copy.wait_send()
+
+
+def start(shard, freq, table, bias_one, bias_two, ident):
+    f32 = jnp.float32
+    wide = (CLIPS, EMB_LOCAL)
+    vmem, remote = pl.BlockSpec(memory_space=pltpu.VMEM), pl.BlockSpec(memory_space=pl.ANY)
+    return pl.pallas_call(
+        start_kernel,
+        out_shape=[
+            jax.ShapeDtypeStruct((shard.shape[0], 4, 8) + shard.shape[1:], shard.dtype),
+            jax.ShapeDtypeStruct((CLIPS, SPAN), f32),
+            jax.ShapeDtypeStruct((CLIPS, D), f32),
+            jax.ShapeDtypeStruct((CLIPS, 1, EMB_LOCAL), f32),
+        ],
+        in_specs=[remote, vmem, vmem, vmem, vmem],
+        out_specs=[remote, vmem, vmem, vmem],
+        scratch_shapes=[
+            pltpu.VMEM((CLIPS, CLIPS, SPAN), f32),
+            pltpu.VMEM((PARTS,) + wide, f32),
+            pltpu.VMEM((2,) + wide, f32),
+            pltpu.VMEM((PARTS,) + wide, f32),
+            pltpu.VMEM((CLIPS, SPAN), f32),
+            pltpu.VMEM(wide, f32),
+            pltpu.VMEM((CLIPS, 1, EMB_LOCAL), f32),
+            pltpu.SemaphoreType.DMA((32,)),
+            pltpu.SemaphoreType.DMA((32,)),
+        ]
+        + GATHER_SEMS * GATHER_PIECES[shard.shape[0]],
+        compiler_params=pltpu.CompilerParams(
+            collective_id=ident, has_side_effects=True, vmem_limit_bytes=BIG
+        ),
+    )(shard, freq, table, bias_one, bias_two)
+
+
+def to_time_kernel(x, out, local, send, recv):
+    part = lax.axis_index(MP)
+    greet_all(all_peers((MP,)))
+    own = pltpu.make_async_copy(x.at[part], out.at[:, part], local)
+    own.start()
+    trade(MP, PARTS, lambda to: x.at[to], lambda: out.at[:, part], lambda at: out.at[:, at], send, recv)
+    own.wait()
+
+
+def to_space_kernel(x, out, local, send, recv):
+    part = lax.axis_index(MP)
+    greet_all(all_peers((MP,)))
+    own = pltpu.make_async_copy(x.at[:, part], out.at[part], local)
+    own.start()
+    trade(MP, PARTS, lambda to: x.at[:, to], lambda: out.at[part], lambda at: out.at[at], send, recv)
+    own.wait()
+
+
+def to_time(x, ident):
+    shape = jax.ShapeDtypeStruct((2, FR, PM // 8, D), x.dtype)
+    operand = x.reshape(FR, 2, PM // 8, D)
+    return exchange_call(
+        to_time_kernel, ident, shape, [pltpu.SemaphoreType.DMA], operand, True
+    ).reshape(PM, D)
+
+
+def to_space(x, ident):
+    shape = jax.ShapeDtypeStruct((FR, 2, PM // 8, D), x.dtype)
+    operand = x.reshape(2, FR, PM // 8, D)
+    return exchange_call(
+        to_space_kernel, ident, shape, [pltpu.SemaphoreType.DMA], operand, True
+    ).reshape(PM, D)
 
 
 def modulate_back(x, shift_vec, scale_vec, grad):
@@ -1902,7 +2089,6 @@
         full = full.reshape(full.shape[:2] + (D, D))
         return full if full.shape[0] > 1 else full[0]
 
-    w_space = panels(gather_all(attn_low[0:1], 0))
 
     pick = jnp.arange(clips, dtype=jnp.int32) == group
 
@@ -1929,24 +2115,24 @@
     freq = waves(timesteps.astype(f32), TFREQ).astype(bf16)
     freq_rows = local_rows(jnp.pad(freq, ((0, 0), (0, EMB_ALL - TFREQ))), group)
 
-    def from_rows(local):
-        return part_sum(local, 1).swapaxes(0, 1).reshape(clips, EMB_ALL)
+    full, t_pre, t_emb_all, mod_rows = start(
+        attn_low[0:1],
+        freq_rows,
+        embed_low,
+        own_slice(parts[T_BIAS_ONE], part, width_local)[None],
+        parts[T_BIAS_TWO][None],
+        0,
+    )
+    w_space = panels(full)
+    t_hidden = jax.nn.silu(t_pre).astype(bf16)
+    t_emb_local = lax.dynamic_slice_in_dim(t_emb_all, part * width_local, width_local, 1)
+    silu_local = jax.nn.silu(t_emb_local).astype(bf16)
+    mod_sum = mod_rows.reshape(EMB_ALL)
+    t_mod_vec = mod_sum[lead + 2 * D :] + parts[T_BIAS_MOD]
+    t_emb = jnp.sum(jnp.where(pick[:, None], t_emb_all, 0.0), 0)
 
     def over_clips(value):
         return jnp.sum(share(value, DP, 2), 0)
-
-    t_pre = over_clips(jnp.dot(freq_rows, embed_low, preferred_element_type=f32))
-    t_pre = t_pre + own_slice(parts[T_BIAS_ONE], part, width_local)
-    t_hidden = jax.nn.silu(t_pre).astype(bf16)
-    t_sum = from_rows(lax.dot_general(t_hidden, embed_low, CONTRACT_LAST, preferred_element_type=f32))
-    t_emb_all = t_sum[:, lead : lead + D] + parts[T_BIAS_TWO]
-    t_emb_local = lax.dynamic_slice_in_dim(t_emb_all, part * width_local, width_local, 1)
-    silu_local = jax.nn.silu(t_emb_local).astype(bf16)
-    mod_sum = from_rows(
-        lax.dot_general(silu_local, embed_low, CONTRACT_LAST, preferred_element_type=f32)
-    )[:, lead + 2 * D :]
-    t_mod_vec = jnp.sum(jnp.where(pick[:, None], mod_sum, 0.0), 0) + parts[T_BIAS_MOD]
-    t_emb = jnp.sum(jnp.where(pick[:, None], t_emb_all, 0.0), 0)
 
     c_two_row = lead + D - group * EMB_LOCAL
     c_row_ids = c_two_row + jnp.arange(D, dtype=jnp.int32)
@@ -1954,7 +2140,8 @@
     c_two = lax.dynamic_slice_in_dim(embed_low, jnp.clip(c_two_row, 0, EMB_LOCAL - D), D, 0)
     c_two = lax.psum(jnp.where(c_held, c_two, jnp.zeros_like(c_two)), DP)
     c_product = jnp.dot(cap_rows, embed_low, preferred_element_type=f32)
-    c_pre = jnp.sum(deal(c_product.reshape(clips, CAP, width_local), 3), 0)
+    c_product = jnp.pad(c_product.astype(bf16).reshape(clips, CAP, width_local), ((0, 0), (0, 8), (0, 0)))
+    c_pre = jnp.sum(deal(c_product, 3).astype(f32), 0)[:CAP]
     c_pre = c_pre + own_slice(parts[C_BIAS_ONE], part, width_local)
     c_hidden = gelu_tanh(c_pre).astype(bf16)
     c_part = lax.dot_general(c_hidden, c_two, CONTRACT_LAST, preferred_element_type=f32)
@@ -2091,7 +2278,10 @@
     c_hidden_all = caption_all[:, D : D + width_local]
     d_c_pre_all = caption_all[:, D + width_local :]
     d_c_one = lax.dot_general(cap_rows, d_c_pre_all, CONTRACT_ROWS, preferred_element_type=f32)
-    d_c_two = lax.dot_general(d_context_all, c_hidden_all, CONTRACT_ROWS, preferred_element_type=f32)
+    context_rows = local_rows(
+        jnp.pad(d_context_all, ((0, 0), (lead + D, EMB_ALL - lead - 2 * D))), group
+    )
+    d_c_two = lax.dot_general(context_rows, c_hidden_all, CONTRACT_ROWS, preferred_element_type=f32)
 
     grad_x, sums0, bias0, d_space, g_cross = self_backward(
         x0, grad_x, m_space, branch0, source0, proj0, mixed0, w_space, mask_space, 1, blocks(d_cross), 17
@@ -2134,49 +2324,48 @@
         lax.dot_general(d_mod_rows, silu_local, CONTRACT_ROWS, preferred_element_type=f32)
         + outer(jnp.concatenate([d_temb_rows, freq_rows.astype(f32)]), jnp.concatenate([t_hidden.astype(f32), d_t_pre]))
         + d_c_one
-    )
-    here = lax.dynamic_slice_in_dim(g_embed, jnp.clip(c_two_row, 0, EMB_LOCAL - D), D, 0)
-    g_embed = lax.dynamic_update_slice_in_dim(
-        g_embed, jnp.where(c_held, d_c_two, here), jnp.clip(c_two_row, 0, EMB_LOCAL - D), 0
-    )
-
-    first_clip = pick.astype(f32) * first_part
-    vector_grads = {
-        PATCH_W: d_patch_w,
-        PATCH_B: d_patch_b,
-        FINAL_W: d_final_w,
-        FINAL_B: d_final_b,
-        T_BIAS_ONE: placed(jnp.sum(d_t_pre * pick.astype(f32)[:, None], 0), part, D),
-        T_BIAS_TWO: d_temb_part
-        + placed(jnp.sum(d_temb_local * pick.astype(f32)[:, None], 0), part, D),
-        T_BIAS_MOD: d_mod_part,
-        C_BIAS_ONE: placed(d_c_bias_one, part, D),
-        C_BIAS_TWO: d_c_bias_two,
-        ATTN_BIAS: jnp.stack(
-            [
-                side_sums(bias0, 0, 2 * SPAN, sums0[3]),
-                side_sums(bias4, 0, 2 * SPAN, sums4[3]),
-                side_sums(bias1, 0, 416 + SPAN, sums1[0]),
-            ]
-        ),
-        FFN_BIAS_ONE: jnp.stack([bias2, bias5]),
-        FFN_BIAS_TWO: jnp.stack([sums2[3], sums5[3]]),
-        TABLES: jnp.stack([d_mods0, d_mods1]),
-        FINAL_TABLE: jnp.stack([d_final_shift, d_final_scale]),
-    }
-    vector_grad = jnp.concatenate(
-        [vector_grads[label].reshape(-1) for label, extent in vector_parts()]
-    )
+        + d_c_two
+    )
+
+    here = pick.astype(f32)[:, None]
+
+    def place_row(local):
+        return placed(jnp.sum(local * here, 0), part, D)[None]
+
+    vector_rows = [
+            d_patch_w,
+            d_patch_b[None],
+            d_final_w,
+            place_row(d_t_pre),
+            d_temb_part[None] + place_row(d_temb_local),
+            d_mods0 + d_mods1,
+            placed(d_c_bias_one, part, D)[None],
+            d_c_bias_two[None],
+            side_sums(bias0, 0, 2 * SPAN, sums0[3]),
+            side_sums(bias4, 0, 2 * SPAN, sums4[3]),
+            side_sums(bias1, 0, 416 + SPAN, sums1[0]),
+            bias2[:, 0],
+            bias5[:, 0],
+            sums2[3:4],
+            sums5[3:4],
+            d_mods0,
+            d_mods1,
+            d_final_shift[None],
+            d_final_scale[None],
+    ]
     g_attn = jnp.stack([g_space[0], g_time[0], g_cross[0]])
     g_ffn = jnp.stack([g_ffn0, g_ffn1])
     matrix_squares = jnp.sum(g_attn * g_attn) + jnp.sum(g_ffn * g_ffn) + jnp.sum(g_embed * g_embed)
-    length = vector_grad.shape[0]
-    spare = -(length + 2) % (8 * 8 * 128)
-    totals = jnp.concatenate([vector_grad, matrix_squares[None], loss_part[None], jnp.zeros((spare,), f32)])
-    totals = whole_sum(totals.reshape(8, -1, 128), 15).reshape(-1)
-    g_vector = totals[:length]
-    loss_total = totals[length + 1]
-    squares = totals[length] + jnp.sum(g_vector * g_vector)
+    count_rows = sum(rows.shape[0] for rows in vector_rows)
+    tail = jnp.concatenate([d_final_b, matrix_squares[None], loss_part[None], jnp.zeros((D - COUT - 2,), f32)])
+    totals = whole_sum(vector_rows + [tail[None]], 15)
+    tail = totals[count_rows]
+    cut = CIN + 1 + COUT
+    g_vector = jnp.concatenate(
+        [totals[:cut].reshape(-1), tail[:COUT], totals[cut:count_rows].reshape(-1)]
+    )
+    loss_total = tail[COUT + 1]
+    squares = tail[COUT] + jnp.sum(g_vector * g_vector)
     grad_norm = jnp.sqrt(squares)
     factor = CLIP_NORM / (grad_norm + 1e-06)
     new_attn = adam_update(

time: 1460 us -> 1400 us (0.959)
  local copies, waits for them, and re-layouts: 99.1 us -> 65.9 us
    pallas_call x1 -> x2, Pallas kernels: 62 us -> 181 us  [the longest x1 145 us: start(): pl.pallas_call(start_kernel, out_shape=[jax.ShapeDtypeStruct((shard.shape...]
    pallas_call x13 -> x9, Pallas kernels: 259 us -> 146 us  [exchange_call(): pl.pallas_call(kernel, out_shape=out_shape, in_specs=[spec], out_specs=sp...]
  transfers between devices with their start and end apart: 4 -> 4, of which waited for: 0 -> 0; matrix products, arithmetic and copies ran while one was open for 9% -> 7% of each run, Pallas kernels for 30% -> 31%
where the time goes in v2:
time: 1400 us; the launch traced here: 1390 us
  Pallas kernels  1190 us (85%)
  other arithmetic  75.1 us (5%)
  local copies, waits for them, and re-layouts  65.9 us (5%)
  between operations  32.2 us (2%)
  matrix products  22.4 us (2%)
    pallas_call x8, Pallas kernels, call_with(): pl.pallas_call(beside(kernel, ticks, spots, len(in_specs), len(out_specs)...  738 us
    pallas_call x9, Pallas kernels, exchange_call(): pl.pallas_call(kernel, out_shape=out_shape, in_specs=[spec], out_specs=sp...  146 us
    pallas_call x1, Pallas kernels, start(): pl.pallas_call(start_kernel, out_shape=[jax.ShapeDtypeStruct((shard.shape...  145 us
    pallas_call x1, Pallas kernels, scatter_one(): pl.pallas_call(functools.partial(scatter_kernel, chunks), out_shape=jax.S...  61.9 us
    pallas_call x2, Pallas kernels, call_with(): pl.pallas_call(functools.partial(kernel, no_ticks), grid=(4,), in_specs=i...  59.5 us
    pallas_call x1, Pallas kernels, whole_sum(): pl.pallas_call(functools.partial(whole_sum_kernel, rows, len(pieces)), ou...  36.6 us
  transfers between devices with their start and end apart: 4, of which 0 were waited for; matrix products, arithmetic and copies ran while one was open for 7% of the time, Pallas kernels for 31%

profile of v2, /device:TPU:24, one launch (start us, length us, event | category | flops | bytes accessed | tf_op | source)
XLA Modules:
  0.0 1389.8 jit_solution(2011426499632587854)
XLA Ops:
  53.4 144.6 %shard_map.367 = (bf16[1,4,8,144,1152]{4,3,2,1,0:T(8,128)(2,1)}, f32[8,288]{1,0:T(8,128)}, f32[8,1152]{1,0:T(8,128)}, f32[8,1,1696]{2,1,0:T(1,128)}) custom-call(bf16[1,144,1152]{2,1,0:T(8,128)(2,1)} %get-tuple-element.178.shard, bf16[8,1696]{1,0:T(8,128)(2,1)} %get-tuple-element.170.freq, bf16[1696,288]{1,0:T(8,128)(2,1)} %copy-done.1, ...), custom_call_target="tpu_custom_call" | custom-call | tf_op jit(solution)/shard_map/pallas_call | solution.py:1978
  201.6 6.5 multiply_cosine_fusion
  224.2 65.6 %shard_map.368 = (f32[448,1152]{1,0:T(8,128)}, f32[448,1152]{1,0:T(8,128)}, bf16[448,1152]{1,0:T(8,128)(2,1)}, bf16[4,448,896]{2,1,0:T(8,128)(2,1)}, bf16[4,448,...) custom-call(f32[448,1152]{1,0:T(8,128)} %fusion.1.refs_0_, f32[8,1152]{1,0:T(8,128)} %get-tuple-element.215.refs_1_.refs_2_, ...), custom_call_target="tpu_custom_call" | custom-call | tf_op jit(solution)/shard_map/pallas_call | solution.py:1281
  293.4 23.5 %shard_map.369 = bf16[3,128,288]{2,1,0:T(8,128)(2,1)} custom-call(bf16[8,128,288]{2,1,0:T(8,128)(2,1)} %pad.43.x), custom_call_target="tpu_custom_call" | custom-call | tf_op jit(solution)/shard_map/pallas_call | solution.py:1745
  321.5 18.8 %shard_map.370 = bf16[4,128,1152]{2,1,0:T(8,128)(2,1)} custom-call(bf16[128,1152]{1,0:T(8,128)(2,1)} %pad.44.x), custom_call_target="tpu_custom_call" | custom-call | tf_op jit(solution)/shard_map/pallas_call | solution.py:1745
  342.6 100.5 %shard_map.371 = (f32[448,1152]{1,0:T(8,128)}, bf16[4,448,384]{2,1,0:T(8,128)(2,1)}, bf16[4,128,640]{2,1,0:T(8,128)(2,1)}, bf16[4,448,384]{2,1,0:T(8,128)(2,1)}, bf16[2,4,8,144,1152]{4,3,2,1,0:T(8,128)(2,1)}) custom-call(f32[448,1152]{1,0:T(8,128)} %get-tuple-element.76.refs_0_, f32[8,1152]{1,0:T(8,128)} %get-tuple-element.216.refs_1_, ...), custom_call_target="tpu_custom_call" | custom-call | tf_op jit(solution)/shard_map/pallas_call | solution.py:1281
  443.1 61.9 %shard_map.372 = (f32[448,1152]{1,0:T(8,128)}, f32[448,1152]{1,0:T(8,128)}, bf16[448,1152]{1,0:T(8,128)(2,1)}, f32[4,448,1152]{2,1,0:T(8,128)}, bf16[1,4,8,144,1152]{4,3,2,1,0:T(8,128)(2,1)}) custom-call(f32[448,1152]{1,0:T(8,128)} %get-tuple-element.78.refs_0_, f32[8,1152]{1,0:T(8,128)} %get-tuple-element.217.refs_1_.refs_2_, ...), custom_call_target="tpu_custom_call" | custom-call | tf_op jit(solution)/shard_map/pallas_call | solution.py:1281
  508.0 25.3 %shard_map.373 = f32[2,4,56,1152]{3,2,1,0:T(8,128)} custom-call(f32[4,2,56,1152]{3,2,1,0:T(8,128)} %bitcast.115), custom_call_target="tpu_custom_call" | custom-call | tf_op jit(solution)/shard_map/pallas_call | solution.py:1745
  533.2 103.0 %shard_map.374 = (f32[448,1152]{1,0:T(8,128)}, f32[448,1152]{1,0:T(8,128)}, bf16[448,1152]{1,0:T(8,128)(2,1)}, bf16[4,448,896]{2,1,0:T(8,128)(2,1)}, bf16[4,448,...) custom-call(f32[448,1152]{1,0:T(8,128)} %bitcast.109, f32[8,1152]{1,0:T(8,128)} %get-tuple-element.204.refs_1_.refs_2_, ...), custom_call_target="tpu_custom_call" | custom-call | tf_op jit(solution)/shard_map/pallas_call | solution.py:1281
  636.2 20.9 %shard_map.375 = (f32[448,1152]{1,0:T(8,128)}, f32[448,1152]{1,0:T(8,128)}, bf16[448,1152]{1,0:T(8,128)(2,1)}, f32[4,448,1152]{2,1,0:T(8,128)}) custom-call(f32[448,1152]{1,0:T(8,128)} %get-tuple-element.82.x, f32[8,1152]{1,0:T(8,128)} %get-tuple-element.203.mods, f32[4,1,1152]{2,1,0:T(1,128)} %slice.349.bias, bf16[2,4,1152,1152]{3,2,1,0:T(8,128)(2,1)} %bitcast.97, ...), custom_call_target="tpu_custom_call" | custom-call | tf_op jit(solution)/shard_map/pallas_call | solution.py:1261
  665.3 38.6 %shard_map.376 = (f32[448,1152]{1,0:T(8,128)}, f32[8,1152]{1,0:T(8,128)}, f32[4,1,1152]{2,1,0:T(1,128)}, bf16[2,4,1152,1152]{3,2,1,0:T(8,128)(2,1)}) custom-call(f32[448,1152]{1,0:T(8,128)} %get-tuple-element.82.x, f32[448,1152]{1,0:T(8,128)} %broadcast_add_fusion.grad, f32[8,1152]{1,0:T(8,128)} %get-tuple-element.203.mods, ...), custom_call_target="tpu_custom_call" | custom-call | tf_op jit(solution)/shard_map/pallas_call | solution.py:1261
  703.9 118.1 %shard_map.377 = (f32[448,1152]{1,0:T(8,128)}, f32[8,1152]{1,0:T(8,128)}, f32[4,1,896]{2,1,0:T(1,128)}, bf16[4,1152,1152]{2,1,0:T(8,128)(2,1)}, f32[2,144,1152]{2,1,0:T(8,128)}) custom-call(f32[448,1152]{1,0:T(8,128)} %bitcast.110, f32[448,1152]{1,0:T(8,128)} %get-tuple-element.89.refs_1_, f32[8,1152]{1,0:T(8,128)} %get-tuple-element.204.refs_1_.refs_2_, ...), custom_call_target="tpu_custom_call" | custom-call | tf_op jit(solution)/shard_map/pallas_call | solution.py:1281
  822.0 23.8 %shard_map.378 = f32[4,2,56,1152]{3,2,1,0:T(8,128)} custom-call(f32[2,4,56,1152]{3,2,1,0:T(8,128)} %bitcast.123), custom_call_target="tpu_custom_call" | custom-call | tf_op jit(solution)/shard_map/pallas_call | solution.py:1745
  845.8 78.5 %shard_map.379 = (f32[448,1152]{1,0:T(8,128)}, f32[8,1152]{1,0:T(8,128)}, f32[4,1,1152]{2,1,0:T(1,128)}, bf16[2,4,1152,1152]{3,2,1,0:T(8,128)(2,1)}, f32[1,144,1152]{2,1,0:T(8,128)}) custom-call(f32[448,1152]{1,0:T(8,128)} %get-tuple-element.78.refs_0_, f32[448,1152]{1,0:T(8,128)} %bitcast.114, f32[8,1152]{1,0:T(8,128)} %get-tuple-element.217.refs_1_.refs_2_, ...), custom_call_target="tpu_custom_call" | custom-call | tf_op jit(solution)/shard_map/pallas_call | solution.py:1281
  924.3 111.0 %shard_map.380 = (f32[448,1152]{1,0:T(8,128)}, f32[128,1152]{1,0:T(8,128)}, f32[8,1152]{1,0:T(8,128)}, f32[4,1,1024]{2,1,0:T(1,128)}, bf16[4,1152,1152]{2,1,0:T(8,128)(2,1)}, /*index=5*/f32[2,144,1152]{2,1,0:T(8,128)}) custom-call(f32[448,1152]{1,0:T(8,128)} %get-tuple-element.76.refs_0_, f32[448,1152]{1,0:T(8,128)} %get-tuple-element.100.refs_1_, ...), custom_call_target="tpu_custom_call" | custom-call | tf_op jit(solution)/shard_map/pallas_call | solution.py:1281
  1037.1 16.1 %shard_map.386 = bf16[4,128,1152]{2,1,0:T(8,128)(2,1)} custom-call(bf16[128,1152]{1,0:T(8,128)(2,1)} %convert_element_type.161.x), custom_call_target="tpu_custom_call" | custom-call | tf_op jit(solution)/shard_map/pallas_call | solution.py:1745
  1057.1 99.7 %shard_map.381 = (f32[448,1152]{1,0:T(8,128)}, f32[8,1152]{1,0:T(8,128)}, f32[4,1,896]{2,1,0:T(1,128)}, bf16[4,1152,1152]{2,1,0:T(8,128)(2,1)}, f32[1,144,1152]{2,1,0:T(8,128)}) custom-call(f32[448,1152]{1,0:T(8,128)} %fusion.1.refs_0_, f32[448,1152]{1,0:T(8,128)} %get-tuple-element.105.refs_1_, f32[8,1152]{1,0:T(8,128)} %get-tuple-element.215.refs_1_.refs_2_, ...), custom_call_target="tpu_custom_call" | custom-call | tf_op jit(solution)/shard_map/pallas_call | solution.py:1281
  1164.7 61.9 %shard_map.387 = f32[1,144,1152]{2,1,0:T(8,128)} custom-call(bf16[1,4,8,144,1152]{4,3,2,1,0:T(8,128)(2,1)} %bitcast.113), custom_call_target="tpu_custom_call" | custom-call | tf_op jit(solution)/shard_map/pallas_call | solution.py:1129
  1237.1 15.5 %shard_map.382 = f32[8,8,1008]{2,1,0:T(8,128)} custom-call(f32[8,1008]{1,0:T(8,128)} %reshape.402.x), custom_call_target="tpu_custom_call" | custom-call | tf_op jit(solution)/shard_map/pallas_call | solution.py:1745
  1254.7 8.6 shard_map.383
  1273.9 8.7 shard_map.385
  1312.3 36.6 %shard_map.388 = f32[8,16,1152]{2,1,0:T(8,128)} custom-call(f32[16,1152]{1,0:T(8,128)} %fusion.11.refs_0_, f32[1,1152]{1,0:T(1,128)} %broadcast_in_dim.164.refs_1_, f32[32,1152]{1,0:T(8,128)} %fusion.83.refs_2_, f32[1,1152]{1,0:T(1,128)} %copy-done.53, f32[1,1152]{1,0:T(1,128)} %copy-done.45, f32[6,1152]{1,0:T(8,128)} %copy-done.36, f32[1,1152]{1,0:T(1,128)} %copy-done.52, ...), custom_call_target="tpu_custom_call" | custom-call | tf_op jit(solution)/shard_map/pallas_call | solution.py:1822
  1360.1 6.8 multiply_add_fusion.5
  1369.5 6.0 multiply_add_fusion.3
  (394 shorter events, 157.4 us)
Async XLA Ops:
  7.2 283.1 %all-gather.6.cloned.1.call-start = ((), (), s32[]{:S(2)}) async-start(), calls=%async_computation.3 | async-start | bytes 8847360 | tf_op jit(solution)/shard_map/all_gather | solution.py:2112
  10.3 279.6 %all-to-all-start = ((f32[4,112,32]{1,2,0:T(8,128)}), f32[4,112,32]{1,2,0:T(8,128)S(1)}, u32[]{:S(2)}, u32[]{:S(2)}) async-start(f32[4,112,32]{1,2,0:T(8,128)} %pad_maximum_fusion.7), calls=%async_computation | async-start | bytes 131072 | tf_op jit(solution)/shard_map/all_to_all | solution.py:2208
  13.6 305.5 %all-reduce.13.cloned.1.call-start = ((), (), s32[]{:S(2)}) async-start(), calls=%async_computation.1 | async-start | bytes 1769472 | tf_op jit(solution)/shard_map/psum | solution.py:2141
  17.7 1283.5 %all-gather.4.cloned.1.call-start = ((), (), s32[]{:S(2)}) async-start(), calls=%async_computation.2 | async-start | bytes 3870720 | tf_op jit(solution)/shard_map/all_gather | solution.py:2274
  51.3 147.8 %copy-start.82 = (pred[8]{0:T(512)(128)(4,1)S(1)}, pred[8]{0:T(512)(128)(4,1)}, u32[]{:S(2)}) copy-start(pred[8]{0:T(512)(128)(4,1)} %get-tuple-element.236) | copy-start | bytes 28
  51.3 149.4 %copy-start.39 = (f32[1,448,16]{1,2,0:T(8,128)S(1)}, f32[1,448,16]{1,2,0:T(8,128)}, u32[]{:S(2)}) copy-start(f32[1,448,16]{1,2,0:T(8,128)} %param.24) | copy-start | bytes 86020
  51.3 149.4 %copy-start.40 = (f32[1,448,16]{1,2,0:T(8,128)S(1)}, f32[1,448,16]{1,2,0:T(8,128)}, u32[]{:S(2)}) copy-start(f32[1,448,16]{1,2,0:T(8,128)} %param.23) | copy-start | bytes 86020
  51.3 149.4 %copy-start.79 = (s32[224]{0:T(256)S(1)}, s32[224]{0:T(256)}, u32[]{:S(2)}) copy-start(s32[224]{0:T(256)} %and_select_fusion.2) | copy-start | bytes 2692
  51.4 149.4 %copy-start.83 = (pred[224]{0:T(512)(128)(4,1)S(1)}, pred[224]{0:T(512)(128)(4,1)}, u32[]{:S(2)}) copy-start(pred[224]{0:T(512)(128)(4,1)} %fusion.72) | copy-start | bytes 676
  52.5 149.0 %copy-start.75 = (f32[448]{0:T(512)S(1)}, f32[448]{0:T(512)}, u32[]{:S(2)}) copy-start(f32[448]{0:T(512)} %fusion.47) | copy-start | bytes 5380
  52.5 149.0 %copy-start.76 = (f32[448]{0:T(512)S(1)}, f32[448]{0:T(512)}, u32[]{:S(2)}) copy-start(f32[448]{0:T(512)} %fusion.56) | copy-start | bytes 5380
  52.5 149.0 %copy-start.77 = (f32[288]{0:T(512)S(1)}, f32[288]{0:T(512)}, u32[]{:S(2)}) copy-start(f32[288]{0:T(512)} %multiply_exponential_fusion) | copy-start | bytes 3460
  224.1 65.6 %copy-start.73 = (f32[1,576]{1,0:T(1,128)S(1)}, f32[1,576]{1,0:T(1,128)}, u32[]{:S(2)}) copy-start(f32[1,576]{1,0:T(1,128)} %fusion.70) | copy-start | bytes 6916
  224.2 65.6 %copy-start.74 = (f32[1,576]{1,0:T(1,128)S(1)}, f32[1,576]{1,0:T(1,128)}, u32[]{:S(2)}) copy-start(f32[1,576]{1,0:T(1,128)} %fusion.71) | copy-start | bytes 6916
  224.2 66.1 %copy-start.2 = (bf16[1696,288]{1,0:T(8,128)(2,1)S(1)}, bf16[1696,288]{1,0:T(8,128)(2,1)}, u32[]{:S(2)}) copy-start(bf16[1696,288]{1,0:T(8,128)(2,1)} %copy-done.1) | copy-start | bytes 2930692
  290.2 370.4 %copy-start.34 = (f32[448,32]{0,1:T(8,128)}, f32[448,32]{0,1:T(8,128)S(1)}, u32[]{:S(2)}) copy-start(f32[448,32]{0,1:T(8,128)S(1)} %reshape.393) | copy-start | bytes 172036
  318.1 23.7 %copy-start.30 = (f32[120,288]{0,1:T(8,128)}, f32[120,288]{0,1:T(8,128)S(1)}, u32[]{:S(2)}) copy-start(f32[120,288]{0,1:T(8,128)S(1)} %copy.82) | copy-start | bytes 414724
  1054.7 102.1 %copy-start.25 = (bf16[128,1152]{1,0:T(8,128)(2,1)}, bf16[128,1152]{1,0:T(8,128)(2,1)S(1)}, u32[]{:S(2)}) copy-start(bf16[128,1152]{1,0:T(8,128)(2,1)S(1)} %reduce) | copy-start | bytes 884740
  1057.0 101.9 %copy-start.71 = (f32[8,1152]{1,0:T(8,128)S(1)}, f32[8,1152]{1,0:T(8,128)}, u32[]{:S(2)}) copy-start(f32[8,1152]{1,0:T(8,128)} %get-tuple-element.113) | copy-start | bytes 110596
  1057.0 103.1 %copy-start.70 = (f32[8,1152]{1,0:T(8,128)S(1)}, f32[8,1152]{1,0:T(8,128)}, u32[]{:S(2)}) copy-start(f32[8,1152]{1,0:T(8,128)} %get-tuple-element.114) | copy-start | bytes 110596
  1057.1 103.7 %copy-start.69 = (f32[8,1152]{1,0:T(8,128)S(1)}, f32[8,1152]{1,0:T(8,128)}, u32[]{:S(2)}) copy-start(f32[8,1152]{1,0:T(8,128)} %get-tuple-element.115) | copy-start | bytes 110596
  1164.7 64.0 %copy-start.7 = (f32[448,1152]{1,0:T(8,128)S(1)}, f32[448,1152]{1,0:T(8,128)}, u32[]{:S(2)}) copy-start(f32[448,1152]{1,0:T(8,128)} %get-tuple-element.111) | copy-start | bytes 6193156
  1236.4 37.5 %copy-start.36 = (f32[6,1152]{1,0:T(8,128)}, f32[6,1152]{1,0:T(8,128)S(1)}, u32[]{:S(2)}) copy-start(f32[6,1152]{1,0:T(8,128)S(1)} %get-tuple-element.209.refs_5_) | copy-start | bytes 82948
  1253.7 33.6 %copy-start.14 = (f32[2,144,1152]{2,1,0:T(8,128)S(1)}, f32[2,144,1152]{2,1,0:T(8,128)}, u32[]{:S(2)}) copy-start(f32[2,144,1152]{2,1,0:T(8,128)} %get-tuple-element.128) | copy-start | bytes 3981316
  (69 other events, 423.2 us)
Sparse Core Ops, SparseCore 0:
  10.2 150.1 all-gather.5
  164.5 89.9 all-reduce.12
  1057.1 92.3 all-gather.3
